TPU v7x, 32 devices: a whole 2x2x4 slice. The times are simulated.
32 devices in a mesh: row: 8 (over z, x), col: 4 (over y, core).
Axes of the slice: x: 2, y: 2, z: 4, core: 2. Of those that a mesh axis runs over, the one named last changes fastest.
Arguments:
- rhs: float32 [2048, 512], P('row', 'col'), may hold values from -6 to 6
- factor: float32 [2048, 4, 256], P('row', None, 'col'), may hold values from -0.1875 to 0.1875
- inverses: float32 [4, 256, 256], P(None, 'row'), may hold values from -2 to 2, as said below
Outputs:
- solved: float32 [2048, 512], P('row', 'col')
Inputs may be any that keep to these rules, and one draw needn't show every extreme that they name: Each inverses[k] is lower triangular with diagonal entries between 0.5 and 2.
All inputs are finite; a program needn't handle non-finite values.
Results may differ from a plain program's by a relative error of at most 0.0001.
Values sent between devices are 32-bit elements; how exact they have to be, the bound alone decides.
No kernel may reach another device: no remote copies, remote signals or barrier semaphores. Data moves between devices by JAX's collectives and lax.ppermute only.
A program may use at most 64 MiB of HBM per device.

v0:
```python
import jax
import jax.numpy as jnp
from jax import lax
from jax.sharding import PartitionSpec as P

NPAN = 4


def spread(value, axis, source):
    kept = jnp.where(lax.axis_index(axis) == source, value, 0).astype(value.dtype)
    return lax.psum(kept, axis)


def body(rhs, factor, inverses):
    row_index = lax.axis_index("row")
    running = jnp.zeros_like(rhs)
    result = jnp.zeros_like(rhs)
    whole_inverse = lax.all_gather(inverses, "row", axis=1, tiled=True)
    for section in range(NPAN):
        remaining = rhs - running
        own_solve = jnp.dot(
            whole_inverse[section],
            remaining,
            precision=lax.Precision.HIGHEST,
            preferred_element_type=jnp.float32,
        )
        panel_block = spread(own_solve, "row", section)
        weight = (row_index > section).astype(jnp.float32)

        def add_columns(total, columns, offset, solution=panel_block):
            return jnp.dot(
                columns,
                solution,
                precision=lax.Precision.HIGHEST,
                preferred_element_type=jnp.float32,
            )

        update = add_columns(
            jnp.zeros_like(rhs),
            lax.all_gather(factor[:, section, :], "col", axis=1, tiled=True),
            jnp.int32(0),
        )
        running = running + weight * update
        result = jnp.where(row_index == section, panel_block, result)
    return jnp.where(row_index >= NPAN, rhs - running, result)


def solution(mesh):
    placed = (P("row", "col"), P("row", None, "col"), P(None, "row", None))
    return jax.shard_map(
        body, mesh=mesh, in_specs=placed, out_specs=P("row", "col"), check_vma=False
    )
```

profile of v0, /device:TPU:18, one launch (start us, length us, event | category | flops | bytes accessed | tf_op | source)
XLA Modules:
  0.0 348.2 jit_solution(14686547627103789740)
XLA Ops:
  6.5 0.0 copy-start
  6.5 0.0 all-gather.6.cloned.1.call-start
  6.5 0.7 all-gather.6.cloned.1.call-update
  7.3 0.0 all-reduce.5.cloned.1.call-start
  7.3 0.0 copy-start.5
  7.3 40.9 %all-gather.6.cloned.1.call-done = f32[4,256,256]{2,1,0:T(8,128)} async-done(((f32[4,32,256]{2,1,0:T(8,128)}), f32[4,256,256]{2,1,0:T(8,128)}) %all-gather.6.cloned.1.call-update) | async-done | bytes 1048592 | tf_op jit(solution)/shard_map/all_gather | solution.py:18
  48.2 0.0 copy-done
  48.2 0.0 copy-start.1
  48.2 2.1 convolution_select_fusion.3
  50.3 0.0 all-reduce.5.cloned.1.call-update
  50.3 0.0 all-reduce.7.cloned.1.call-start
  50.3 0.0 copy-done.5
  50.4 5.8 %all-gather = f32[256,1,256]{0,2,1:T(8,128)S(1)} all-gather(f32[256,1,64]{0,2,1:T(8,128)S(1)} %get-tuple-element.7), channel_id=2, replica_groups=mesh['row'=8,'col'=4] {'col'}, dimensions={2}, use_global_device_ids=true | all-gather | bytes 327680 | tf_op jit(solution)/shard_map/all_gather | solution.py:40
  56.2 65.7 %all-reduce.5.cloned.1.call-done = f32[256,128]{1,0:T(8,128)} async-done(((f32[256,128]{1,0:T(8,128)}), f32[256,128]{1,0:T(8,128)}) %all-reduce.5.cloned.1.call-update) | async-done | bytes 131088 | tf_op jit(solution)/shard_map/psum | solution.py:11
  121.9 1.5 fusion.11
  123.4 0.0 copy-done.1
  123.4 1.0 fusion.10
  124.5 0.0 all-reduce.7.cloned.1.call-update
  124.5 0.0 all-reduce.9.cloned.1.call-start
  124.5 5.8 %all-gather.1 = f32[256,1,256]{0,2,1:T(8,128)S(1)} all-gather(f32[256,1,64]{0,2,1:T(8,128)S(1)} %get-tuple-element.6), channel_id=3, replica_groups=mesh['row'=8,'col'=4] {'col'}, dimensions={2}, use_global_device_ids=true | all-gather | bytes 327680 | tf_op jit(solution)/shard_map/all_gather | solution.py:40
  130.3 64.3 %all-reduce.7.cloned.1.call-done = f32[256,128]{1,0:T(8,128)} async-done(((f32[256,128]{1,0:T(8,128)}), f32[256,128]{1,0:T(8,128)}) %all-reduce.7.cloned.1.call-update) | async-done | bytes 131088 | tf_op jit(solution)/shard_map/psum | solution.py:11
  194.6 1.5 fusion.9
  196.1 1.0 fusion.7
  197.1 0.0 all-reduce.9.cloned.1.call-update
  197.2 0.0 all-reduce.11.cloned.1.call-start
  197.2 5.8 %all-gather.2 = f32[256,1,256]{0,2,1:T(8,128)S(1)} all-gather(f32[256,1,64]{0,2,1:T(8,128)S(1)} %get-tuple-element.8), channel_id=4, replica_groups=mesh['row'=8,'col'=4] {'col'}, dimensions={2}, use_global_device_ids=true | all-gather | bytes 327680 | tf_op jit(solution)/shard_map/all_gather | solution.py:40
  203.0 63.8 %all-reduce.9.cloned.1.call-done = f32[256,128]{1,0:T(8,128)} async-done(((f32[256,128]{1,0:T(8,128)}), f32[256,128]{1,0:T(8,128)}) %all-reduce.9.cloned.1.call-update) | async-done | bytes 131088 | tf_op jit(solution)/shard_map/psum | solution.py:11
  266.9 1.5 fusion.6
  268.4 1.0 fusion.4
  269.4 0.0 copy-start.4
  269.4 0.0 all-reduce.11.cloned.1.call-update
  269.4 0.0 copy-start.2
  269.4 0.0 copy-start.3
  269.5 5.9 %all-gather.3 = f32[256,1,256]{0,2,1:T(8,128)S(1)} all-gather(f32[256,1,64]{0,2,1:T(8,128)S(1)} %get-tuple-element.5), channel_id=5, replica_groups=mesh['row'=8,'col'=4] {'col'}, dimensions={2}, use_global_device_ids=true | all-gather | bytes 327680 | tf_op jit(solution)/shard_map/all_gather | solution.py:40
  275.4 64.0 %all-reduce.11.cloned.1.call-done = f32[256,128]{1,0:T(8,128)} async-done(((f32[256,128]{1,0:T(8,128)}), f32[256,128]{1,0:T(8,128)}) %all-reduce.11.cloned.1.call-update) | async-done | bytes 131088 | tf_op jit(solution)/shard_map/psum | solution.py:11
  339.4 0.0 copy-done.4
  339.4 0.0 copy-done.2
  339.4 0.0 copy-done.3
  339.4 2.2 fusion.3
  (1 shorter events, 0.0 us)
Async XLA Ops:
  6.5 41.6 %copy-start = (f32[256,128]{1,0:T(8,128)S(1)}, f32[256,128]{1,0:T(8,128)}, u32[]{:S(2)}) copy-start(f32[256,128]{1,0:T(8,128)} %param.3) | copy-start | bytes 393220
  6.5 41.6 %all-gather.6.cloned.1.call-start = ((), (), s32[]{:S(2)}) async-start(), calls=%async_computation | async-start | bytes 1179648 | tf_op jit(solution)/shard_map/all_gather | solution.py:18
  7.3 114.6 %all-reduce.5.cloned.1.call-start = ((), (), s32[]{:S(2)}) async-start(), calls=%async_computation.1 | async-start | bytes 262144 | tf_op jit(solution)/shard_map/psum | solution.py:11
  7.3 43.0 %copy-start.5 = (f32[256,4,64]{0,2,1:T(8,128)S(1)}, f32[256,4,64]{0,2,1:T(8,128)}, u32[]{:S(2)}) copy-start(f32[256,4,64]{0,2,1:T(8,128)} %param.4) | copy-start | bytes 786436
  48.2 75.2 %copy-start.1 = (f32[4,256,256]{2,1,0:T(8,128)S(1)}, f32[4,256,256]{2,1,0:T(8,128)}, u32[]{:S(2)}) copy-start(f32[4,256,256]{2,1,0:T(8,128)} %all-gather.6.cloned.1.call-done) | copy-start | bytes 3145732
  50.3 144.3 %all-reduce.7.cloned.1.call-start = ((), (), s32[]{:S(2)}) async-start(), calls=%async_computation.2 | async-start | bytes 262144 | tf_op jit(solution)/shard_map/psum | solution.py:11
  124.5 142.4 %all-reduce.9.cloned.1.call-start = ((), (), s32[]{:S(2)}) async-start(), calls=%async_computation.3 | async-start | bytes 262144 | tf_op jit(solution)/shard_map/psum | solution.py:11
  197.2 142.2 %all-reduce.11.cloned.1.call-start = ((), (), s32[]{:S(2)}) async-start(), calls=%async_computation.4 | async-start | bytes 262144 | tf_op jit(solution)/shard_map/psum | solution.py:11
  269.4 70.0 %copy-start.4 = (f32[256,128]{1,0:T(8,128)S(1)}, f32[256,128]{1,0:T(8,128)}, u32[]{:S(2)}) copy-start(f32[256,128]{1,0:T(8,128)} %all-reduce.9.cloned.1.call-done) | copy-start | bytes 393220
  269.4 70.0 %copy-start.2 = (f32[256,128]{1,0:T(8,128)S(1)}, f32[256,128]{1,0:T(8,128)}, u32[]{:S(2)}) copy-start(f32[256,128]{1,0:T(8,128)} %all-reduce.5.cloned.1.call-done) | copy-start | bytes 393220
  269.4 70.0 %copy-start.3 = (f32[256,128]{1,0:T(8,128)S(1)}, f32[256,128]{1,0:T(8,128)}, u32[]{:S(2)}) copy-start(f32[256,128]{1,0:T(8,128)} %all-reduce.7.cloned.1.call-done) | copy-start | bytes 393220
Sparse Core Ops, SparseCore 0:
  9.5 38.5 all-gather.5
  51.5 70.3 all-reduce.4
  125.6 68.9 all-reduce.6
  197.8 68.9 all-reduce.8
  270.4 68.9 all-reduce.10
where the time goes:
time: 351 us; the launch traced here: 348 us
  waiting for transfers between devices  300 us (85%)
  blocking collectives  23.3 us (7%)
  between operations  13.2 us (4%)
  matrix products  11.9 us (3%)
    psum x4, waiting for transfers between devices, spread(): return lax.psum(kept, axis)  258 us
    all_gather x1, waiting for transfers between devices, body(): whole_inverse = lax.all_gather(inverses, 'row', axis=1, tiled=True)  40.9 us
    all_gather x4, blocking collectives, body(): lax.all_gather(factor[:, section, :], 'col', axis=1, tiled=True)  23.3 us
  transfers between devices with their start and end apart: 5, of which 5 were waited for; matrix products, arithmetic and copies ran while one was open for 0% of the time, Pallas kernels for 0%

commit v1 on v0

v1 whole, which is shorter than its diff:
```python
import jax
import jax.numpy as jnp
from jax import lax
from jax.sharding import PartitionSpec as P

AXES = ("row", "col")


def dot(left, right):
    return jnp.dot(left, right, precision=lax.Precision.HIGHEST, preferred_element_type=jnp.float32)


def solution(mesh):
    n_row, n_col = mesh.shape["row"], mesh.shape["col"]
    n_pair, n_half = n_row // 2, n_col // 2

    def hop(value, move):
        edges = []
        for q in range(n_pair):
            for x in range(2):
                for j in range(n_half):
                    for k in range(2):
                        end = move(q, x, j, k)
                        if end is not None:
                            a, b, c, d = end
                            edges.append(((q * 2 + x) * n_col + j * 2 + k, (a * 2 + b) * n_col + c * 2 + d))
        return lax.ppermute(value, AXES, edges)

    def body(rhs, factor, inverses):
        n_pan = factor.shape[1]
        n_win = n_pan // 2
        rows, part = factor.shape[0], factor.shape[2]
        shard = inverses.shape[1]
        row, col = lax.axis_index("row"), lax.axis_index("col")
        q, x, j, k = row // 2, row % 2, col // 2, col % 2
        flat = jnp.transpose(factor, (1, 0, 2))
        own = [flat] + [hop(flat, lambda q, x, j, k, s=s: (q, x, (j + s) % n_half, k)) for s in range(1, n_half)]
        own = jnp.stack(own)
        beside = hop(own, lambda q, x, j, k: (q, 1 - x, j, k))
        mine = jnp.where(x == k, own, beside)
        other = hop(jnp.where(x == k, beside, own), lambda q, x, j, k: (q, x, j, 1 - k))
        pieces = jnp.concatenate([mine, other])
        block = [jnp.concatenate([pieces[i, p] for i in range(n_col)], axis=1) for p in range(n_pan)]
        order = [((j - s) % n_half) * 2 + c for c in (k, 1 - k) for s in range(n_half)]

        def ordered(solved):
            return jnp.concatenate([lax.dynamic_slice_in_dim(solved, part * o, part) for o in order])

        def panels_for(target):
            return lax.dynamic_slice_in_dim(inverses, jnp.clip(2 * target, 0, n_pan - 2), 2)

        parts = []
        turned = lambda q, x, j, k: (q, k, j, x)
        for s in range(n_pair):
            sent = panels_for((q - s) % n_pair)

            def move(q, x, j, k, s=s):
                t = (q - s) % n_pair
                return (t, k, j, x) if t < n_win else None

            parts.append(hop(sent, move))
        got = jnp.stack(parts)
        got = jnp.roll(got, q, axis=0) if False else got
        keep = jnp.where(k == 0, got[:, 0], got[:, 1])
        send = jnp.where(k == 0, got[:, 1], got[:, 0])
        recv = hop(send, lambda q, x, j, k: (q, x, j, 1 - k) if q < n_win else None)
        even = jnp.where(k == 0, keep, recv)
        odd = jnp.where(k == 0, recv, keep)
        inverse = jnp.stack([even, odd], axis=1).reshape(n_row * shard, -1)
        inverse = jnp.roll(inverse, q * 2 * shard, axis=0)
        rhs_w = hop(rhs, turned)
        base = dot(inverse, rhs_w)
        steps = [dot(inverse, block[p]) for p in range(n_pan - 1)]

        known = []
        result = jnp.zeros_like(rhs)
        for w in range(n_win):
            first = base - sum(dot(steps[p], ordered(known[p])) for p in range(2 * w)) if w else base
            got_first = hop(first, lambda q, x, j, k: (q, x, j, 1 - k) if q == w else None)
            second = base - sum(
                dot(steps[p], ordered(v)) for p, v in enumerate(known + [got_first])
            )
            solved = jnp.where(k == 0, first, second)
            result = jnp.where(q == w, solved, result)
            arrived = jnp.zeros_like(rhs)
            for t in range(w + 1, n_pair):
                arrived = arrived + hop(solved, lambda q, x, j, k: (t, x, j, k) if q == w else None)
            swapped = hop(arrived, lambda q, x, j, k: (q, x, j, 1 - k) if q > w else None)
            known = known + [jnp.where(k == 0, arrived, swapped), jnp.where(k == 0, swapped, arrived)]
        final = rhs_w - sum(dot(block[p], ordered(known[p])) for p in range(n_pan))
        result = jnp.where(q < n_win, result, final)
        return hop(result, turned)

    placed = (P("row", "col"), P("row", None, "col"), P(None, "row", None))
    return jax.shard_map(body, mesh=mesh, in_specs=placed, out_specs=P("row", "col"), check_vma=False)
```

time: 351 us -> 79.5 us (0.23)
  waiting for transfers between devices: 300 us -> 40.3 us
  starting transfers between devices: 0.17 us -> 28.9 us
  blocking collectives: 23.3 us -> 0 us
  between operations: 13.2 us -> 0.52 us
  matrix products: 11.9 us -> 5.5 us
    psum x4 -> x0, waiting for transfers between devices: 258 us -> none  [spread(): return lax.psum(kept, axis)]
    all_gather x1 -> x0, waiting for transfers between devices: 40.9 us -> none  [body(): whole_inverse = lax.all_gather(inverses, 'row', axis=1, tiled=True)]
    ppermute x0 -> x19, waiting for transfers between devices: none -> 40.3 us  [hop(): return lax.ppermute(value, AXES, edges)]
    ppermute x0 -> x19, starting transfers between devices: none -> 28.9 us  [hop(): return lax.ppermute(value, AXES, edges)]
    all_gather x4 -> x0, blocking collectives: 23.3 us -> none  [body(): lax.all_gather(factor[:, section, :], 'col', axis=1, tiled=True)]
    dot_general x8 -> x12, matrix products: 11.9 us -> 5.5 us  [dot(): jnp.dot(left, right, precision=lax.Precision.HIGHEST, preferred_element_t...]
  transfers between devices with their start and end apart: 5 -> 19, of which waited for: 5 -> 9; matrix products, arithmetic and copies ran while one was open for 0% -> 4% of each run, Pallas kernels for 0% -> 0%
where the time goes in v1:
time: 79.5 us; the launch traced here: 78.1 us
  waiting for transfers between devices  40.3 us (51%)
  starting transfers between devices  28.9 us (36%)
  matrix products  5.5 us (7%)
  local copies, waits for them, and re-layouts  2.56 us (3%)
    ppermute x19, waiting for transfers between devices, hop(): return lax.ppermute(value, AXES, edges)  40.3 us
    ppermute x19, starting transfers between devices, hop(): return lax.ppermute(value, AXES, edges)  28.9 us
    dot_general x12, matrix products, dot(): jnp.dot(left, right, precision=lax.Precision.HIGHEST, preferred_element_t...  5.5 us
    unnamed x7, local copies, waits for them, and re-layouts  2.35 us
  transfers between devices with their start and end apart: 19, of which 9 were waited for; matrix products, arithmetic and copies ran while one was open for 4% of the time, Pallas kernels for 0%

profile of v1, /device:TPU:18, one launch (start us, length us, event | category | flops | bytes accessed | tf_op | source)
XLA Modules:
  0.0 78.1 jit_solution(9026291222282282262)
XLA Ops:
  0.0 0.0 copy-start.1
  0.0 0.9 %copy-done.1 = f32[4,32,256]{2,1,0:T(8,128)S(1)} copy-done((f32[4,32,256]{2,1,0:T(8,128)S(1)}, f32[4,32,256]{2,1,0:T(8,128)}, u32[]{:S(2)}) %copy-start.1) | copy-done | bytes 131096
  0.9 0.0 copy-start
  0.9 0.8 %collective-permute-start = (f32[2,32,256]{2,1,0:T(8,128)S(1)}, f32[2,32,256]{2,1,0:T(8,128)S(1)}, u32[]{:S(2)}, u32[]{:S(2)}) collective-permute-start(f32[2,32,256]{2,1,0:T(8,128)S(1)} %get-tuple-element.53), channel_id=1, source_target_pairs={{0,0},{1,4},{2,2},{3,6},{4,1},{5,5},{6,3},{7,7},{8,8},{9,12},{10,1... | collective-permute-start | bytes 196616 | tf_op jit(solution)/shard_map/ppermute | solution.py:27
  1.7 4.8 %collective-permute-start.1 = (f32[2,32,256]{2,1,0:T(8,128)S(1)}, f32[2,32,256]{2,1,0:T(8,128)S(1)}, u32[]{:S(2)}, u32[]{:S(2)}) collective-permute-start(f32[2,32,256]{2,1,0:T(8,128)S(1)} %get-tuple-element.54), channel_id=1, source_target_pairs={{8,0},{9,4},{10,2},{11,6},{12,1},{13,5},{14,3},{15,7},{16,8},{17,1... | collective-permute-start | bytes 196616 | tf_op jit(solution)/shard_map/ppermute | solution.py:27
  6.5 0.7 collective-permute-start.3
  7.2 5.7 %collective-permute-start.2 = (f32[2,32,256]{2,1,0:T(8,128)S(1)}, f32[2,32,256]{2,1,0:T(8,128)S(1)}, u32[]{:S(2)}, u32[]{:S(2)}) collective-permute-start(f32[2,32,256]{2,1,0:T(8,128)S(1)} %get-tuple-element.56), channel_id=1, source_target_pairs={{16,0},{17,4},{18,2},{19,6},{20,1},{21,5},{22,3},{23,7},{24,8},{25... | collective-permute-start | bytes 196616 | tf_op jit(solution)/shard_map/ppermute | solution.py:27
  12.9 0.0 copy-done
  12.9 1.6 %collective-permute-start.6 = (f32[4,256,64]{1,2,0:T(8,128)S(1)}, f32[4,256,64]{1,2,0:T(8,128)S(1)}, u32[]{:S(2)}, u32[]{:S(2)}) collective-permute-start(f32[4,256,64]{1,2,0:T(8,128)S(1)} %bitcast.66), channel_id=1, source_target_pairs={{0,2},{1,3},{2,0},{3,1},{4,6},{5,7},{6,4},{7,5},{8,10},{9,11},{10,... | collective-permute-start | bytes 786440 | tf_op jit(solution)/shard_map/ppermute | solution.py:27
  14.5 0.0 collective-permute-done
  14.5 0.0 collective-permute-done.1
  14.5 0.0 collective-permute-done.3
  14.5 0.3 collective-permute-done.2
  14.8 0.7 collective-permute-start.4
  15.5 3.8 %collective-permute-done.6 = f32[4,256,64]{1,2,0:T(8,128)S(1)} collective-permute-done((f32[4,256,64]{1,2,0:T(8,128)S(1)}, f32[4,256,64]{1,2,0:T(8,128)S(1)}, u32[]{:S(2)}, u32[]{:S(2)}) %collective-permute-start.6) | collective-permute-done | bytes 262176 | tf_op jit(solution)/shard_map/ppermute | solution.py:27
  19.3 0.0 copy-start.2
  19.4 0.1 collective-permute-start.7
  19.5 0.8 %copy-done.2 = f32[256,128]{1,0:T(8,128)S(1)} copy-done((f32[256,128]{1,0:T(8,128)S(1)}, f32[256,128]{1,0:T(8,128)}, u32[]{:S(2)}) %copy-start.2) | copy-done | bytes 131096
  20.2 1.9 %collective-permute-start.5 = (f32[256,128]{1,0:T(8,128)S(1)}, f32[256,128]{1,0:T(8,128)S(1)}, u32[]{:S(2)}, u32[]{:S(2)}) collective-permute-start(f32[256,128]{1,0:T(8,128)S(1)} %copy-done.2), channel_id=1, source_target_pairs={{0,0},{1,4},{2,2},{3,6},{4,1},{5,5},{6,3},{7,7},{8,8},{9,12},{10,1... | collective-permute-start | bytes 393224 | tf_op jit(solution)/shard_map/ppermute | solution.py:27
  22.2 0.0 collective-permute-done.4
  22.3 0.1 fusion.4
  22.4 10.2 %collective-permute-done.7 = f32[2,4,256,64]{2,3,1,0:T(8,128)S(1)} collective-permute-done((f32[2,4,256,64]{2,3,1,0:T(8,128)S(1)}, f32[2,4,256,64]{2,3,1,0:T(8,128)S(1)}, u32[]{:S(2)}, u32[]{:S(2)}) %collective-permute-start.7) | collective-permute-done | bytes 524320 | tf_op jit(solution)/shard_map/ppermute | solution.py:27
  32.6 0.1 broadcast_select_fusion.1
  32.7 0.1 collective-permute-start.8
  32.8 0.0 collective-permute-done.5
  32.8 0.4 fusion.63
  33.2 0.7 collective-permute-start.9
  33.9 0.0 collective-permute-done.9
  34.0 0.7 collective-permute-done.8
  34.7 0.4 fusion.15
  35.1 0.4 fusion.3
  35.5 0.7 collective-permute-start.12
  36.2 1.3 %collective-permute-start.11 = (f32[256,128]{1,0:T(8,128)S(1)}, f32[256,128]{1,0:T(8,128)S(1)}, u32[]{:S(2)}, u32[]{:S(2)}) collective-permute-start(f32[256,128]{1,0:T(8,128)S(1)} %fusion.3), channel_id=1, source_target_pairs={{0,16},{1,17},{2,18},{3,19},{4,20},{5,21},{6,22},{7,23}} | collective-permute-start | bytes 393224 | tf_op jit(solution)/shard_map/ppermute | solution.py:27
  37.5 0.7 collective-permute-start.10
  38.2 0.0 collective-permute-done.12
  38.2 9.9 %collective-permute-done.11 = f32[256,128]{1,0:T(8,128)S(1)} collective-permute-done((f32[256,128]{1,0:T(8,128)S(1)}, f32[256,128]{1,0:T(8,128)S(1)}, u32[]{:S(2)}, u32[]{:S(2)}) %collective-permute-start.11) | collective-permute-done | bytes 131104 | tf_op jit(solution)/shard_map/ppermute | solution.py:27
  48.1 0.0 collective-permute-done.10
  48.1 1.9 %collective-permute-start.13 = (f32[256,128]{1,0:T(8,128)S(1)}, f32[256,128]{1,0:T(8,128)S(1)}, u32[]{:S(2)}, u32[]{:S(2)}) collective-permute-start(f32[256,128]{1,0:T(8,128)S(1)} %add_add_fusion), channel_id=1, source_target_pairs={{8,9},{9,8},{10,11},{11,10},{12,13},{13,12},{14,15},{15,14},{16,17... | collective-permute-start | bytes 393224 | tf_op jit(solution)/shard_map/ppermute | solution.py:27
  50.0 0.4 fusion.14
  50.4 0.9 %collective-permute-done.13 = f32[256,128]{1,0:T(8,128)S(1)} collective-permute-done((f32[256,128]{1,0:T(8,128)S(1)}, f32[256,128]{1,0:T(8,128)S(1)}, u32[]{:S(2)}, u32[]{:S(2)}) %collective-permute-start.13) | collective-permute-done | bytes 131104 | tf_op jit(solution)/shard_map/ppermute | solution.py:27
  51.4 0.4 fusion.46
  51.8 0.4 fusion.62
  52.2 0.7 collective-permute-start.14
  52.9 0.4 fusion.12
  53.3 0.0 collective-permute-done.14
  53.3 0.4 fusion.2
  53.7 0.7 collective-permute-start.16
  54.4 1.3 %collective-permute-start.15 = (f32[256,128]{1,0:T(8,128)S(1)}, f32[256,128]{1,0:T(8,128)S(1)}, u32[]{:S(2)}, u32[]{:S(2)}) collective-permute-start(f32[256,128]{1,0:T(8,128)S(1)} %fusion.2), channel_id=1, source_target_pairs={{8,16},{9,17},{10,18},{11,19},{12,20},{13,21},{14,22},{15,23}} | collective-permute-start | bytes 393224 | tf_op jit(solution)/shard_map/ppermute | solution.py:27
  55.7 0.6 fusion.13
  56.3 0.0 collective-permute-done.16
  56.3 10.3 %collective-permute-done.15 = f32[256,128]{1,0:T(8,128)S(1)} collective-permute-done((f32[256,128]{1,0:T(8,128)S(1)}, f32[256,128]{1,0:T(8,128)S(1)}, u32[]{:S(2)}, u32[]{:S(2)}) %collective-permute-start.15) | collective-permute-done | bytes 131104 | tf_op jit(solution)/shard_map/ppermute | solution.py:27
  66.6 1.9 %collective-permute-start.17 = (f32[256,128]{1,0:T(8,128)S(1)}, f32[256,128]{1,0:T(8,128)S(1)}, u32[]{:S(2)}, u32[]{:S(2)}) collective-permute-start(f32[256,128]{1,0:T(8,128)S(1)} %add.155), channel_id=1, source_target_pairs={{16,17},{17,16},{18,19},{19,18},{20,21},{21,20},{22,23},{23,22},{2... | collective-permute-start | bytes 393224 | tf_op jit(solution)/shard_map/ppermute | solution.py:27
  68.6 0.6 convolution_add_fusion.2
  69.2 0.7 collective-permute-done.17
  69.9 0.6 convolution_add_fusion.1
  70.5 0.6 select_select_fusion
  71.1 2.9 %collective-permute-start.18 = (f32[256,128]{1,0:T(8,128)S(1)}, f32[256,128]{1,0:T(8,128)S(1)}, u32[]{:S(2)}, u32[]{:S(2)}) collective-permute-start(f32[256,128]{1,0:T(8,128)S(1)} %select_select_fusion), channel_id=1, source_target_pairs={{0,0},{1,4},{2,2},{3,6},{4,1},{5,5},{6,3},{7,7},{8,8},{9,12},{10,1... | collective-permute-start | bytes 393224 | tf_op jit(solution)/shard_map/ppermute | solution.py:27
  74.0 3.4 %collective-permute-done.18 = f32[256,128]{1,0:T(8,128)S(1)} collective-permute-done((f32[256,128]{1,0:T(8,128)S(1)}, f32[256,128]{1,0:T(8,128)S(1)}, u32[]{:S(2)}, u32[]{:S(2)}) %collective-permute-start.18) | collective-permute-done | bytes 131104 | tf_op jit(solution)/shard_map/ppermute | solution.py:27
  77.4 0.7 copy.10
  (17 shorter events, 0.4 us)
Async XLA Ops:
  0.0 0.9 %copy-start.1 = (f32[4,32,256]{2,1,0:T(8,128)S(1)}, f32[4,32,256]{2,1,0:T(8,128)}, u32[]{:S(2)}) copy-start(f32[4,32,256]{2,1,0:T(8,128)} %param.5) | copy-start | bytes 393220
  0.9 12.0 %copy-start = (f32[256,4,64]{0,2,1:T(8,128)S(1)}, f32[256,4,64]{0,2,1:T(8,128)}, u32[]{:S(2)}) copy-start(f32[256,4,64]{0,2,1:T(8,128)} %param.4) | copy-start | bytes 786436
  0.9 13.6 %collective-permute-start = (f32[2,32,256]{2,1,0:T(8,128)S(1)}, f32[2,32,256]{2,1,0:T(8,128)S(1)}, u32[]{:S(2)}, u32[]{:S(2)}) collective-permute-start(f32[2,32,256]{2,1,0:T(8,128)S(1)} %get-tuple-element.53), channel_id=1, source_target_pairs={{0,0},{1,4},{2,2},{3,6},{4,1},{5,5},{6,3},{7,7},{8,8},{9,12},{10,1... | collective-permute-start | bytes 196616 | tf_op jit(solution)/shard_map/ppermute | solution.py:27
  1.7 12.8 %collective-permute-start.1 = (f32[2,32,256]{2,1,0:T(8,128)S(1)}, f32[2,32,256]{2,1,0:T(8,128)S(1)}, u32[]{:S(2)}, u32[]{:S(2)}) collective-permute-start(f32[2,32,256]{2,1,0:T(8,128)S(1)} %get-tuple-element.54), channel_id=1, source_target_pairs={{8,0},{9,4},{10,2},{11,6},{12,1},{13,5},{14,3},{15,7},{16,8},{17,1... | collective-permute-start | bytes 196616 | tf_op jit(solution)/shard_map/ppermute | solution.py:27
  6.5 8.0 %collective-permute-start.3 = (f32[2,32,256]{2,1,0:T(8,128)S(1)}, f32[2,32,256]{2,1,0:T(8,128)S(1)}, u32[]{:S(2)}, u32[]{:S(2)}) collective-permute-start(f32[2,32,256]{2,1,0:T(8,128)S(1)} %get-tuple-element.55), channel_id=1, source_target_pairs={{0,8},{1,12},{2,10},{3,14},{4,9},{5,13},{6,11},{7,15},{24,0},{25,4... | collective-permute-start | bytes 196616 | tf_op jit(solution)/shard_map/ppermute | solution.py:27
  7.2 7.6 %collective-permute-start.2 = (f32[2,32,256]{2,1,0:T(8,128)S(1)}, f32[2,32,256]{2,1,0:T(8,128)S(1)}, u32[]{:S(2)}, u32[]{:S(2)}) collective-permute-start(f32[2,32,256]{2,1,0:T(8,128)S(1)} %get-tuple-element.56), channel_id=1, source_target_pairs={{16,0},{17,4},{18,2},{19,6},{20,1},{21,5},{22,3},{23,7},{24,8},{25... | collective-permute-start | bytes 196616 | tf_op jit(solution)/shard_map/ppermute | solution.py:27
  12.9 6.4 %collective-permute-start.6 = (f32[4,256,64]{1,2,0:T(8,128)S(1)}, f32[4,256,64]{1,2,0:T(8,128)S(1)}, u32[]{:S(2)}, u32[]{:S(2)}) collective-permute-start(f32[4,256,64]{1,2,0:T(8,128)S(1)} %bitcast.66), channel_id=1, source_target_pairs={{0,2},{1,3},{2,0},{3,1},{4,6},{5,7},{6,4},{7,5},{8,10},{9,11},{10,... | collective-permute-start | bytes 786440 | tf_op jit(solution)/shard_map/ppermute | solution.py:27
  14.8 7.4 %collective-permute-start.4 = (f32[4,32,256]{2,1,0:T(8,128)S(1)}, f32[4,32,256]{2,1,0:T(8,128)S(1)}, u32[]{:S(2)}, u32[]{:S(2)}) collective-permute-start(f32[4,32,256]{2,1,0:T(8,128)S(1)} %select_bitcast_fusion), channel_id=1, source_target_pairs={{0,1},{1,0},{2,3},{3,2},{4,5},{5,4},{6,7},{7,6},{8,9},{9,8},{10,11... | collective-permute-start | bytes 393224 | tf_op jit(solution)/shard_map/ppermute | solution.py:27
  19.3 0.9 %copy-start.2 = (f32[256,128]{1,0:T(8,128)S(1)}, f32[256,128]{1,0:T(8,128)}, u32[]{:S(2)}) copy-start(f32[256,128]{1,0:T(8,128)} %param.3) | copy-start | bytes 393220
  19.4 13.2 %collective-permute-start.7 = (f32[2,4,256,64]{2,3,1,0:T(8,128)S(1)}, f32[2,4,256,64]{2,3,1,0:T(8,128)S(1)}, u32[]{:S(2)}, u32[]{:S(2)}) collective-permute-start(f32[2,4,256,64]{2,3,1,0:T(8,128)S(1)} %pad_maximum_fusion), channel_id=1, source_target_pairs={{0,4},{1,5},{2,6},{3,7},{4,0},{5,1},{6,2},{7,3},{8,12},{9,13},{10,... | collective-permute-start | bytes 1572872 | tf_op jit(solution)/shard_map/ppermute | solution.py:27
  20.2 12.6 %collective-permute-start.5 = (f32[256,128]{1,0:T(8,128)S(1)}, f32[256,128]{1,0:T(8,128)S(1)}, u32[]{:S(2)}, u32[]{:S(2)}) collective-permute-start(f32[256,128]{1,0:T(8,128)S(1)} %copy-done.2), channel_id=1, source_target_pairs={{0,0},{1,4},{2,2},{3,6},{4,1},{5,5},{6,3},{7,7},{8,8},{9,12},{10,1... | collective-permute-start | bytes 393224 | tf_op jit(solution)/shard_map/ppermute | solution.py:27
  32.7 2.0 %collective-permute-start.8 = (f32[2,4,256,64]{2,3,1,0:T(8,128)S(1)}, f32[2,4,256,64]{2,3,1,0:T(8,128)S(1)}, u32[]{:S(2)}, u32[]{:S(2)}) collective-permute-start(f32[2,4,256,64]{2,3,1,0:T(8,128)S(1)} %get-tuple-element.6), channel_id=1, source_target_pairs={{0,1},{1,0},{2,3},{3,2},{4,5},{5,4},{6,7},{7,6},{8,9},{9,8},{10,11... | collective-permute-start | bytes 1572872 | tf_op jit(solution)/shard_map/ppermute | solution.py:27
  33.2 0.8 collective-permute-start.9
  35.5 2.7 %collective-permute-start.12 = (f32[256,128]{1,0:T(8,128)S(1)}, f32[256,128]{1,0:T(8,128)S(1)}, u32[]{:S(2)}, u32[]{:S(2)}) collective-permute-start(f32[256,128]{1,0:T(8,128)S(1)} %fusion.3), channel_id=1, source_target_pairs={{0,24},{1,25},{2,26},{3,27},{4,28},{5,29},{6,30},{7,31}} | collective-permute-start | bytes 393224 | tf_op jit(solution)/shard_map/ppermute | solution.py:27
  36.2 11.8 %collective-permute-start.11 = (f32[256,128]{1,0:T(8,128)S(1)}, f32[256,128]{1,0:T(8,128)S(1)}, u32[]{:S(2)}, u32[]{:S(2)}) collective-permute-start(f32[256,128]{1,0:T(8,128)S(1)} %fusion.3), channel_id=1, source_target_pairs={{0,16},{1,17},{2,18},{3,19},{4,20},{5,21},{6,22},{7,23}} | collective-permute-start | bytes 393224 | tf_op jit(solution)/shard_map/ppermute | solution.py:27
  37.5 10.5 %collective-permute-start.10 = (f32[256,128]{1,0:T(8,128)S(1)}, f32[256,128]{1,0:T(8,128)S(1)}, u32[]{:S(2)}, u32[]{:S(2)}) collective-permute-start(f32[256,128]{1,0:T(8,128)S(1)} %fusion.3), channel_id=1, source_target_pairs={{0,8},{1,9},{2,10},{3,11},{4,12},{5,13},{6,14},{7,15}} | collective-permute-start | bytes 393224 | tf_op jit(solution)/shard_map/ppermute | solution.py:27
  48.1 3.2 %collective-permute-start.13 = (f32[256,128]{1,0:T(8,128)S(1)}, f32[256,128]{1,0:T(8,128)S(1)}, u32[]{:S(2)}, u32[]{:S(2)}) collective-permute-start(f32[256,128]{1,0:T(8,128)S(1)} %add_add_fusion), channel_id=1, source_target_pairs={{8,9},{9,8},{10,11},{11,10},{12,13},{13,12},{14,15},{15,14},{16,17... | collective-permute-start | bytes 393224 | tf_op jit(solution)/shard_map/ppermute | solution.py:27
  52.2 1.1 %collective-permute-start.14 = (f32[256,128]{1,0:T(8,128)S(1)}, f32[256,128]{1,0:T(8,128)S(1)}, u32[]{:S(2)}, u32[]{:S(2)}) collective-permute-start(f32[256,128]{1,0:T(8,128)S(1)} %get-tuple-element.57), channel_id=1, source_target_pairs={{8,9},{9,8},{10,11},{11,10},{12,13},{13,12},{14,15},{15,14}} | collective-permute-start | bytes 393224 | tf_op jit(solution)/shard_map/ppermute | solution.py:27
  53.7 2.6 %collective-permute-start.16 = (f32[256,128]{1,0:T(8,128)S(1)}, f32[256,128]{1,0:T(8,128)S(1)}, u32[]{:S(2)}, u32[]{:S(2)}) collective-permute-start(f32[256,128]{1,0:T(8,128)S(1)} %fusion.2), channel_id=1, source_target_pairs={{8,24},{9,25},{10,26},{11,27},{12,28},{13,29},{14,30},{15,31}} | collective-permute-start | bytes 393224 | tf_op jit(solution)/shard_map/ppermute | solution.py:27
  54.4 12.2 %collective-permute-start.15 = (f32[256,128]{1,0:T(8,128)S(1)}, f32[256,128]{1,0:T(8,128)S(1)}, u32[]{:S(2)}, u32[]{:S(2)}) collective-permute-start(f32[256,128]{1,0:T(8,128)S(1)} %fusion.2), channel_id=1, source_target_pairs={{8,16},{9,17},{10,18},{11,19},{12,20},{13,21},{14,22},{15,23}} | collective-permute-start | bytes 393224 | tf_op jit(solution)/shard_map/ppermute | solution.py:27
  66.6 3.2 %collective-permute-start.17 = (f32[256,128]{1,0:T(8,128)S(1)}, f32[256,128]{1,0:T(8,128)S(1)}, u32[]{:S(2)}, u32[]{:S(2)}) collective-permute-start(f32[256,128]{1,0:T(8,128)S(1)} %add.155), channel_id=1, source_target_pairs={{16,17},{17,16},{18,19},{19,18},{20,21},{21,20},{22,23},{23,22},{2... | collective-permute-start | bytes 393224 | tf_op jit(solution)/shard_map/ppermute | solution.py:27
  71.1 6.3 %collective-permute-start.18 = (f32[256,128]{1,0:T(8,128)S(1)}, f32[256,128]{1,0:T(8,128)S(1)}, u32[]{:S(2)}, u32[]{:S(2)}) collective-permute-start(f32[256,128]{1,0:T(8,128)S(1)} %select_select_fusion), channel_id=1, source_target_pairs={{0,0},{1,4},{2,2},{3,6},{4,1},{5,5},{6,3},{7,7},{8,8},{9,12},{10,1... | collective-permute-start | bytes 393224 | tf_op jit(solution)/shard_map/ppermute | solution.py:27

commit v2 on v1

v2 whole, which is shorter than its diff:
```python
import jax
import jax.numpy as jnp
from jax import lax
from jax.sharding import PartitionSpec as P

AXES = ("row", "col")


def dot(left, right):
    return jnp.dot(left, right, precision=lax.Precision.HIGHEST, preferred_element_type=jnp.float32)


def after(value, earlier):
    return lax.optimization_barrier((value, earlier))[0]


def solution(mesh):
    n_row, n_col = mesh.shape["row"], mesh.shape["col"]
    n_pair, n_half = n_row // 2, n_col // 2

    def hop(value, move):
        edges = []
        for q in range(n_pair):
            for x in range(2):
                for j in range(n_half):
                    for k in range(2):
                        end = move(q, x, j, k)
                        if end is not None:
                            a, b, c, d = end
                            edges.append(((q * 2 + x) * n_col + j * 2 + k, (a * 2 + b) * n_col + c * 2 + d))
        return lax.ppermute(value, AXES, edges)

    def body(rhs, factor, inverses):
        rows, n_pan, part = factor.shape
        width = rhs.shape[1]
        shard, wide = inverses.shape[1:]
        n_win = n_pan // 2
        row, col = lax.axis_index("row"), lax.axis_index("col")
        q, x, j, k = row // 2, row % 2, col // 2, col % 2

        def along(value, which):
            shifted = [
                hop(value, lambda q, x, j, k, s=s: (q, x, (j + s) % n_half, k) if which(q) else None)
                for s in range(1, n_half)
            ]
            return jnp.stack([value] + shifted)

        def swap_rows(value, which):
            return hop(value, lambda q, x, j, k: (q, 1 - x, j, k) if which(q) else None)

        def swap_cores(value, which):
            return hop(value, lambda q, x, j, k: (q, x, j, 1 - k) if which(q) else None)

        def panels_for(target):
            return lax.dynamic_slice_in_dim(inverses, jnp.clip(2 * target, 0, n_pan - 2), 2)

        across = jnp.transpose(factor, (1, 2, 0))
        head_own = along(across[0], lambda q: q == 0)

        parts = []
        for s in range(n_pair - 1, 0, -1):

            def inward(q, x, j, k, s=s):
                t = (q - s) % n_pair
                return (t, k, j, x) if t < n_win else None

            parts.append(hop(panels_for((q - s) % n_pair), inward))
        parts = jnp.stack(parts[::-1])
        half = rows // 2
        here = panels_for(q)
        folded = jnp.concatenate([rhs[:half], rhs[half:]], axis=1).reshape(-1, wide)
        packed = jnp.concatenate([folded, here.reshape(-1, wide)])
        beside = swap_rows(packed, lambda q: q < n_win)
        there = beside[-2 * shard :].reshape(2, shard, wide)
        folded = beside[: -2 * shard].reshape(half, 2 * width)
        rhs_beside = jnp.concatenate([folded[:, :width], folded[:, width:]])
        rhs_even = jnp.where(x == 0, rhs, rhs_beside)
        rhs_odd = jnp.where(x == 0, rhs_beside, rhs)

        whole_own = along(across, lambda q: q > 0)
        head_beside = hop(head_own, lambda q, x, j, k: (q, 0, j, k) if q == 0 and x == 1 else None)
        head_odd = jnp.where(x == 0, head_beside, head_own).reshape(-1, rows)

        crossed = swap_cores(parts, lambda q: q < n_win)
        even_row = jnp.concatenate([jnp.where(x == 0, here, there)[None], jnp.where(k == 0, parts, crossed)])
        odd_row = jnp.concatenate([jnp.where(x == 0, there, here)[None], jnp.where(k == 0, crossed, parts)])
        inverse = jnp.stack([even_row, odd_row], axis=1)
        inverse = jnp.transpose(inverse, (2, 0, 1, 3, 4)).reshape(2, n_row * shard, wide)
        inverse = jnp.roll(inverse, q * 2 * shard, axis=1)

        order = [((j - s) % n_half) * 2 + c for c in (k, 1 - k) for s in range(n_half)]

        def ordered(solved):
            return jnp.concatenate([lax.dynamic_slice_in_dim(solved, part * o, part) for o in order])

        head_full = jnp.concatenate([head_odd, swap_cores(head_odd, lambda q: q == 0)])

        near = n_pan - 1
        tail_beside = swap_rows(whole_own[:, :near], lambda q: 0 < q < n_win)
        whole_other = swap_cores(whole_own, lambda q: q > 0)

        solved = []
        first = dot(inverse[0], rhs_even)
        climb = [hop(first, lambda q, x, j, k: (1, x, j, k) if q == 0 else None)]
        second = dot(inverse[1], rhs_odd - dot(head_full.T, ordered(first)))
        climb.append(hop(second, lambda q, x, j, k: (1, x, j, k) if q == 0 else None))
        solved += [first, second]
        result = jnp.where(x == 0, first, second)

        tail_other = swap_cores(after(tail_beside, climb[1]), lambda q: 0 < q < n_win)
        own_full = [
            jnp.concatenate([whole_own[:, p].reshape(-1, rows), whole_other[:, p].reshape(-1, rows)])
            for p in range(n_pan)
        ]
        beside_full = [
            jnp.concatenate([tail_beside[:, p].reshape(-1, rows), tail_other[:, p].reshape(-1, rows)])
            for p in range(near)
        ]
        even_full = [jnp.where(x == 0, own_full[p], beside_full[p]) for p in range(near)]
        odd_full = [jnp.where(x == 0, beside_full[p], own_full[p]) for p in range(near)]

        known = climb
        for w in range(1, n_win):
            left_even, left_odd = rhs_even, rhs_odd
            for p, v in enumerate(known):
                turned = ordered(v)
                left_even = left_even - dot(even_full[p].T, turned)
                left_odd = left_odd - dot(odd_full[p].T, turned)
            first = dot(inverse[0], left_even)
            second = dot(inverse[1], left_odd - dot(odd_full[2 * w].T, ordered(first)))
            solved += [first, second]
            result = jnp.where(q == w, jnp.where(x == 0, first, second), result)
            if w + 1 < n_win:
                known = [
                    v + hop(v if q_from < w else u, lambda q, x, j, k: (w + 1, x, j, k) if q == w else None)
                    for v, u, q_from in ()
                ]

        depth = n_pair - n_win
        waves = []
        for i in range(near - 1 + depth):
            value = waves[-1] if waves else rhs
            if i < near:
                value = jnp.where(q < n_win, solved[i], value)
            origin = i // 2 if i < near else None

            def move(q, x, j, k):
                if q == origin:
                    return (n_win, x, j, k)
                if n_win <= q < n_pair - 1 and i > q - n_win and i - 1 - (q - n_win) < near:
                    return (q + 1, x, j, k)
                return None

            waves.append(hop(value, move))
        last = 0
        for t in range(n_pair - 1, n_win - 1, -1):
            last = last + hop(solved[-1], lambda q, x, j, k: (t, x, j, k) if q == n_win - 1 else None)
        final = rhs
        for p in range(near):
            value = waves[p]
            for d in range(1, depth):
                value = jnp.where(q == n_win + d, waves[p + d], value)
            final = final - dot(own_full[p].T, ordered(value))
        final = final - dot(own_full[near].T, ordered(last))
        return jnp.where(q < n_win, result, final)

    placed = (P("row", "col"), P("row", None, "col"), P(None, "row", None))
    return jax.shard_map(body, mesh=mesh, in_specs=placed, out_specs=P("row", "col"), check_vma=False)
```

time: 79.5 us -> 59.5 us (0.75)
  waiting for transfers between devices: 40.3 us -> 24.7 us
  starting transfers between devices: 28.9 us -> 23.6 us
  matrix products: 5.5 us -> 8.16 us
  local copies, waits for them, and re-layouts: 2.56 us -> 1.24 us
    ppermute x19 -> x20, waiting for transfers between devices: 40.3 us -> 24.7 us  [hop(): return lax.ppermute(value, AXES, edges)]
    ppermute x19 -> x20, starting transfers between devices: 28.9 us -> 23.6 us  [hop(): return lax.ppermute(value, AXES, edges)]
    dot_general x12 -> x14, matrix products: 5.5 us -> 8.16 us  [dot(): jnp.dot(left, right, precision=lax.Precision.HIGHEST, preferred_element_t...]
    unnamed x7 -> x6, local copies, waits for them, and re-layouts: 2.35 us -> 0.91 us
  transfers between devices with their start and end apart: 19 -> 20, of which waited for: 9 -> 5; matrix products, arithmetic and copies ran while one was open for 4% -> 9% of each run, Pallas kernels for 0% -> 0%
where the time goes in v2:
time: 59.5 us; the launch traced here: 58.9 us
  waiting for transfers between devices  24.7 us (42%)
  starting transfers between devices  23.6 us (40%)
  matrix products  8.16 us (14%)
  local copies, waits for them, and re-layouts  1.24 us (2%)
  between operations  0.71 us (1%)
    ppermute x20, waiting for transfers between devices, hop(): return lax.ppermute(value, AXES, edges)  24.7 us
    ppermute x20, starting transfers between devices, hop(): return lax.ppermute(value, AXES, edges)  23.6 us
    dot_general x14, matrix products, dot(): jnp.dot(left, right, precision=lax.Precision.HIGHEST, preferred_element_t...  8.16 us
  transfers between devices with their start and end apart: 20, of which 5 were waited for; matrix products, arithmetic and copies ran while one was open for 9% of the time, Pallas kernels for 0%

profile of v2, /device:TPU:18, one launch (start us, length us, event | category | flops | bytes accessed | tf_op | source)
XLA Modules:
  0.0 58.9 jit_solution(16871046279791903587)
XLA Ops:
  0.0 0.0 copy-start.2
  0.0 0.9 %copy-done.2 = f32[4,32,256]{2,1,0:T(8,128)S(1)} copy-done((f32[4,32,256]{2,1,0:T(8,128)S(1)}, f32[4,32,256]{2,1,0:T(8,128)}, u32[]{:S(2)}) %copy-start.2) | copy-done | bytes 131096
  0.9 0.0 copy-start.1
  0.9 0.0 copy-start
  0.9 1.9 %collective-permute-start.1 = (f32[2,32,256]{2,1,0:T(8,128)S(1)}, f32[2,32,256]{2,1,0:T(8,128)S(1)}, u32[]{:S(2)}, u32[]{:S(2)}) collective-permute-start(f32[2,32,256]{2,1,0:T(8,128)S(1)} %get-tuple-element.67), channel_id=1, source_target_pairs={{8,0},{9,4},{10,2},{11,6},{12,1},{13,5},{14,3},{15,7},{16,8},{17,1... | collective-permute-start | bytes 196616 | tf_op jit(solution)/shard_map/ppermute | solution.py:31
  2.8 1.3 %collective-permute-start.2 = (f32[2,32,256]{2,1,0:T(8,128)S(1)}, f32[2,32,256]{2,1,0:T(8,128)S(1)}, u32[]{:S(2)}, u32[]{:S(2)}) collective-permute-start(f32[2,32,256]{2,1,0:T(8,128)S(1)} %get-tuple-element.69), channel_id=1, source_target_pairs={{16,0},{17,4},{18,2},{19,6},{20,1},{21,5},{22,3},{23,7},{24,8},{25... | collective-permute-start | bytes 196616 | tf_op jit(solution)/shard_map/ppermute | solution.py:31
  4.1 0.7 %collective-permute-start.3 = (f32[2,32,256]{2,1,0:T(8,128)S(1)}, f32[2,32,256]{2,1,0:T(8,128)S(1)}, u32[]{:S(2)}, u32[]{:S(2)}) collective-permute-start(f32[2,32,256]{2,1,0:T(8,128)S(1)} %get-tuple-element.68), channel_id=1, source_target_pairs={{0,8},{1,12},{2,10},{3,14},{4,9},{5,13},{6,11},{7,15},{24,0},{25,4... | collective-permute-start | bytes 196616 | tf_op jit(solution)/shard_map/ppermute | solution.py:31
  4.8 0.0 copy-done.1
  4.8 3.4 %collective-permute-start.5 = (f32[4,64,256]{2,1,0:T(8,128)S(1)}, f32[4,64,256]{2,1,0:T(8,128)S(1)}, u32[]{:S(2)}, u32[]{:S(2)}) collective-permute-start(f32[4,64,256]{2,1,0:T(8,128)S(1)} %bitcast.59), channel_id=1, source_target_pairs={{8,10},{9,11},{10,8},{11,9},{12,14},{13,15},{14,12},{15,13},{16,18... | collective-permute-start | bytes 786440 | tf_op jit(solution)/shard_map/ppermute | solution.py:31
  8.3 0.7 %collective-permute-start.8 = (f32[64,256]{1,0:T(8,128)S(1)}, f32[64,256]{1,0:T(8,128)S(1)}, u32[]{:S(2)}, u32[]{:S(2)}) collective-permute-start(f32[64,256]{1,0:T(8,128)S(1)} %get-tuple-element.24), channel_id=1, source_target_pairs={{0,2},{1,3},{2,0},{3,1},{4,6},{5,7},{6,4},{7,5}} | collective-permute-start | bytes 196616 | tf_op jit(solution)/shard_map/ppermute | solution.py:31
  9.0 0.0 copy-done
  9.0 0.0 collective-permute-done.8
  9.0 0.7 %collective-permute-start.9 = (f32[2,64,256]{2,1,0:T(8,128)S(1)}, f32[2,64,256]{2,1,0:T(8,128)S(1)}, u32[]{:S(2)}, u32[]{:S(2)}) collective-permute-start(f32[2,64,256]{2,1,0:T(8,128)S(1)} %pad_maximum_fusion.22), channel_id=1, source_target_pairs={{4,0},{5,1},{6,2},{7,3}} | collective-permute-start | bytes 393224 | tf_op jit(solution)/shard_map/ppermute | solution.py:31
  9.8 0.0 collective-permute-done.1
  9.8 0.7 %collective-permute-start = (f32[192,256]{1,0:T(8,128)S(1)}, f32[192,256]{1,0:T(8,128)S(1)}, u32[]{:S(2)}, u32[]{:S(2)}) collective-permute-start(f32[192,256]{1,0:T(8,128)S(1)} %pad_maximum_fusion.13), channel_id=1, source_target_pairs={{0,4},{1,5},{2,6},{3,7},{4,0},{5,1},{6,2},{7,3},{8,12},{9,13},{10,... | collective-permute-start | bytes 589832 | tf_op jit(solution)/shard_map/ppermute | solution.py:31
  10.5 0.0 collective-permute-done.2
  10.5 0.0 collective-permute-done.3
  10.6 0.7 %collective-permute-start.4 = (f32[3,2,32,256]{3,2,0,1:T(8,128)S(1)}, f32[3,2,32,256]{3,2,0,1:T(8,128)S(1)}, u32[]{:S(2)}, u32[]{:S(2)}) collective-permute-start(f32[3,2,32,256]{3,2,0,1:T(8,128)S(1)} %pad_maximum_fusion.14), channel_id=1, source_target_pairs={{0,1},{1,0},{2,3},{3,2},{4,5},{5,4},{6,7},{7,6},{8,9},{9,8},{10,11... | collective-permute-start | bytes 589832 | tf_op jit(solution)/shard_map/ppermute | solution.py:31
  11.2 0.0 collective-permute-done.9
  11.3 0.7 %collective-permute-start.10 = (f32[128,256]{1,0:T(8,128)S(1)}, f32[128,256]{1,0:T(8,128)S(1)}, u32[]{:S(2)}, u32[]{:S(2)}) collective-permute-start(f32[128,256]{1,0:T(8,128)S(1)} %bitcast.93), channel_id=1, source_target_pairs={{0,1},{1,0},{2,3},{3,2},{4,5},{5,4},{6,7},{7,6}} | collective-permute-start | bytes 393224 | tf_op jit(solution)/shard_map/ppermute | solution.py:31
  12.0 0.0 collective-permute-done
  12.0 0.0 collective-permute-done.4
  12.2 0.1 fusion.4
  12.3 2.8 %collective-permute-done.5 = f32[4,64,256]{2,1,0:T(8,128)S(1)} collective-permute-done((f32[4,64,256]{2,1,0:T(8,128)S(1)}, f32[4,64,256]{2,1,0:T(8,128)S(1)}, u32[]{:S(2)}, u32[]{:S(2)}) %collective-permute-start.5) | collective-permute-done | bytes 262176 | tf_op jit(solution)/shard_map/ppermute | solution.py:31
  15.1 0.4 broadcast_select_fusion.8
  15.5 1.3 %collective-permute-start.14 = (f32[256,128]{1,0:T(8,128)S(1)}, f32[256,128]{1,0:T(8,128)S(1)}, u32[]{:S(2)}, u32[]{:S(2)}) collective-permute-start(f32[256,128]{1,0:T(8,128)S(1)} %get-tuple-element.70), channel_id=1, source_target_pairs={{0,16},{1,17},{2,18},{3,19},{4,20},{5,21},{6,22},{7,23}} | collective-permute-start | bytes 393224 | tf_op jit(solution)/shard_map/ppermute | solution.py:31
  16.8 0.7 %collective-permute-start.7 = (f32[2,3,64,256]{3,2,1,0:T(8,128)S(1)}, f32[2,3,64,256]{3,2,1,0:T(8,128)S(1)}, u32[]{:S(2)}, u32[]{:S(2)}) collective-permute-start(f32[2,3,64,256]{3,2,1,0:T(8,128)S(1)} %fusion.5), channel_id=1, source_target_pairs={{8,12},{9,13},{10,14},{11,15},{12,8},{13,9},{14,10},{15,11}} | collective-permute-start | bytes 1179656 | tf_op jit(solution)/shard_map/ppermute | solution.py:31
  17.5 1.9 %collective-permute-start.6 = (f32[2,4,64,256]{3,2,1,0:T(8,128)S(1)}, f32[2,4,64,256]{3,2,1,0:T(8,128)S(1)}, u32[]{:S(2)}, u32[]{:S(2)}) collective-permute-start(f32[2,4,64,256]{3,2,1,0:T(8,128)S(1)} %pad_maximum_fusion), channel_id=1, source_target_pairs={{8,9},{9,8},{10,11},{11,10},{12,13},{13,12},{14,15},{15,14},{16,17... | collective-permute-start | bytes 1572872 | tf_op jit(solution)/shard_map/ppermute | solution.py:31
  19.5 0.7 %collective-permute-start.13 = (f32[256,128]{1,0:T(8,128)S(1)}, f32[256,128]{1,0:T(8,128)S(1)}, u32[]{:S(2)}, u32[]{:S(2)}) collective-permute-start(f32[256,128]{1,0:T(8,128)S(1)} %get-tuple-element.71), channel_id=1, source_target_pairs={{0,8},{1,9},{2,10},{3,11},{4,12},{5,13},{6,14},{7,15}} | collective-permute-start | bytes 393224 | tf_op jit(solution)/shard_map/ppermute | solution.py:31
  20.2 0.0 collective-permute-done.10
  20.2 0.6 %convolution_subtract_fusion.6 = f32[256,128]{1,0:T(8,128)S(1)} fusion(f32[128,256]{1,0:T(8,128)S(1)} %collective-permute-done.10, f32[128,256]{1,0:T(8,128)S(1)} %bitcast.94, f32[64,128]{1,0:T(8,128)S(1)} %get-tuple-element.59, f32[64,128]{1,0:T(8,128)S(1)} %get-tuple-element.60, f32[64,128]{1,0:T(8,128)S(1)} %get-tuple-element.61, ...), kind=kOutput, calls=%fused_computation.10 | convolution fusion | flops 100925440 | bytes 786433 | tf_op jit(solution)/shard_map/dot_general | solution.py:10
  20.8 11.4 %collective-permute-done.14 = f32[256,128]{1,0:T(8,128)S(1)} collective-permute-done((f32[256,128]{1,0:T(8,128)S(1)}, f32[256,128]{1,0:T(8,128)S(1)}, u32[]{:S(2)}, u32[]{:S(2)}) %collective-permute-start.14) | collective-permute-done | bytes 131104 | tf_op jit(solution)/shard_map/ppermute | solution.py:31
  32.2 0.4 broadcast_select_fusion.7
  32.6 0.7 %collective-permute-start.11 = (f32[256,128]{1,0:T(8,128)S(1)}, f32[256,128]{1,0:T(8,128)S(1)}, u32[]{:S(2)}, u32[]{:S(2)}) collective-permute-start(f32[256,128]{1,0:T(8,128)S(1)} %get-tuple-element.73), channel_id=1, source_target_pairs={{0,8},{1,9},{2,10},{3,11},{4,12},{5,13},{6,14},{7,15}} | collective-permute-start | bytes 393224 | tf_op jit(solution)/shard_map/ppermute | solution.py:31
  33.3 1.9 %collective-permute-start.15 = (f32[256,128]{1,0:T(8,128)S(1)}, f32[256,128]{1,0:T(8,128)S(1)}, u32[]{:S(2)}, u32[]{:S(2)}) collective-permute-start(f32[256,128]{1,0:T(8,128)S(1)} %get-tuple-element.72), channel_id=1, source_target_pairs={{0,16},{1,17},{2,18},{3,19},{4,20},{5,21},{6,22},{7,23},{16,24},{1... | collective-permute-start | bytes 393224 | tf_op jit(solution)/shard_map/ppermute | solution.py:31
  35.3 0.0 collective-permute-done.13
  35.3 0.0 collective-permute-done.11
  35.3 0.0 collective-permute-done.7
  35.4 0.7 %collective-permute-start.12 = (f32[2,3,64,256]{3,2,1,0:T(8,128)S(1)}, f32[2,3,64,256]{3,2,1,0:T(8,128)S(1)}, u32[]{:S(2)}, u32[]{:S(2)}) collective-permute-start(f32[2,3,64,256]{3,2,1,0:T(8,128)S(1)} %collective-permute-done.7), channel_id=1, source_target_pairs={{8,9},{9,8},{10,11},{11,10},{12,13},{13,12},{14,15},{15,14}} | collective-permute-start | bytes 1179656 | tf_op jit(solution)/shard_map/ppermute | solution.py:31
  36.1 0.0 collective-permute-done.6
  36.1 0.0 collective-permute-done.12
  36.2 0.6 %fusion.18 = f32[256,128]{1,0:T(8,128)S(1)} fusion(f32[128,256]{1,0:T(8,128)S(1)} %bitcast.90, f32[128,256]{1,0:T(8,128)S(1)} %bitcast.88, f32[128,256]{1,0:T(8,128)S(1)} %bitcast.74, f32[128,256]{1,0:T(8,128)S(1)} %bitcast.68, pred[]{:T(512)S(6)} %eq.40, f32[64,128]{1,0:T(8,128)S(1)} %get-tuple-element.51, f32[64,128]{1,0:T(8,128)S(1)} %get-tuple-element.52, ...), kind=kOutput, calls=%fused_computation.49 | convolution fusion | flops 100958208 | bytes 786433 | tf_op jit(solution)/shard_map/dot_general | solution.py:10
  36.8 0.6 %fusion.3 = f32[256,128]{1,0:T(8,128)S(1)} fusion(f32[256,128]{1,0:T(8,128)S(1)} %fusion.18, f32[128,256]{1,0:T(8,128)S(1)} %bitcast.86, f32[128,256]{1,0:T(8,128)S(1)} %bitcast.84, f32[128,256]{1,0:T(8,128)S(1)} %bitcast.77, f32[128,256]{1,0:T(8,128)S(1)} %bitcast.71, pred[]{:T(512)S(6)} %eq.40, f32[64,128]{1,0:T(8,128)S(1)} %get-tuple-element.47, ...), kind=kOutput, calls=%fused_computation.9 | convolution fusion | flops 101089280 | bytes 1179649 | tf_op jit(solution)/shard_map/dot_general | solution.py:10
  37.4 0.6 %fusion.15 = f32[256,128]{1,0:T(8,128)S(1)} fusion(f32[128,256]{1,0:T(8,128)S(1)} %bitcast.91, f32[128,256]{1,0:T(8,128)S(1)} %bitcast.89, f32[128,256]{1,0:T(8,128)S(1)} %bitcast.75, f32[128,256]{1,0:T(8,128)S(1)} %bitcast.69, pred[]{:T(512)S(6)} %eq.40, f32[64,128]{1,0:T(8,128)S(1)} %get-tuple-element.51, f32[64,128]{1,0:T(8,128)S(1)} %get-tuple-element.52, ...), kind=kOutput, calls=%fused_computation.46 | convolution fusion | flops 100958208 | bytes 786433 | tf_op jit(solution)/shard_map/dot_general | solution.py:10
  38.0 3.1 %collective-permute-done.15 = f32[256,128]{1,0:T(8,128)S(1)} collective-permute-done((f32[256,128]{1,0:T(8,128)S(1)}, f32[256,128]{1,0:T(8,128)S(1)}, u32[]{:S(2)}, u32[]{:S(2)}) %collective-permute-start.15) | collective-permute-done | bytes 131104 | tf_op jit(solution)/shard_map/ppermute | solution.py:31
  41.1 0.4 broadcast_select_fusion.6
  41.5 1.9 %collective-permute-start.16 = (f32[256,128]{1,0:T(8,128)S(1)}, f32[256,128]{1,0:T(8,128)S(1)}, u32[]{:S(2)}, u32[]{:S(2)}) collective-permute-start(f32[256,128]{1,0:T(8,128)S(1)} %get-tuple-element.74), channel_id=1, source_target_pairs={{8,16},{9,17},{10,18},{11,19},{12,20},{13,21},{14,22},{15,23},{16,... | collective-permute-start | bytes 393224 | tf_op jit(solution)/shard_map/ppermute | solution.py:31
  43.4 0.6 %fusion.9 = f32[256,128]{1,0:T(8,128)S(1)} fusion(f32[128,256]{1,0:T(8,128)S(1)} %bitcast.98, f32[128,256]{1,0:T(8,128)S(1)} %bitcast.97, f32[128,256]{1,0:T(8,128)S(1)} %bitcast.82, f32[128,256]{1,0:T(8,128)S(1)} %bitcast.80, f32[64,128]{1,0:T(8,128)S(1)} %get-tuple-element.32, f32[64,128]{1,0:T(8,128)S(1)} %get-tuple-element.33, ...), kind=kOutput, calls=%fused_computation.39 | convolution fusion | flops 100958208 | bytes 786433 | tf_op jit(solution)/shard_map/dot_general | solution.py:10
  44.0 0.6 %fusion.2 = f32[256,128]{1,0:T(8,128)S(1)} fusion(f32[256,128]{1,0:T(8,128)S(1)} %fusion.9, f32[256,128]{1,0:T(8,128)S(1)} %fusion.15, f32[128,256]{1,0:T(8,128)S(1)} %bitcast.87, f32[128,256]{1,0:T(8,128)S(1)} %bitcast.85, f32[128,256]{1,0:T(8,128)S(1)} %bitcast.78, f32[128,256]{1,0:T(8,128)S(1)} %bitcast.72, pred[]{:T(512)S(6)} %eq.40, ...), kind=kOutput, calls=%fused_computation.7 | convolution fusion | flops 101122048 | bytes 1310721 | tf_op jit(solution)/shard_map/dot_general | solution.py:10
  44.6 0.4 fusion.23
  45.0 0.7 %collective-permute-start.18 = (f32[256,128]{1,0:T(8,128)S(1)}, f32[256,128]{1,0:T(8,128)S(1)}, u32[]{:S(2)}, u32[]{:S(2)}) collective-permute-start(f32[256,128]{1,0:T(8,128)S(1)} %fusion.23), channel_id=1, source_target_pairs={{8,24},{9,25},{10,26},{11,27},{12,28},{13,29},{14,30},{15,31}} | collective-permute-start | bytes 393224 | tf_op jit(solution)/shard_map/ppermute | solution.py:31
  45.7 1.3 %collective-permute-start.19 = (f32[256,128]{1,0:T(8,128)S(1)}, f32[256,128]{1,0:T(8,128)S(1)}, u32[]{:S(2)}, u32[]{:S(2)}) collective-permute-start(f32[256,128]{1,0:T(8,128)S(1)} %fusion.23), channel_id=1, source_target_pairs={{8,16},{9,17},{10,18},{11,19},{12,20},{13,21},{14,22},{15,23}} | collective-permute-start | bytes 393224 | tf_op jit(solution)/shard_map/ppermute | solution.py:31
  47.0 2.9 %collective-permute-done.16 = f32[256,128]{1,0:T(8,128)S(1)} collective-permute-done((f32[256,128]{1,0:T(8,128)S(1)}, f32[256,128]{1,0:T(8,128)S(1)}, u32[]{:S(2)}, u32[]{:S(2)}) %collective-permute-start.16) | collective-permute-done | bytes 131104 | tf_op jit(solution)/shard_map/ppermute | solution.py:31
  49.9 1.3 %collective-permute-start.17 = (f32[256,128]{1,0:T(8,128)S(1)}, f32[256,128]{1,0:T(8,128)S(1)}, u32[]{:S(2)}, u32[]{:S(2)}) collective-permute-start(f32[256,128]{1,0:T(8,128)S(1)} %collective-permute-done.16), channel_id=1, source_target_pairs={{16,24},{17,25},{18,26},{19,27},{20,28},{21,29},{22,30},{23,31}} | collective-permute-start | bytes 393224 | tf_op jit(solution)/shard_map/ppermute | solution.py:31
  51.2 0.0 collective-permute-done.18
  51.2 4.4 %collective-permute-done.19 = f32[256,128]{1,0:T(8,128)S(1)} collective-permute-done((f32[256,128]{1,0:T(8,128)S(1)}, f32[256,128]{1,0:T(8,128)S(1)}, u32[]{:S(2)}, u32[]{:S(2)}) %collective-permute-start.19) | collective-permute-done | bytes 131104 | tf_op jit(solution)/shard_map/ppermute | solution.py:31
  55.7 0.0 collective-permute-done.17
  55.8 0.6 %convolution_subtract_fusion.3 = f32[256,128]{1,0:T(8,128)S(1)} fusion(f32[256,128]{1,0:T(8,128)S(1)} %copy-done, f32[128,256]{1,0:T(8,128)S(1)} %bitcast.79, f32[128,256]{1,0:T(8,128)S(1)} %bitcast.73, f32[64,128]{1,0:T(8,128)S(1)} %get-tuple-element.55, f32[64,128]{1,0:T(8,128)S(1)} %get-tuple-element.56, f32[64,128]{1,0:T(8,128)S(1)} %get-tuple-element.57, ...), kind=kOutput, calls=%fused_computation.4 | convolution fusion | flops 100859904 | bytes 655360 | tf_op jit(solution)/shard_map/dot_general | solution.py:10
  56.4 0.6 %convolution_subtract_fusion.2 = f32[256,128]{1,0:T(8,128)S(1)} fusion(f32[256,128]{1,0:T(8,128)S(1)} %convolution_subtract_fusion.3, f32[128,256]{1,0:T(8,128)S(1)} %bitcast.76, f32[128,256]{1,0:T(8,128)S(1)} %bitcast.70, f32[64,128]{1,0:T(8,128)S(1)} %get-tuple-element.43, f32[64,128]{1,0:T(8,128)S(1)} %get-tuple-element.44, ...), kind=kOutput, calls=%fused_computation.3 | convolution fusion | flops 100859904 | bytes 655360 | tf_op jit(solution)/shard_map/dot_general | solution.py:10
  57.0 0.6 %convolution_subtract_fusion.1 = f32[256,128]{1,0:T(8,128)S(1)} fusion(f32[256,128]{1,0:T(8,128)S(1)} %convolution_subtract_fusion.2, f32[128,256]{1,0:T(8,128)S(1)} %bitcast.83, f32[128,256]{1,0:T(8,128)S(1)} %bitcast.81, f32[64,128]{1,0:T(8,128)S(1)} %get-tuple-element.36, f32[64,128]{1,0:T(8,128)S(1)} %get-tuple-element.37, ...), kind=kOutput, calls=%fused_computation.2 | convolution fusion | flops 100859904 | bytes 655360 | tf_op jit(solution)/shard_map/dot_general | solution.py:10
  57.6 1.3 %fusion = f32[256,128]{1,0:T(8,128)} fusion(f32[256,128]{1,0:T(8,128)S(1)} %convolution_subtract_fusion.1, f32[128,256]{1,0:T(8,128)S(1)} %bitcast.96, f32[128,256]{1,0:T(8,128)S(1)} %bitcast.95, f32[64,128]{1,0:T(8,128)S(1)} %get-tuple-element.28, f32[64,128]{1,0:T(8,128)S(1)} %get-tuple-element.29, f32[64,128]{1,0:T(8,128)S(1)} %get-tuple-element.30, ...), kind=kOutput, calls=%fused_computation.1 | convolution fusion | flops 100990976 | bytes 1179651 | tf_op jit(solution)/shard_map/dot_general | solution.py:10
  (29 shorter events, 0.7 us)
Async XLA Ops:
  0.0 0.9 %copy-start.2 = (f32[4,32,256]{2,1,0:T(8,128)S(1)}, f32[4,32,256]{2,1,0:T(8,128)}, u32[]{:S(2)}) copy-start(f32[4,32,256]{2,1,0:T(8,128)} %param.5) | copy-start | bytes 393220
  0.9 3.9 %copy-start.1 = (f32[256,4,64]{0,2,1:T(8,128)S(1)}, f32[256,4,64]{0,2,1:T(8,128)}, u32[]{:S(2)}) copy-start(f32[256,4,64]{0,2,1:T(8,128)} %param.4) | copy-start | bytes 786436
  0.9 8.0 %copy-start = (f32[256,128]{1,0:T(8,128)S(1)}, f32[256,128]{1,0:T(8,128)}, u32[]{:S(2)}) copy-start(f32[256,128]{1,0:T(8,128)} %param.3) | copy-start | bytes 393220
  0.9 8.9 %collective-permute-start.1 = (f32[2,32,256]{2,1,0:T(8,128)S(1)}, f32[2,32,256]{2,1,0:T(8,128)S(1)}, u32[]{:S(2)}, u32[]{:S(2)}) collective-permute-start(f32[2,32,256]{2,1,0:T(8,128)S(1)} %get-tuple-element.67), channel_id=1, source_target_pairs={{8,0},{9,4},{10,2},{11,6},{12,1},{13,5},{14,3},{15,7},{16,8},{17,1... | collective-permute-start | bytes 196616 | tf_op jit(solution)/shard_map/ppermute | solution.py:31
  2.8 7.7 %collective-permute-start.2 = (f32[2,32,256]{2,1,0:T(8,128)S(1)}, f32[2,32,256]{2,1,0:T(8,128)S(1)}, u32[]{:S(2)}, u32[]{:S(2)}) collective-permute-start(f32[2,32,256]{2,1,0:T(8,128)S(1)} %get-tuple-element.69), channel_id=1, source_target_pairs={{16,0},{17,4},{18,2},{19,6},{20,1},{21,5},{22,3},{23,7},{24,8},{25... | collective-permute-start | bytes 196616 | tf_op jit(solution)/shard_map/ppermute | solution.py:31
  4.1 6.4 %collective-permute-start.3 = (f32[2,32,256]{2,1,0:T(8,128)S(1)}, f32[2,32,256]{2,1,0:T(8,128)S(1)}, u32[]{:S(2)}, u32[]{:S(2)}) collective-permute-start(f32[2,32,256]{2,1,0:T(8,128)S(1)} %get-tuple-element.68), channel_id=1, source_target_pairs={{0,8},{1,12},{2,10},{3,14},{4,9},{5,13},{6,11},{7,15},{24,0},{25,4... | collective-permute-start | bytes 196616 | tf_op jit(solution)/shard_map/ppermute | solution.py:31
  4.8 10.2 %collective-permute-start.5 = (f32[4,64,256]{2,1,0:T(8,128)S(1)}, f32[4,64,256]{2,1,0:T(8,128)S(1)}, u32[]{:S(2)}, u32[]{:S(2)}) collective-permute-start(f32[4,64,256]{2,1,0:T(8,128)S(1)} %bitcast.59), channel_id=1, source_target_pairs={{8,10},{9,11},{10,8},{11,9},{12,14},{13,15},{14,12},{15,13},{16,18... | collective-permute-start | bytes 786440 | tf_op jit(solution)/shard_map/ppermute | solution.py:31
  8.3 0.7 %collective-permute-start.8 = (f32[64,256]{1,0:T(8,128)S(1)}, f32[64,256]{1,0:T(8,128)S(1)}, u32[]{:S(2)}, u32[]{:S(2)}) collective-permute-start(f32[64,256]{1,0:T(8,128)S(1)} %get-tuple-element.24), channel_id=1, source_target_pairs={{0,2},{1,3},{2,0},{3,1},{4,6},{5,7},{6,4},{7,5}} | collective-permute-start | bytes 196616 | tf_op jit(solution)/shard_map/ppermute | solution.py:31
  9.0 2.2 %collective-permute-start.9 = (f32[2,64,256]{2,1,0:T(8,128)S(1)}, f32[2,64,256]{2,1,0:T(8,128)S(1)}, u32[]{:S(2)}, u32[]{:S(2)}) collective-permute-start(f32[2,64,256]{2,1,0:T(8,128)S(1)} %pad_maximum_fusion.22), channel_id=1, source_target_pairs={{4,0},{5,1},{6,2},{7,3}} | collective-permute-start | bytes 393224 | tf_op jit(solution)/shard_map/ppermute | solution.py:31
  9.8 2.1 %collective-permute-start = (f32[192,256]{1,0:T(8,128)S(1)}, f32[192,256]{1,0:T(8,128)S(1)}, u32[]{:S(2)}, u32[]{:S(2)}) collective-permute-start(f32[192,256]{1,0:T(8,128)S(1)} %pad_maximum_fusion.13), channel_id=1, source_target_pairs={{0,4},{1,5},{2,6},{3,7},{4,0},{5,1},{6,2},{7,3},{8,12},{9,13},{10,... | collective-permute-start | bytes 589832 | tf_op jit(solution)/shard_map/ppermute | solution.py:31
  10.6 1.5 %collective-permute-start.4 = (f32[3,2,32,256]{3,2,0,1:T(8,128)S(1)}, f32[3,2,32,256]{3,2,0,1:T(8,128)S(1)}, u32[]{:S(2)}, u32[]{:S(2)}) collective-permute-start(f32[3,2,32,256]{3,2,0,1:T(8,128)S(1)} %pad_maximum_fusion.14), channel_id=1, source_target_pairs={{0,1},{1,0},{2,3},{3,2},{4,5},{5,4},{6,7},{7,6},{8,9},{9,8},{10,11... | collective-permute-start | bytes 589832 | tf_op jit(solution)/shard_map/ppermute | solution.py:31
  11.3 8.9 %collective-permute-start.10 = (f32[128,256]{1,0:T(8,128)S(1)}, f32[128,256]{1,0:T(8,128)S(1)}, u32[]{:S(2)}, u32[]{:S(2)}) collective-permute-start(f32[128,256]{1,0:T(8,128)S(1)} %bitcast.93), channel_id=1, source_target_pairs={{0,1},{1,0},{2,3},{3,2},{4,5},{5,4},{6,7},{7,6}} | collective-permute-start | bytes 393224 | tf_op jit(solution)/shard_map/ppermute | solution.py:31
  15.5 16.7 %collective-permute-start.14 = (f32[256,128]{1,0:T(8,128)S(1)}, f32[256,128]{1,0:T(8,128)S(1)}, u32[]{:S(2)}, u32[]{:S(2)}) collective-permute-start(f32[256,128]{1,0:T(8,128)S(1)} %get-tuple-element.70), channel_id=1, source_target_pairs={{0,16},{1,17},{2,18},{3,19},{4,20},{5,21},{6,22},{7,23}} | collective-permute-start | bytes 393224 | tf_op jit(solution)/shard_map/ppermute | solution.py:31
  16.8 18.5 %collective-permute-start.7 = (f32[2,3,64,256]{3,2,1,0:T(8,128)S(1)}, f32[2,3,64,256]{3,2,1,0:T(8,128)S(1)}, u32[]{:S(2)}, u32[]{:S(2)}) collective-permute-start(f32[2,3,64,256]{3,2,1,0:T(8,128)S(1)} %fusion.5), channel_id=1, source_target_pairs={{8,12},{9,13},{10,14},{11,15},{12,8},{13,9},{14,10},{15,11}} | collective-permute-start | bytes 1179656 | tf_op jit(solution)/shard_map/ppermute | solution.py:31
  17.5 18.5 %collective-permute-start.6 = (f32[2,4,64,256]{3,2,1,0:T(8,128)S(1)}, f32[2,4,64,256]{3,2,1,0:T(8,128)S(1)}, u32[]{:S(2)}, u32[]{:S(2)}) collective-permute-start(f32[2,4,64,256]{3,2,1,0:T(8,128)S(1)} %pad_maximum_fusion), channel_id=1, source_target_pairs={{8,9},{9,8},{10,11},{11,10},{12,13},{13,12},{14,15},{15,14},{16,17... | collective-permute-start | bytes 1572872 | tf_op jit(solution)/shard_map/ppermute | solution.py:31
  19.5 15.8 %collective-permute-start.13 = (f32[256,128]{1,0:T(8,128)S(1)}, f32[256,128]{1,0:T(8,128)S(1)}, u32[]{:S(2)}, u32[]{:S(2)}) collective-permute-start(f32[256,128]{1,0:T(8,128)S(1)} %get-tuple-element.71), channel_id=1, source_target_pairs={{0,8},{1,9},{2,10},{3,11},{4,12},{5,13},{6,14},{7,15}} | collective-permute-start | bytes 393224 | tf_op jit(solution)/shard_map/ppermute | solution.py:31
  32.6 2.7 %collective-permute-start.11 = (f32[256,128]{1,0:T(8,128)S(1)}, f32[256,128]{1,0:T(8,128)S(1)}, u32[]{:S(2)}, u32[]{:S(2)}) collective-permute-start(f32[256,128]{1,0:T(8,128)S(1)} %get-tuple-element.73), channel_id=1, source_target_pairs={{0,8},{1,9},{2,10},{3,11},{4,12},{5,13},{6,14},{7,15}} | collective-permute-start | bytes 393224 | tf_op jit(solution)/shard_map/ppermute | solution.py:31
  33.3 7.8 %collective-permute-start.15 = (f32[256,128]{1,0:T(8,128)S(1)}, f32[256,128]{1,0:T(8,128)S(1)}, u32[]{:S(2)}, u32[]{:S(2)}) collective-permute-start(f32[256,128]{1,0:T(8,128)S(1)} %get-tuple-element.72), channel_id=1, source_target_pairs={{0,16},{1,17},{2,18},{3,19},{4,20},{5,21},{6,22},{7,23},{16,24},{1... | collective-permute-start | bytes 393224 | tf_op jit(solution)/shard_map/ppermute | solution.py:31
  35.4 0.8 %collective-permute-start.12 = (f32[2,3,64,256]{3,2,1,0:T(8,128)S(1)}, f32[2,3,64,256]{3,2,1,0:T(8,128)S(1)}, u32[]{:S(2)}, u32[]{:S(2)}) collective-permute-start(f32[2,3,64,256]{3,2,1,0:T(8,128)S(1)} %collective-permute-done.7), channel_id=1, source_target_pairs={{8,9},{9,8},{10,11},{11,10},{12,13},{13,12},{14,15},{15,14}} | collective-permute-start | bytes 1179656 | tf_op jit(solution)/shard_map/ppermute | solution.py:31
  41.5 8.4 %collective-permute-start.16 = (f32[256,128]{1,0:T(8,128)S(1)}, f32[256,128]{1,0:T(8,128)S(1)}, u32[]{:S(2)}, u32[]{:S(2)}) collective-permute-start(f32[256,128]{1,0:T(8,128)S(1)} %get-tuple-element.74), channel_id=1, source_target_pairs={{8,16},{9,17},{10,18},{11,19},{12,20},{13,21},{14,22},{15,23},{16,... | collective-permute-start | bytes 393224 | tf_op jit(solution)/shard_map/ppermute | solution.py:31
  45.0 6.2 %collective-permute-start.18 = (f32[256,128]{1,0:T(8,128)S(1)}, f32[256,128]{1,0:T(8,128)S(1)}, u32[]{:S(2)}, u32[]{:S(2)}) collective-permute-start(f32[256,128]{1,0:T(8,128)S(1)} %fusion.23), channel_id=1, source_target_pairs={{8,24},{9,25},{10,26},{11,27},{12,28},{13,29},{14,30},{15,31}} | collective-permute-start | bytes 393224 | tf_op jit(solution)/shard_map/ppermute | solution.py:31
  45.7 9.9 %collective-permute-start.19 = (f32[256,128]{1,0:T(8,128)S(1)}, f32[256,128]{1,0:T(8,128)S(1)}, u32[]{:S(2)}, u32[]{:S(2)}) collective-permute-start(f32[256,128]{1,0:T(8,128)S(1)} %fusion.23), channel_id=1, source_target_pairs={{8,16},{9,17},{10,18},{11,19},{12,20},{13,21},{14,22},{15,23}} | collective-permute-start | bytes 393224 | tf_op jit(solution)/shard_map/ppermute | solution.py:31
  49.9 5.8 %collective-permute-start.17 = (f32[256,128]{1,0:T(8,128)S(1)}, f32[256,128]{1,0:T(8,128)S(1)}, u32[]{:S(2)}, u32[]{:S(2)}) collective-permute-start(f32[256,128]{1,0:T(8,128)S(1)} %collective-permute-done.16), channel_id=1, source_target_pairs={{16,24},{17,25},{18,26},{19,27},{20,28},{21,29},{22,30},{23,31}} | collective-permute-start | bytes 393224 | tf_op jit(solution)/shard_map/ppermute | solution.py:31

commit v3 on v0

v3 whole, which is shorter than its diff:
```python
import itertools

import jax
import jax.numpy as jnp
from jax import lax
from jax.experimental import pallas as pl
from jax.experimental.pallas import tpu as pltpu
from jax.sharding import PartitionSpec as P

AXES = ("row", "col")
VMEM = pl.BlockSpec(memory_space=pltpu.VMEM)
ANY = pl.BlockSpec(memory_space=pl.ANY)
FREE = pl.CostEstimate(flops=0, bytes_accessed=0, transcendentals=0)
LIMIT = 24 * 1024 * 1024


def split(value):
    high = value.astype(jnp.bfloat16)
    return high, (value - high.astype(jnp.float32)).astype(jnp.bfloat16)


def dot(left, right, over=1):
    (a, b), (c, d) = split(left), split(right)

    def one(u, v):
        return lax.dot_general(u, v, (((over,), (0,)), ((), ())), preferred_element_type=jnp.float32)

    return one(a, c) + (one(a, d) + one(b, c))


def call(body, shapes, held, first=(), last=(), home=False, scratch=()):
    out = [jax.ShapeDtypeStruct(s, jnp.float32) if home else pltpu.VMEM(s, jnp.float32) for s in shapes]
    n_in, n_last = len(first) + len(held), len(last)

    def kernel(*refs):
        body(*refs[:n_in], *refs[n_in + n_last :])

    got = pl.pallas_call(
        kernel,
        out_shape=out,
        in_specs=[ANY] * len(first) + [VMEM] * len(held) + [ANY] * n_last,
        out_specs=[VMEM] * len(shapes),
        scratch_shapes=scratch,
        cost_estimate=FREE,
        compiler_params=pltpu.CompilerParams(vmem_limit_bytes=LIMIT),
    )(*[pltpu.with_memory_space_constraint(v, pltpu.HBM) for v in first], *[pltpu.with_memory_space_constraint(v, pltpu.VMEM) for v in held], *last)
    return got[0] if len(shapes) == 1 else got


def solution(mesh):
    n_row, n_col = mesh.shape["row"], mesh.shape["col"]
    n_pair, n_half = n_row // 2, n_col // 2

    def place():
        row, col = lax.axis_index("row"), lax.axis_index("col")
        return row // 2, row % 2, col // 2, col % 2

    def hop(value, move):
        edges = []
        for q in range(n_pair):
            for x in range(2):
                for j in range(n_half):
                    for k in range(2):
                        a, b, c, d = move(q, x, j, k)
                        edges.append(((q * 2 + x) * n_col + j * 2 + k, (a * 2 + b) * n_col + c * 2 + d))
        return lax.ppermute(value, AXES, edges)

    def along(value):
        return [hop(value, lambda q, x, j, k, s=s: (q, x, (j + s) % n_half, k)) for s in range(1, n_half)]

    def swap_rows(value):
        return hop(value, lambda q, x, j, k: (q, 1 - x, j, k))

    def swap_cores(value):
        return hop(value, lambda q, x, j, k: (q, x, j, 1 - k))

    def climb(value, w, t):
        free = [q for q in range(n_pair) if q != w]
        ends = [q for q in range(n_pair) if q != t]
        if n_pair <= 6:
            choices = itertools.permutations(ends)
        else:
            choices = (ends[r:] + ends[:r] for r in range(len(ends)))
        choices = [c for c in choices if all(a != b for a, b in zip(free, c, strict=True))]
        best = min(choices, key=lambda c: sum(max(b - a, 0) for a, b in zip(free, c, strict=True)))
        to = dict(zip(free, best, strict=True)) | {w: t}
        return hop(value, lambda q, x, j, k: (to[q], x, j, k))

    def body(rhs, factor, inverses):
        rows, n_pan, part = factor.shape
        width = rhs.shape[1]
        shard, wide = inverses.shape[1:]
        n_win, near = n_pan // 2, n_pan - 1
        half, units, pair = rows // 2, near * part, 2 * shard
        at_head = half + pair
        at_parts = (n_pair - 1) * pair

        def unfold(ref):
            return jnp.concatenate([ref[:half, :width], ref[:half, width:]])

        def arrived(values):
            got = values[0]
            for i, value in enumerate(values[1:], 1):
                got = jnp.where(place()[0] == n_pair - 1 - i, value, got)
            return got

        def ordered(refs, at=0):
            q, x, j, k = place()
            got = []
            for c in (k, 1 - k):
                for s in range(n_half):
                    start = pl.multiple_of((lax.rem(j - s + n_half, n_half) * 2 + c) * part + at, part)
                    got.append(arrived([ref[pl.ds(start, part), :] for ref in refs]))
            return jnp.concatenate(got)

        def turn(value):
            q, step = place()[0], 1
            while step < n_pair:
                run = step * pair
                pieces = [value[at : at + run] for at in range(0, n_pair * pair, run)]
                other = [pieces[i ^ 1] for i in range(len(pieces))]
                value = jnp.where((q // step) % 2 == 1, jnp.concatenate(other), value)
                step *= 2
            return value

        across = jnp.transpose(factor, (1, 2, 0)).reshape(-1, rows)

        def prepare(rhs, across, inverses, packed, own, here, mine, *refs):
            sent, panels, sems = refs[:-2], refs[-2], refs[-1]
            q = place()[0]
            copies = [
                pltpu.make_async_copy(a, b, sems.at[i])
                for i, (a, b) in enumerate(((rhs, here), (inverses, panels), (across, own)))
            ]
            for copy in copies:
                copy.start()
            copies[0].wait()
            packed[:half] = jnp.concatenate([here[:half], here[half:]], axis=1)
            copies[1].wait()

            def both(target):
                first = 2 * jnp.minimum(target, n_win - 1)
                return jnp.concatenate([panels[first], panels[first + 1]])

            for s, ref in enumerate(sent, 1):
                ref[...] = both(jnp.bitwise_xor(q, s))
            mine[...] = both(q)
            packed[half:at_head] = mine[...]
            copies[2].wait()
            packed[at_head:] = own[:part]

        packed, own, rhs, mine, *sent = call(
            prepare,
            [(at_head + part, wide), (n_pan * part, rows), (rows, width)]
            + [(pair, wide)] * n_pair,
            [],
            first=[rhs, across, inverses],
            scratch=[pltpu.VMEM((n_pan, shard, wide), jnp.float32), pltpu.SemaphoreType.DMA((3,))],
        )

        beside = swap_rows(packed)
        parts = [
            hop(sent[s - 1], lambda q, x, j, k, s=s: (q ^ s, k, j, x)) for s in range(1, n_pair)
        ]

        def cut(own, tail):
            tail[...] = own[part:units]

        tail = call(cut, [(units - part, rows)], [own])
        tail_beside = swap_rows(tail)

        def pick_head(own, beside, head):
            head[...] = jnp.where(place()[1] == 0, beside[at_head:], own[:part])

        head = call(pick_head, [(part, rows)], [own, beside])
        head_along = along(head)

        own_along = along(own)

        def join(beside, tail, joined):
            joined[:part] = beside[at_head:]
            joined[part:] = tail[...]

        joined = call(join, [(units, rows)], [beside, tail_beside])
        joined_along = along(joined)

        def pack(*refs):
            packed = refs[-1]
            for s in range(n_pair - 1):
                packed[s * pair : (s + 1) * pair] = refs[s][...]
            for s in range(n_half):
                packed[at_parts + s * part : at_parts + (s + 1) * part] = refs[n_pair - 1 + s][...]

        packed = call(pack, [(at_parts + n_half * part, wide)], [*parts, head, *head_along])
        other = swap_cores(packed)

        def solve_first(packed, other, mine, beside, rhs, solved, inverse):
            q, x, j, k = place()
            theirs = beside[half:at_head]
            for m in range(2):
                at = m * shard
                got = [mine[at : at + shard], theirs[at : at + shard]]
                got = [jnp.where(x == 0, got[0], got[1]), jnp.where(x == 0, got[1], got[0])]
                for s in range(n_pair - 1):
                    a, b = (ref[s * pair + at : s * pair + at + shard] for ref in (packed, other))
                    got += [jnp.where(k == 0, a, b), jnp.where(k == 0, b, a)]
                inverse[m] = jnp.concatenate(got)
            a, b = rhs[...], unfold(beside)
            first = turn(dot(inverse[0], jnp.where(x == 0, a, b)))
            solved[:rows] = first
            panel = jnp.concatenate([packed[at_parts:], other[at_parts:]])
            left = jnp.where(x == 0, b, a) - dot(panel, ordered([solved]), 0)
            second = turn(dot(inverse[1], left))
            solved[rows:] = second

        solved, inverse = call(
            solve_first, [(2 * rows, width), (2, wide, wide)], [packed, other, mine, beside, rhs]
        )

        def choose(solved, either):
            either[...] = jnp.where(place()[1] == 0, solved[:rows], solved[rows:])

        known = [climb(solved, 0, 1)]
        either = call(choose, [(rows, width)], [solved])
        results = [either]

        whole = n_pan * part

        def stack(*refs):
            at = 0
            for ref in refs[:-1]:
                refs[-1][at : at + ref.shape[0]] = ref[...]
                at += ref.shape[0]

        soon = call(stack, [(n_half * whole + units, rows)], [own, *own_along, joined])
        soon = (soon, swap_cores(soon))
        late = call(stack, [((n_half - 1) * units, rows)], joined_along, last=[either])
        late = (late, swap_cores(late))
        blocks = [soon[0], soon[1], late[0], late[1]]

        def columns(blocks, theirs, panel, count=1):
            got = []
            for p in range(panel, panel + count):
                for core in range(2):
                    for s in range(n_half):
                        ref, at = blocks[core], s * whole
                        if theirs:
                            at = n_half * whole
                            if s:
                                ref, at = blocks[2 + core], (s - 1) * units
                        got.append(ref[at + p * part : at + (p + 1) * part])
            return jnp.concatenate(got)

        def lift(value, w):
            return [climb(value, w, t) for t in range(n_pair - 1, n_win - 1, -1)]

        lifted = [lift(either, 0)]
        for w in range(1, n_win):

            def solve_next(inverse, beside, rhs, *refs, w=w):
                blocks, known, (solved, either) = refs[:4], refs[4:-2], refs[-2:]
                x = place()[1]
                turned = [ordered([ref], at) for ref in known for at in (0, rows)]
                lefts = [
                    start - dot(columns(blocks, theirs, 0, 2 * w), jnp.concatenate(turned), 0)
                    for theirs, start in ((False, rhs[...]), (True, unfold(beside)))
                ]
                first = turn(dot(inverse[0], jnp.where(x == 0, lefts[0], lefts[1])))
                solved[:rows] = first
                block = jnp.where(
                    x == 0, columns(blocks, True, 2 * w), columns(blocks, False, 2 * w)
                )
                left = jnp.where(x == 0, lefts[1], lefts[0]) - dot(block, ordered([solved]), 0)
                second = turn(dot(inverse[1], left))
                solved[rows:] = second
                either[...] = jnp.where(x == 0, first, second)

            solved, either = call(
                solve_next,
                [(2 * rows, width), (rows, width)],
                [inverse, beside, rhs, *blocks, *known],
            )
            results.append(either)
            if w + 1 < n_win:
                lifted.append(lift(either, w))
                known = [climb(v, w, w + 1) for v in known + [solved]]
        final = lift(solved, n_win - 1)

        def gather(*refs):
            refs[-1][...] = arrived([ref[...] for ref in refs[:-1]])

        early = []
        for v in lifted:
            v = call(gather, [(rows, width)], v, last=[solved])
            early += [v, swap_rows(v)]

        def update(rhs, *refs):
            blocks, early, out = refs[:4], refs[4:-1], refs[-1]
            x = place()[1]
            turned = []
            for v, t in zip(early[::2], early[1::2], strict=True):
                a, b = ordered([v]), ordered([t])
                turned += [jnp.where(x == 0, a, b), jnp.where(x == 0, b, a)]
            out[...] = rhs[...] - dot(columns(blocks, False, 0, len(turned)), jnp.concatenate(turned), 0)

        left = call(update, [(rows, width)], [rhs, *blocks, *early])

        def finish(left, *refs):
            blocks, results, final, out = refs[:4], refs[4 : 4 + n_win], refs[4 + n_win : -1], refs[-1]
            q = place()[0]
            turned = jnp.concatenate([ordered(final), ordered(final, rows)])
            out[...] = left[...] - dot(columns(blocks, False, n_pan - 2, 2), turned, 0)
            for w in range(n_win):

                @pl.when(q == w)
                def _(w=w):
                    out[...] = results[w][...]

        return call(finish, [(rows, width)], [left, *blocks, *results, *final], home=True)

    placed = (P("row", "col"), P("row", None, "col"), P(None, "row", None))
    return jax.shard_map(body, mesh=mesh, in_specs=placed, out_specs=P("row", "col"), check_vma=False)
```

time: 351 us -> 55.3 us (0.16)
  the two profiles are of different devices: /device:TPU:18 before, /device:TPU:0 now
where the time goes in v3:
time: 55.3 us; the launch traced here: 55.1 us
  waiting for transfers between devices  29.4 us (53%)
  starting transfers between devices  20.5 us (37%)
  Pallas kernels  5.09 us (9%)
    ppermute x17, waiting for transfers between devices, hop(): return lax.ppermute(value, AXES, edges)  29.4 us
    ppermute x17, starting transfers between devices, hop(): return lax.ppermute(value, AXES, edges)  20.5 us
    pallas_call x13, Pallas kernels, call(): pl.pallas_call(kernel, out_shape=out, in_specs=[ANY] * len(first) + [VMEM...  5.09 us
  transfers between devices with their start and end apart: 17, of which 9 were waited for; matrix products, arithmetic and copies ran while one was open for 0% of the time, Pallas kernels for 5%

profile of v3, /device:TPU:0, one launch (start us, length us, event | category | flops | bytes accessed | tf_op | source)
XLA Modules:
  0.0 55.1 jit_solution(9609328276619630151)
XLA Ops:
  0.0 1.1 %shard_map.37 = (f32[256,256]{1,0:T(8,128)S(1)}, f32[256,256]{1,0:T(8,128)S(1)}, f32[256,128]{1,0:T(8,128)S(1)}, f32[64,256]{1,0:T(8,128)S(1)}, f32[64,256]{1,0:...) custom-call(f32[256,128]{1,0:T(8,128)} %refs_0_.1, f32[256,256]{1,0:T(8,128)} %bitcast.3, f32[4,32,256]{2,1,0:T(8,128)} %refs_2_.1), custom_call_target="tpu_custom_call" | custom-call | tf_op jit(solution)/shard_map/pallas_call | solution.py:38
  1.1 3.0 %collective-permute-start.1 = (f32[256,256]{1,0:T(8,128)S(1)}, f32[256,256]{1,0:T(8,128)S(1)}, u32[]{:S(2)}, u32[]{:S(2)}) collective-permute-start(f32[256,256]{1,0:T(8,128)S(1)} %get-tuple-element.18), channel_id=1, source_target_pairs={{0,4},{1,5},{2,6},{3,7},{4,0},{5,1},{6,2},{7,3},{8,12},{9,13},{10,... | collective-permute-start | bytes 786440 | tf_op jit(solution)/shard_map/ppermute | solution.py:66
  4.1 1.5 %collective-permute-start = (f32[256,256]{1,0:T(8,128)S(1)}, f32[256,256]{1,0:T(8,128)S(1)}, u32[]{:S(2)}, u32[]{:S(2)}) collective-permute-start(f32[256,256]{1,0:T(8,128)S(1)} %get-tuple-element.17.refs_0_), channel_id=1, source_target_pairs={{0,2},{1,3},{2,0},{3,1},{4,6},{5,7},{6,4},{7,5},{8,10},{9,11},{10,... | collective-permute-start | bytes 786440 | tf_op jit(solution)/shard_map/ppermute | solution.py:66
  5.7 0.6 %collective-permute-start.2 = (f32[128,256]{1,0:T(8,128)S(1)}, f32[128,256]{1,0:T(8,128)S(1)}, u32[]{:S(2)}, u32[]{:S(2)}) collective-permute-start(f32[128,256]{1,0:T(8,128)S(1)} %shard_map.38), channel_id=1, source_target_pairs={{0,4},{1,5},{2,6},{3,7},{4,0},{5,1},{6,2},{7,3},{8,12},{9,13},{10,... | collective-permute-start | bytes 393224 | tf_op jit(solution)/shard_map/ppermute | solution.py:66
  6.3 7.0 %collective-permute-done.2.refs_1_ = f32[128,256]{1,0:T(8,128)S(1)} collective-permute-done((f32[128,256]{1,0:T(8,128)S(1)}, f32[128,256]{1,0:T(8,128)S(1)}, u32[]{:S(2)}, u32[]{:S(2)}) %collective-permute-start.2) | collective-permute-done | bytes 131104 | tf_op jit(solution)/shard_map/ppermute | solution.py:66
  13.2 0.0 collective-permute-done.1.refs_0_.refs_1_.refs_3_
  13.3 0.0 collective-permute-done.refs_1_
  13.3 0.1 collective-permute-start.3
  13.4 1.9 %collective-permute-start.5 = (f32[64,256]{1,0:T(8,128)S(1)}, f32[64,256]{1,0:T(8,128)S(1)}, u32[]{:S(2)}, u32[]{:S(2)}) collective-permute-start(f32[64,256]{1,0:T(8,128)S(1)} %get-tuple-element.19), channel_id=1, source_target_pairs={{0,8},{1,12},{2,10},{3,14},{4,9},{5,13},{6,11},{7,15},{8,0},{9,4},... | collective-permute-start | bytes 196616 | tf_op jit(solution)/shard_map/ppermute | solution.py:66
  15.3 2.6 %collective-permute-start.6 = (f32[64,256]{1,0:T(8,128)S(1)}, f32[64,256]{1,0:T(8,128)S(1)}, u32[]{:S(2)}, u32[]{:S(2)}) collective-permute-start(f32[64,256]{1,0:T(8,128)S(1)} %get-tuple-element.20), channel_id=1, source_target_pairs={{0,16},{1,20},{2,18},{3,22},{4,17},{5,21},{6,19},{7,23},{8,24},{9,... | collective-permute-start | bytes 196616 | tf_op jit(solution)/shard_map/ppermute | solution.py:66
  17.9 0.0 collective-permute-start.7
  17.9 1.8 %collective-permute-start.8 = (f32[64,256]{1,0:T(8,128)S(1)}, f32[64,256]{1,0:T(8,128)S(1)}, u32[]{:S(2)}, u32[]{:S(2)}) collective-permute-start(f32[64,256]{1,0:T(8,128)S(1)} %shard_map.41.refs_3_), channel_id=1, source_target_pairs={{0,2},{1,3},{2,0},{3,1},{4,6},{5,7},{6,4},{7,5},{8,10},{9,11},{10,... | collective-permute-start | bytes 196616 | tf_op jit(solution)/shard_map/ppermute | solution.py:66
  19.7 0.0 collective-permute-done.5.refs_0_
  19.7 2.6 %collective-permute-done.6.refs_1_ = f32[64,256]{1,0:T(8,128)S(1)} collective-permute-done((f32[64,256]{1,0:T(8,128)S(1)}, f32[64,256]{1,0:T(8,128)S(1)}, u32[]{:S(2)}, u32[]{:S(2)}) %collective-permute-start.6) | collective-permute-done | bytes 65568 | tf_op jit(solution)/shard_map/ppermute | solution.py:66
  22.3 1.7 %collective-permute-done.7.refs_2_ = f32[64,256]{1,0:T(8,128)S(1)} collective-permute-done((f32[64,256]{1,0:T(8,128)S(1)}, f32[64,256]{1,0:T(8,128)S(1)}, u32[]{:S(2)}, u32[]{:S(2)}) %collective-permute-start.7) | collective-permute-done | bytes 65568 | tf_op jit(solution)/shard_map/ppermute | solution.py:66
  24.1 0.0 collective-permute-done.8.refs_4_
  24.1 1.4 %collective-permute-start.9 = (f32[320,256]{1,0:T(8,128)S(1)}, f32[320,256]{1,0:T(8,128)S(1)}, u32[]{:S(2)}, u32[]{:S(2)}) collective-permute-start(f32[320,256]{1,0:T(8,128)S(1)} %shard_map.42.refs_0_), channel_id=1, source_target_pairs={{0,1},{1,0},{2,3},{3,2},{4,5},{5,4},{6,7},{7,6},{8,9},{9,8},{10,11... | collective-permute-start | bytes 983048 | tf_op jit(solution)/shard_map/ppermute | solution.py:66
  25.5 1.5 %collective-permute-start.4 = (f32[192,256]{1,0:T(8,128)S(1)}, f32[192,256]{1,0:T(8,128)S(1)}, u32[]{:S(2)}, u32[]{:S(2)}) collective-permute-start(f32[192,256]{1,0:T(8,128)S(1)} %shard_map.39.refs_2_), channel_id=1, source_target_pairs={{0,2},{1,3},{2,0},{3,1},{4,6},{5,7},{6,4},{7,5},{8,10},{9,11},{10,... | collective-permute-start | bytes 589832 | tf_op jit(solution)/shard_map/ppermute | solution.py:66
  27.0 0.0 collective-permute-done.9.refs_1_
  27.0 0.8 %shard_map.43 = (f32[512,128]{1,0:T(8,128)S(1)}, f32[2,256,256]{2,1,0:T(8,128)S(1)}) custom-call(f32[320,256]{1,0:T(8,128)S(1)} %shard_map.42.refs_0_, f32[320,256]{1,0:T(8,128)S(1)} %collective-permute-done.9.refs_1_, f32[64,256]{1,0:T(8,128)S(1)} %get-tuple-element.22.refs_2_, f32[256,256]{1,0:T(8,128)S(1)} %collective-permute-done.1.refs_0_.refs_1_.refs_3_, ...), custom_call_target="tpu_custom_call" | custom-call | tf_op jit(solution)/shard_map/pallas_call | solution.py:38
  27.9 0.8 %collective-permute-start.13 = (f32[512,128]{1,0:T(8,128)S(1)}, f32[512,128]{1,0:T(8,128)S(1)}, u32[]{:S(2)}, u32[]{:S(2)}) collective-permute-start(f32[512,128]{1,0:T(8,128)S(1)} %get-tuple-element.23.refs_0_), channel_id=1, source_target_pairs={{0,8},{1,9},{2,10},{3,11},{4,12},{5,13},{6,14},{7,15},{8,0},{9,1},... | collective-permute-start | bytes 786440 | tf_op jit(solution)/shard_map/ppermute | solution.py:66
  28.8 3.6 %collective-permute-done.4.refs_0_ = f32[192,256]{1,0:T(8,128)S(1)} collective-permute-done((f32[192,256]{1,0:T(8,128)S(1)}, f32[192,256]{1,0:T(8,128)S(1)}, u32[]{:S(2)}, u32[]{:S(2)}) %collective-permute-start.4) | collective-permute-done | bytes 196640 | tf_op jit(solution)/shard_map/ppermute | solution.py:66
  32.4 0.1 collective-permute-start.10
  32.5 1.7 %collective-permute-start.11 = (f32[256,128]{1,0:T(8,128)S(1)}, f32[256,128]{1,0:T(8,128)S(1)}, u32[]{:S(2)}, u32[]{:S(2)}) collective-permute-start(f32[256,128]{1,0:T(8,128)S(1)} %shard_map.44.refs_1_.refs_5_), channel_id=1, source_target_pairs={{0,24},{1,25},{2,26},{3,27},{4,28},{5,29},{6,30},{7,31},{8,0},{9,1... | collective-permute-start | bytes 393224 | tf_op jit(solution)/shard_map/ppermute | solution.py:66
  34.2 0.6 %collective-permute-start.12 = (f32[256,128]{1,0:T(8,128)S(1)}, f32[256,128]{1,0:T(8,128)S(1)}, u32[]{:S(2)}, u32[]{:S(2)}) collective-permute-start(f32[256,128]{1,0:T(8,128)S(1)} %shard_map.44.refs_1_.refs_5_), channel_id=1, source_target_pairs={{0,16},{1,17},{2,18},{3,19},{4,20},{5,21},{6,22},{7,23},{8,0},{9,1... | collective-permute-start | bytes 393224 | tf_op jit(solution)/shard_map/ppermute | solution.py:66
  34.8 0.0 collective-permute-done.10.refs_6_.refs_4_
  34.8 2.1 %collective-permute-done.13.refs_7_ = f32[512,128]{1,0:T(8,128)S(1)} collective-permute-done((f32[512,128]{1,0:T(8,128)S(1)}, f32[512,128]{1,0:T(8,128)S(1)}, u32[]{:S(2)}, u32[]{:S(2)}) %collective-permute-start.13) | collective-permute-done | bytes 262176 | tf_op jit(solution)/shard_map/ppermute | solution.py:66
  36.9 0.0 collective-permute-done.3.refs_4_.refs_2_
  36.9 1.5 %shard_map.46 = (f32[512,128]{1,0:T(8,128)S(1)}, f32[256,128]{1,0:T(8,128)S(1)}) custom-call(f32[2,256,256]{2,1,0:T(8,128)S(1)} %get-tuple-element.24.refs_0_, f32[256,256]{1,0:T(8,128)S(1)} %collective-permute-done.1.refs_0_.refs_1_.refs_3_, f32[256,128]{1,0:T(8,128)S(1)} %get-tuple-element.16.refs_4_.refs_2_.refs_0_, ...), custom_call_target="tpu_custom_call" | custom-call | tf_op jit(solution)/shard_map/pallas_call | solution.py:38
  38.4 0.2 collective-permute-start.15
  38.6 1.5 %collective-permute-start.16 = (f32[512,128]{1,0:T(8,128)S(1)}, f32[512,128]{1,0:T(8,128)S(1)}, u32[]{:S(2)}, u32[]{:S(2)}) collective-permute-start(f32[512,128]{1,0:T(8,128)S(1)} %get-tuple-element.25.refs_2_), channel_id=1, source_target_pairs={{0,8},{1,9},{2,10},{3,11},{4,12},{5,13},{6,14},{7,15},{8,16},{9,17... | collective-permute-start | bytes 786440 | tf_op jit(solution)/shard_map/ppermute | solution.py:66
  40.0 0.0 collective-permute-done.11.refs_0_
  40.0 2.0 %collective-permute-done.12.refs_1_ = f32[256,128]{1,0:T(8,128)S(1)} collective-permute-done((f32[256,128]{1,0:T(8,128)S(1)}, f32[256,128]{1,0:T(8,128)S(1)}, u32[]{:S(2)}, u32[]{:S(2)}) %collective-permute-start.12) | collective-permute-done | bytes 131104 | tf_op jit(solution)/shard_map/ppermute | solution.py:66
  42.0 1.3 %collective-permute-start.14 = (f32[256,128]{1,0:T(8,128)S(1)}, f32[256,128]{1,0:T(8,128)S(1)}, u32[]{:S(2)}, u32[]{:S(2)}) collective-permute-start(f32[256,128]{1,0:T(8,128)S(1)} %shard_map.47.refs_5_), channel_id=1, source_target_pairs={{0,4},{1,5},{2,6},{3,7},{4,0},{5,1},{6,2},{7,3},{8,12},{9,13},{10,... | collective-permute-start | bytes 393224 | tf_op jit(solution)/shard_map/ppermute | solution.py:66
  43.3 3.8 %collective-permute-done.14.refs_6_ = f32[256,128]{1,0:T(8,128)S(1)} collective-permute-done((f32[256,128]{1,0:T(8,128)S(1)}, f32[256,128]{1,0:T(8,128)S(1)}, u32[]{:S(2)}, u32[]{:S(2)}) %collective-permute-start.14) | collective-permute-done | bytes 131104 | tf_op jit(solution)/shard_map/ppermute | solution.py:66
  47.1 0.4 shard_map.48.refs_0_
  47.5 1.3 %collective-permute-done.15.refs_7_ = f32[512,128]{1,0:T(8,128)S(1)} collective-permute-done((f32[512,128]{1,0:T(8,128)S(1)}, f32[512,128]{1,0:T(8,128)S(1)}, u32[]{:S(2)}, u32[]{:S(2)}) %collective-permute-start.15) | collective-permute-done | bytes 262176 | tf_op jit(solution)/shard_map/ppermute | solution.py:66
  48.8 5.3 %collective-permute-done.16.refs_8_ = f32[512,128]{1,0:T(8,128)S(1)} collective-permute-done((f32[512,128]{1,0:T(8,128)S(1)}, f32[512,128]{1,0:T(8,128)S(1)}, u32[]{:S(2)}, u32[]{:S(2)}) %collective-permute-start.16) | collective-permute-done | bytes 262176 | tf_op jit(solution)/shard_map/ppermute | solution.py:66
  54.1 1.1 %shard_map.49 = f32[256,128]{1,0:T(8,128)} custom-call(f32[256,128]{1,0:T(8,128)S(1)} %shard_map.48.refs_0_, f32[704,256]{1,0:T(8,128)S(1)} %shard_map.40.refs_3_.refs_1_, f32[704,256]{1,0:T(8,128)S(1)} %collective-permute-done.3.refs_4_.refs_2_, f32[192,256]{1,0:T(8,128)S(1)} %shard_map.45.refs_5_.refs_3_, ...), custom_call_target="tpu_custom_call" | custom-call | tf_op jit(solution)/shard_map/pallas_call | solution.py:38
  (8 shorter events, 0.2 us)
Async XLA Ops:
  1.1 12.1 %collective-permute-start.1 = (f32[256,256]{1,0:T(8,128)S(1)}, f32[256,256]{1,0:T(8,128)S(1)}, u32[]{:S(2)}, u32[]{:S(2)}) collective-permute-start(f32[256,256]{1,0:T(8,128)S(1)} %get-tuple-element.18), channel_id=1, source_target_pairs={{0,4},{1,5},{2,6},{3,7},{4,0},{5,1},{6,2},{7,3},{8,12},{9,13},{10,... | collective-permute-start | bytes 786440 | tf_op jit(solution)/shard_map/ppermute | solution.py:66
  4.1 9.1 %collective-permute-start = (f32[256,256]{1,0:T(8,128)S(1)}, f32[256,256]{1,0:T(8,128)S(1)}, u32[]{:S(2)}, u32[]{:S(2)}) collective-permute-start(f32[256,256]{1,0:T(8,128)S(1)} %get-tuple-element.17.refs_0_), channel_id=1, source_target_pairs={{0,2},{1,3},{2,0},{3,1},{4,6},{5,7},{6,4},{7,5},{8,10},{9,11},{10,... | collective-permute-start | bytes 786440 | tf_op jit(solution)/shard_map/ppermute | solution.py:66
  5.7 7.6 %collective-permute-start.2 = (f32[128,256]{1,0:T(8,128)S(1)}, f32[128,256]{1,0:T(8,128)S(1)}, u32[]{:S(2)}, u32[]{:S(2)}) collective-permute-start(f32[128,256]{1,0:T(8,128)S(1)} %shard_map.38), channel_id=1, source_target_pairs={{0,4},{1,5},{2,6},{3,7},{4,0},{5,1},{6,2},{7,3},{8,12},{9,13},{10,... | collective-permute-start | bytes 393224 | tf_op jit(solution)/shard_map/ppermute | solution.py:66
  13.3 23.6 %collective-permute-start.3 = (f32[704,256]{1,0:T(8,128)S(1)}, f32[704,256]{1,0:T(8,128)S(1)}, u32[]{:S(2)}, u32[]{:S(2)}) collective-permute-start(f32[704,256]{1,0:T(8,128)S(1)} %shard_map.40.refs_3_.refs_1_), channel_id=1, source_target_pairs={{0,1},{1,0},{2,3},{3,2},{4,5},{5,4},{6,7},{7,6},{8,9},{9,8},{10,11... | collective-permute-start | bytes 2162696 | tf_op jit(solution)/shard_map/ppermute | solution.py:66
  13.4 6.3 %collective-permute-start.5 = (f32[64,256]{1,0:T(8,128)S(1)}, f32[64,256]{1,0:T(8,128)S(1)}, u32[]{:S(2)}, u32[]{:S(2)}) collective-permute-start(f32[64,256]{1,0:T(8,128)S(1)} %get-tuple-element.19), channel_id=1, source_target_pairs={{0,8},{1,12},{2,10},{3,14},{4,9},{5,13},{6,11},{7,15},{8,0},{9,4},... | collective-permute-start | bytes 196616 | tf_op jit(solution)/shard_map/ppermute | solution.py:66
  15.3 7.0 %collective-permute-start.6 = (f32[64,256]{1,0:T(8,128)S(1)}, f32[64,256]{1,0:T(8,128)S(1)}, u32[]{:S(2)}, u32[]{:S(2)}) collective-permute-start(f32[64,256]{1,0:T(8,128)S(1)} %get-tuple-element.20), channel_id=1, source_target_pairs={{0,16},{1,20},{2,18},{3,22},{4,17},{5,21},{6,19},{7,23},{8,24},{9,... | collective-permute-start | bytes 196616 | tf_op jit(solution)/shard_map/ppermute | solution.py:66
  17.9 6.2 %collective-permute-start.7 = (f32[64,256]{1,0:T(8,128)S(1)}, f32[64,256]{1,0:T(8,128)S(1)}, u32[]{:S(2)}, u32[]{:S(2)}) collective-permute-start(f32[64,256]{1,0:T(8,128)S(1)} %get-tuple-element.21), channel_id=1, source_target_pairs={{0,24},{1,28},{2,26},{3,30},{4,25},{5,29},{6,27},{7,31},{8,16},{9,... | collective-permute-start | bytes 196616 | tf_op jit(solution)/shard_map/ppermute | solution.py:66
  17.9 6.1 %collective-permute-start.8 = (f32[64,256]{1,0:T(8,128)S(1)}, f32[64,256]{1,0:T(8,128)S(1)}, u32[]{:S(2)}, u32[]{:S(2)}) collective-permute-start(f32[64,256]{1,0:T(8,128)S(1)} %shard_map.41.refs_3_), channel_id=1, source_target_pairs={{0,2},{1,3},{2,0},{3,1},{4,6},{5,7},{6,4},{7,5},{8,10},{9,11},{10,... | collective-permute-start | bytes 196616 | tf_op jit(solution)/shard_map/ppermute | solution.py:66
  24.1 3.0 %collective-permute-start.9 = (f32[320,256]{1,0:T(8,128)S(1)}, f32[320,256]{1,0:T(8,128)S(1)}, u32[]{:S(2)}, u32[]{:S(2)}) collective-permute-start(f32[320,256]{1,0:T(8,128)S(1)} %shard_map.42.refs_0_), channel_id=1, source_target_pairs={{0,1},{1,0},{2,3},{3,2},{4,5},{5,4},{6,7},{7,6},{8,9},{9,8},{10,11... | collective-permute-start | bytes 983048 | tf_op jit(solution)/shard_map/ppermute | solution.py:66
  25.5 6.9 %collective-permute-start.4 = (f32[192,256]{1,0:T(8,128)S(1)}, f32[192,256]{1,0:T(8,128)S(1)}, u32[]{:S(2)}, u32[]{:S(2)}) collective-permute-start(f32[192,256]{1,0:T(8,128)S(1)} %shard_map.39.refs_2_), channel_id=1, source_target_pairs={{0,2},{1,3},{2,0},{3,1},{4,6},{5,7},{6,4},{7,5},{8,10},{9,11},{10,... | collective-permute-start | bytes 589832 | tf_op jit(solution)/shard_map/ppermute | solution.py:66
  27.9 9.0 %collective-permute-start.13 = (f32[512,128]{1,0:T(8,128)S(1)}, f32[512,128]{1,0:T(8,128)S(1)}, u32[]{:S(2)}, u32[]{:S(2)}) collective-permute-start(f32[512,128]{1,0:T(8,128)S(1)} %get-tuple-element.23.refs_0_), channel_id=1, source_target_pairs={{0,8},{1,9},{2,10},{3,11},{4,12},{5,13},{6,14},{7,15},{8,0},{9,1},... | collective-permute-start | bytes 786440 | tf_op jit(solution)/shard_map/ppermute | solution.py:66
  32.4 2.4 %collective-permute-start.10 = (f32[192,256]{1,0:T(8,128)S(1)}, f32[192,256]{1,0:T(8,128)S(1)}, u32[]{:S(2)}, u32[]{:S(2)}) collective-permute-start(f32[192,256]{1,0:T(8,128)S(1)} %shard_map.45.refs_5_.refs_3_), channel_id=1, source_target_pairs={{0,1},{1,0},{2,3},{3,2},{4,5},{5,4},{6,7},{7,6},{8,9},{9,8},{10,11... | collective-permute-start | bytes 589832 | tf_op jit(solution)/shard_map/ppermute | solution.py:66
  32.5 7.5 %collective-permute-start.11 = (f32[256,128]{1,0:T(8,128)S(1)}, f32[256,128]{1,0:T(8,128)S(1)}, u32[]{:S(2)}, u32[]{:S(2)}) collective-permute-start(f32[256,128]{1,0:T(8,128)S(1)} %shard_map.44.refs_1_.refs_5_), channel_id=1, source_target_pairs={{0,24},{1,25},{2,26},{3,27},{4,28},{5,29},{6,30},{7,31},{8,0},{9,1... | collective-permute-start | bytes 393224 | tf_op jit(solution)/shard_map/ppermute | solution.py:66
  34.2 7.8 %collective-permute-start.12 = (f32[256,128]{1,0:T(8,128)S(1)}, f32[256,128]{1,0:T(8,128)S(1)}, u32[]{:S(2)}, u32[]{:S(2)}) collective-permute-start(f32[256,128]{1,0:T(8,128)S(1)} %shard_map.44.refs_1_.refs_5_), channel_id=1, source_target_pairs={{0,16},{1,17},{2,18},{3,19},{4,20},{5,21},{6,22},{7,23},{8,0},{9,1... | collective-permute-start | bytes 393224 | tf_op jit(solution)/shard_map/ppermute | solution.py:66
  38.4 10.4 %collective-permute-start.15 = (f32[512,128]{1,0:T(8,128)S(1)}, f32[512,128]{1,0:T(8,128)S(1)}, u32[]{:S(2)}, u32[]{:S(2)}) collective-permute-start(f32[512,128]{1,0:T(8,128)S(1)} %get-tuple-element.25.refs_2_), channel_id=1, source_target_pairs={{0,8},{1,9},{2,10},{3,11},{4,12},{5,13},{6,14},{7,15},{8,24},{9,25... | collective-permute-start | bytes 786440 | tf_op jit(solution)/shard_map/ppermute | solution.py:66
  38.6 15.5 %collective-permute-start.16 = (f32[512,128]{1,0:T(8,128)S(1)}, f32[512,128]{1,0:T(8,128)S(1)}, u32[]{:S(2)}, u32[]{:S(2)}) collective-permute-start(f32[512,128]{1,0:T(8,128)S(1)} %get-tuple-element.25.refs_2_), channel_id=1, source_target_pairs={{0,8},{1,9},{2,10},{3,11},{4,12},{5,13},{6,14},{7,15},{8,16},{9,17... | collective-permute-start | bytes 786440 | tf_op jit(solution)/shard_map/ppermute | solution.py:66
  42.0 5.0 %collective-permute-start.14 = (f32[256,128]{1,0:T(8,128)S(1)}, f32[256,128]{1,0:T(8,128)S(1)}, u32[]{:S(2)}, u32[]{:S(2)}) collective-permute-start(f32[256,128]{1,0:T(8,128)S(1)} %shard_map.47.refs_5_), channel_id=1, source_target_pairs={{0,4},{1,5},{2,6},{3,7},{4,0},{5,1},{6,2},{7,3},{8,12},{9,13},{10,... | collective-permute-start | bytes 393224 | tf_op jit(solution)/shard_map/ppermute | solution.py:66

commit v4 on v0

v4 whole, which is shorter than its diff:
```python
import functools

import jax
import jax.numpy as jnp
from jax import lax
from jax.experimental import pallas as pl
from jax.experimental.pallas import tpu as pltpu
from jax.sharding import PartitionSpec as P

AXES = ("row", "col")
VMEM = pl.BlockSpec(memory_space=pltpu.VMEM)
ANY = pl.BlockSpec(memory_space=pl.ANY)
FREE = pl.CostEstimate(flops=0, bytes_accessed=0, transcendentals=0)
LIMIT = 24 * 1024 * 1024


def split(value):
    high = value.astype(jnp.bfloat16)
    return high, (value - high.astype(jnp.float32)).astype(jnp.bfloat16)


def dot(left, right, over=(1, 0)):
    (a, b), (c, d) = split(left), split(right)

    def one(u, v):
        return lax.dot_general(u, v, (((over[0],), (over[1],)), ((), ())), preferred_element_type=jnp.float32)

    return one(a, c) + (one(a, d) + one(b, c))


def call(body, shapes, held, first=(), last=(), home=False, scratch=()):
    out = [jax.ShapeDtypeStruct(s, jnp.float32) if home else pltpu.VMEM(s, jnp.float32) for s in shapes]
    n_in, n_last = len(first) + len(held), len(last)

    def kernel(*refs):
        body(*refs[:n_in], *refs[n_in + n_last :])

    got = pl.pallas_call(
        kernel,
        out_shape=out,
        in_specs=[ANY] * len(first) + [VMEM] * len(held) + [ANY] * n_last,
        out_specs=[VMEM] * len(shapes),
        scratch_shapes=scratch,
        cost_estimate=FREE,
        compiler_params=pltpu.CompilerParams(vmem_limit_bytes=LIMIT),
    )(
        *[pltpu.with_memory_space_constraint(v, pltpu.HBM) for v in first],
        *[pltpu.with_memory_space_constraint(v, pltpu.VMEM) for v in held],
        *last,
    )
    return got[0] if len(shapes) == 1 else got


def solution(mesh):
    n_row, n_col = mesh.shape["row"], mesh.shape["col"]
    n_pair, n_half = n_row // 2, n_col // 2

    def place():
        row, col = lax.axis_index("row"), lax.axis_index("col")
        return row // 2, row % 2, col // 2, col % 2

    def hop(value, move):
        edges = []
        for q in range(n_pair):
            for x in range(2):
                for j in range(n_half):
                    for k in range(2):
                        a, b, c, d = move(q, x, j, k) or (q, x, j, 1 - k)
                        edges.append(((q * 2 + x) * n_col + j * 2 + k, (a * 2 + b) * n_col + c * 2 + d))
        return lax.ppermute(value, AXES, edges)

    def every(q):
        return True

    def along(value, which=every):
        return [
            hop(value, lambda q, x, j, k, s=s: (q, x, (j + s) % n_half, k) if which(q) else None)
            for s in range(1, n_half)
        ]

    def swap_rows(value, which=every):
        return hop(value, lambda q, x, j, k: (q, 1 - x, j, k) if which(q) else None)

    def swap_cores(value):
        return hop(value, lambda q, x, j, k: None)

    def climb(value, w, t):
        return hop(value, lambda q, x, j, k: ({w: t, t: w}[q], x, j, k) if q in (w, t) else None)

    def body(rhs, factor, inverses):
        rows, n_pan, part = factor.shape
        width = rhs.shape[1]
        shard, wide = inverses.shape[1:]
        n_win = n_pan // 2
        half, pair, whole = rows // 2, 2 * shard, n_pan * part
        units = (n_pan - 2) * part
        at_own = (n_pair - 1) * pair
        at_beside = at_own + n_half * whole

        def unfold(ref):
            return jnp.concatenate([ref[:half, :width], ref[:half, width:]])

        def ordered(ref):
            q, x, j, k = place()
            got = []
            for c in (k, 1 - k):
                for s in range(n_half):
                    start = pl.multiple_of((lax.rem(j - s + n_half, n_half) * 2 + c) * part, part)
                    got.append(ref[pl.ds(start, part), :])
            return jnp.concatenate(got)

        def turn(value):
            q, step = place()[0], 1
            while step < n_pair:
                run = step * pair
                pieces = [value[at : at + run] for at in range(0, n_pair * pair, run)]
                other = [pieces[i ^ 1] for i in range(len(pieces))]
                value = jnp.where((q // step) % 2 == 1, jnp.concatenate(other), value)
                step *= 2
            return value

        across = jnp.transpose(factor, (1, 2, 0)).reshape(-1, rows)

        def prepare(rhs, across, inverses, packed, near, own, here, mine, *refs):
            sent, panels, sems = refs[:-2], refs[-2], refs[-1]
            q = place()[0]
            copies = [
                pltpu.make_async_copy(a, b, sems.at[i])
                for i, (a, b) in enumerate(((rhs, here), (inverses, panels), (across, own)))
            ]
            for copy in copies:
                copy.start()
            copies[0].wait()
            packed[:half] = jnp.concatenate([here[:half], here[half:]], axis=1)
            copies[1].wait()

            def both(target):
                first = 2 * jnp.minimum(target, n_win - 1)
                return jnp.concatenate([panels[first], panels[first + 1]])

            for s, ref in enumerate(sent, 1):
                ref[...] = both(jnp.bitwise_xor(q, s))
            mine[...] = both(q)
            packed[half:] = mine[...]
            copies[2].wait()
            near[...] = own[:units]

        packed, near, own, rhs, mine, *sent = call(
            prepare,
            [(half + pair, wide), (units, rows), (whole, rows), (rows, width)] + [(pair, wide)] * n_pair,
            [],
            first=[rhs, across, inverses],
            scratch=[pltpu.VMEM((n_pan, shard, wide), jnp.float32), pltpu.SemaphoreType.DMA((3,))],
        )

        beside = swap_rows(packed, lambda q: q < n_win)
        near = swap_rows(near, lambda q: 0 < q < n_win)
        parts = [hop(sent[s - 1], lambda q, x, j, k, s=s: (q ^ s, k, j, x)) for s in range(1, n_pair)]
        own_along = along(own)

        def stack(*refs):
            at = 0
            for ref in refs[:-1]:
                refs[-1][at : at + ref.shape[0]] = ref[...]
                at += ref.shape[0]

        soon = call(stack, [(at_beside + units, wide)], [*parts, own, *own_along, near], last=[beside])
        soon = [soon, swap_cores(soon)]
        near_along = along(call(stack, [(units, rows)], [near], last=parts), lambda q: 0 < q < n_win)

        def columns(blocks, panel, count, row=0):
            got = []
            for p in range(panel, panel + count):
                for core in range(2):
                    for s in range(n_half):
                        ref, at = blocks[core], at_own + s * whole
                        if row:
                            at = at_beside
                            if s:
                                ref, at = blocks[2 + core], (s - 1) * units
                        got.append(ref[at + p * part : at + (p + 1) * part])
            return jnp.concatenate(got)

        def solve_first(soon, other, mine, beside, rhs, either, inverse, scratch):
            q, x, j, k = place()
            theirs = beside[half:]
            for m in range(2):
                at = m * shard
                got = [mine[at : at + shard], theirs[at : at + shard]]
                got = [jnp.where(x == 0, got[0], got[1]), jnp.where(x == 0, got[1], got[0])]
                for s in range(n_pair - 1):
                    a, b = (ref[s * pair + at : s * pair + at + shard] for ref in (soon, other))
                    got += [jnp.where(k == 0, a, b), jnp.where(k == 0, b, a)]
                inverse[m] = jnp.concatenate(got)
            first = turn(dot(inverse[0], jnp.where(x == 0, rhs[...], unfold(beside))))
            scratch[...] = first
            either[...] = first

            @pl.when(x == 1)
            def _():
                left = rhs[...] - dot(columns([soon, other], 0, 1), ordered(scratch), (0, 0))
                either[...] = turn(dot(inverse[1], left))

        panel = pltpu.VMEM((rows, width), jnp.float32)
        either, inverse = call(
            solve_first, [(rows, width), (2, wide, wide)], [*soon, mine, beside, rhs], scratch=[panel]
        )
        results = [either]

        def arrive(*refs):
            got = refs[0][...]
            for i, ref in enumerate(refs[1:-1], 1):
                got = jnp.where(place()[0] == n_pair - 1 - i, ref[...], got)
            refs[-1][...] = got

        early, blocks = [], None
        for w in range(n_win - 1):
            here = climb(either, w, w + 1)
            there = swap_rows(here, lambda q, w=w: q == w + 1)
            early.append([climb(either, w, t) for t in range(n_pair - 1, w + 1, -1)])
            late = call(stack, [((n_half - 1) * units, rows)], near_along, last=[here])
            blocks = [*soon, late, swap_cores(late)]

            def lean(inverse, beside, rhs, *refs):
                blocks, here, (fixed, slope, kept) = refs[:4], refs[4], refs[5:]
                x = place()[1]

                def solve(m, start, block, other):
                    fixed[...] = turn(dot(inverse[m], start))
                    slope[...] = turn(dot(inverse[m], block, (1, 1) if other else (1, 0)))

                mine = ordered(here)

                @pl.when(x == 0)
                def _():
                    start = rhs[...] - dot(columns(blocks, 0, 1), mine, (0, 0))
                    solve(0, start, columns(blocks, 1, 1), True)

                @pl.when(x == 1)
                def _():
                    start = unfold(beside) - dot(columns(blocks, 1, 1, 1), mine, (0, 0))
                    solve(0, start, columns(blocks, 0, 1, 1), True)
                    start = rhs[...] - dot(columns(blocks, 1, 1), mine, (0, 0))
                    step = columns(blocks, 2, 1)
                    start = start - dot(step, ordered(fixed), (0, 0))
                    kept[...] = slope[...]
                    block = columns(blocks, 0, 1).T - dot(step, ordered(kept), (0, 0))
                    solve(1, start, block, False)

            def solve_next(fixed, slope, there, either):
                either[...] = fixed[...] - dot(slope[...], ordered(there))

            fixed, slope = call(
                lean,
                [(rows, width), (rows, wide)],
                [inverse, beside, rhs, *blocks, here],
                scratch=[pltpu.VMEM((rows, wide), jnp.float32)],
            )
            either = call(solve_next, [(rows, width)], [fixed, slope, there])
            results.append(either)

        final = [climb(either, n_win - 1, t) for t in range(n_pair - 1, n_win - 1, -1)]
        left = rhs
        for i, values in enumerate([*early, final]):
            value = call(arrive, [(rows, width)], values, last=[either] if i < len(early) else [])
            traded = swap_rows(value, lambda q: q >= n_win)

            def update(start, *refs, other, at=2 * i):
                blocks, value, out = refs[:4], refs[4], refs[5]
                a, b = columns(blocks, at, 1), columns(blocks, at + 1, 1)
                block = jnp.where((place()[1] == 0) == other, b, a)
                out[...] = start[...] - dot(block, ordered(value), (0, 0))

            first = functools.partial(update, other=False)
            left = call(first, [(rows, width)], [left, *blocks, value])
            if i < len(early):
                left = call(functools.partial(update, other=True), [(rows, width)], [left, *blocks, traded])

        def finish(*refs):
            update(*refs[:6], refs[-1], other=True)
            for w in range(n_win):

                @pl.when(place()[0] == w)
                def _(w=w):
                    refs[-1][...] = refs[6 + w][...]

        return call(finish, [(rows, width)], [left, *blocks, traded, *results], home=True)

    placed = (P("row", "col"), P("row", None, "col"), P(None, "row", None))
    return jax.shard_map(body, mesh=mesh, in_specs=placed, out_specs=P("row", "col"), check_vma=False)
```

time: 351 us -> 43.4 us (0.12)
  waiting for transfers between devices: 300 us -> 19.2 us
  blocking collectives: 23.3 us -> 0 us
  starting transfers between devices: 0.17 us -> 18.1 us
  between operations: 13.2 us -> 0.14 us
  matrix products: 11.9 us -> 0 us
  Pallas kernels: 0 us -> 5.83 us
    psum x4 -> x0, waiting for transfers between devices: 258 us -> none  [spread(): return lax.psum(kept, axis)]
    all_gather x1 -> x0, waiting for transfers between devices: 40.9 us -> none  [body(): whole_inverse = lax.all_gather(inverses, 'row', axis=1, tiled=True)]
    all_gather x4 -> x0, blocking collectives: 23.3 us -> none  [body(): lax.all_gather(factor[:, section, :], 'col', axis=1, tiled=True)]
    ppermute x0 -> x17, waiting for transfers between devices: none -> 19.2 us  [hop(): return lax.ppermute(value, AXES, edges)]
    ppermute x0 -> x17, starting transfers between devices: none -> 18.1 us  [hop(): return lax.ppermute(value, AXES, edges)]
    dot_general x8 -> x0, matrix products: 11.9 us -> none  [the longest x4 6.73 us: add_columns(): jnp.dot(columns, solution, precision=lax.Precision.HIGHEST, preferred_ele...]
    pallas_call x0 -> x13, Pallas kernels: none -> 5.83 us  [call(): pl.pallas_call(kernel, out_shape=out, in_specs=[ANY] * len(first) + [VMEM...]
  transfers between devices with their start and end apart: 5 -> 17, of which waited for: 5 -> 8; matrix products, arithmetic and copies ran while one was open for 0% -> 0% of each run, Pallas kernels for 0% -> 8%
where the time goes in v4:
time: 43.4 us; the launch traced here: 43.3 us
  waiting for transfers between devices  19.2 us (44%)
  starting transfers between devices  18.1 us (42%)
  Pallas kernels  5.83 us (13%)
    ppermute x17, waiting for transfers between devices, hop(): return lax.ppermute(value, AXES, edges)  19.2 us
    ppermute x17, starting transfers between devices, hop(): return lax.ppermute(value, AXES, edges)  18.1 us
    pallas_call x13, Pallas kernels, call(): pl.pallas_call(kernel, out_shape=out, in_specs=[ANY] * len(first) + [VMEM...  5.83 us
  transfers between devices with their start and end apart: 17, of which 8 were waited for; matrix products, arithmetic and copies ran while one was open for 0% of the time, Pallas kernels for 8%

profile of v4, /device:TPU:18, one launch (start us, length us, event | category | flops | bytes accessed | tf_op | source)
XLA Modules:
  0.0 43.3 jit_solution(17846200149168905820)
XLA Ops:
  0.0 1.1 %shard_map.37 = (f32[192,256]{1,0:T(8,128)S(1)}, f32[128,256]{1,0:T(8,128)S(1)}, f32[256,256]{1,0:T(8,128)S(1)}, f32[256,128]{1,0:T(8,128)S(1)}, f32[64,256]{1,0...) custom-call(f32[256,128]{1,0:T(8,128)} %refs_0_.1, f32[256,256]{1,0:T(8,128)} %bitcast.3, ...), custom_call_target="tpu_custom_call" | custom-call | tf_op jit(solution)/shard_map/pallas_call | solution.py:38
  1.1 1.6 %collective-permute-start.3 = (f32[256,256]{1,0:T(8,128)S(1)}, f32[256,256]{1,0:T(8,128)S(1)}, u32[]{:S(2)}, u32[]{:S(2)}) collective-permute-start(f32[256,256]{1,0:T(8,128)S(1)} %get-tuple-element.21.refs_3_), channel_id=1, source_target_pairs={{0,2},{1,3},{2,0},{3,1},{4,6},{5,7},{6,4},{7,5},{8,10},{9,11},{10,... | collective-permute-start | bytes 786440 | tf_op jit(solution)/shard_map/ppermute | solution.py:70
  2.7 0.0 collective-permute-start.5
  2.7 1.7 %collective-permute-start = (f32[64,256]{1,0:T(8,128)S(1)}, f32[64,256]{1,0:T(8,128)S(1)}, u32[]{:S(2)}, u32[]{:S(2)}) collective-permute-start(f32[64,256]{1,0:T(8,128)S(1)} %get-tuple-element.18), channel_id=1, source_target_pairs={{0,8},{1,12},{2,10},{3,14},{4,9},{5,13},{6,11},{7,15},{8,0},{9,4},... | collective-permute-start | bytes 196616 | tf_op jit(solution)/shard_map/ppermute | solution.py:70
  4.4 0.1 collective-permute-start.4
  4.5 1.7 %collective-permute-start.1 = (f32[64,256]{1,0:T(8,128)S(1)}, f32[64,256]{1,0:T(8,128)S(1)}, u32[]{:S(2)}, u32[]{:S(2)}) collective-permute-start(f32[64,256]{1,0:T(8,128)S(1)} %get-tuple-element.19), channel_id=1, source_target_pairs={{0,16},{1,20},{2,18},{3,22},{4,17},{5,21},{6,19},{7,23},{8,24},{9,... | collective-permute-start | bytes 196616 | tf_op jit(solution)/shard_map/ppermute | solution.py:70
  6.2 1.5 %collective-permute-done.refs_0_.refs_1_ = f32[64,256]{1,0:T(8,128)S(1)} collective-permute-done((f32[64,256]{1,0:T(8,128)S(1)}, f32[64,256]{1,0:T(8,128)S(1)}, u32[]{:S(2)}, u32[]{:S(2)}) %collective-permute-start) | collective-permute-done | bytes 65568 | tf_op jit(solution)/shard_map/ppermute | solution.py:70
  7.7 0.5 %collective-permute-start.2 = (f32[64,256]{1,0:T(8,128)S(1)}, f32[64,256]{1,0:T(8,128)S(1)}, u32[]{:S(2)}, u32[]{:S(2)}) collective-permute-start(f32[64,256]{1,0:T(8,128)S(1)} %get-tuple-element.20), channel_id=1, source_target_pairs={{0,24},{1,28},{2,26},{3,30},{4,25},{5,29},{6,27},{7,31},{8,16},{9,... | collective-permute-start | bytes 196616 | tf_op jit(solution)/shard_map/ppermute | solution.py:70
  8.2 2.2 %collective-permute-done.1.refs_1_.refs_2_ = f32[64,256]{1,0:T(8,128)S(1)} collective-permute-done((f32[64,256]{1,0:T(8,128)S(1)}, f32[64,256]{1,0:T(8,128)S(1)}, u32[]{:S(2)}, u32[]{:S(2)}) %collective-permute-start.1) | collective-permute-done | bytes 65568 | tf_op jit(solution)/shard_map/ppermute | solution.py:70
  10.4 2.1 %collective-permute-done.2.refs_2_.refs_3_ = f32[64,256]{1,0:T(8,128)S(1)} collective-permute-done((f32[64,256]{1,0:T(8,128)S(1)}, f32[64,256]{1,0:T(8,128)S(1)}, u32[]{:S(2)}, u32[]{:S(2)}) %collective-permute-start.2) | collective-permute-done | bytes 65568 | tf_op jit(solution)/shard_map/ppermute | solution.py:70
  12.5 0.0 collective-permute-done.4.refs_5_.refs_0_
  12.5 0.0 collective-permute-done.5.refs_6_.refs_3_.refs_1_
  12.5 0.0 collective-permute-done.3.refs_4_
  12.5 0.1 shard_map.38.refs_0_.refs_3_.refs_1_
  12.6 0.1 collective-permute-start.6
  12.7 0.6 %collective-permute-start.7 = (f32[128,256]{1,0:T(8,128)S(1)}, f32[128,256]{1,0:T(8,128)S(1)}, u32[]{:S(2)}, u32[]{:S(2)}) collective-permute-start(f32[128,256]{1,0:T(8,128)S(1)} %shard_map.39), channel_id=1, source_target_pairs={{0,1},{1,0},{2,3},{3,2},{4,5},{5,4},{6,7},{7,6},{8,10},{9,11},{10,... | collective-permute-start | bytes 393224 | tf_op jit(solution)/shard_map/ppermute | solution.py:70
  13.2 1.8 %collective-permute-done.6.refs_1_.refs_4_.refs_2_ = f32[832,256]{1,0:T(8,128)S(1)} collective-permute-done((f32[832,256]{1,0:T(8,128)S(1)}, f32[832,256]{1,0:T(8,128)S(1)}, u32[]{:S(2)}, u32[]{:S(2)}) %collective-permute-start.6) | collective-permute-done | bytes 852000 | tf_op jit(solution)/shard_map/ppermute | solution.py:70
  15.0 0.9 %shard_map.40 = (f32[256,128]{1,0:T(8,128)S(1)}, f32[2,256,256]{2,1,0:T(8,128)S(1)}) custom-call(f32[832,256]{1,0:T(8,128)S(1)} %shard_map.38.refs_0_.refs_3_.refs_1_, f32[832,256]{1,0:T(8,128)S(1)} %collective-permute-done.6.refs_1_.refs_4_.refs_2_, f32[64,256]{1,0:T(8,128)S(1)} %get-tuple-element.24.refs_2_, ...), custom_call_target="tpu_custom_call" | custom-call | tf_op jit(solution)/shard_map/pallas_call | solution.py:38
  15.9 0.2 collective-permute-start.8
  16.1 0.0 collective-permute-done.7.refs_0_
  16.1 1.2 %collective-permute-done.8.refs_1_.refs_7_ = f32[256,128]{1,0:T(8,128)S(1)} collective-permute-done((f32[256,128]{1,0:T(8,128)S(1)}, f32[256,128]{1,0:T(8,128)S(1)}, u32[]{:S(2)}, u32[]{:S(2)}) %collective-permute-start.8) | collective-permute-done | bytes 131104 | tf_op jit(solution)/shard_map/ppermute | solution.py:70
  17.4 0.2 collective-permute-start.9
  17.6 0.4 collective-permute-start.12
  17.9 0.1 collective-permute-start.10
  18.1 6.8 %collective-permute-start.11 = (f32[256,128]{1,0:T(8,128)S(1)}, f32[256,128]{1,0:T(8,128)S(1)}, u32[]{:S(2)}, u32[]{:S(2)}) collective-permute-start(f32[256,128]{1,0:T(8,128)S(1)} %get-tuple-element.25.refs_6_), channel_id=1, source_target_pairs={{0,16},{1,17},{2,18},{3,19},{4,20},{5,21},{6,22},{7,23},{8,9},{9,8... | collective-permute-start | bytes 393224 | tf_op jit(solution)/shard_map/ppermute | solution.py:70
  24.9 0.0 collective-permute-done.9.refs_6_.refs_4_
  24.9 1.5 %shard_map.42 = (f32[256,128]{1,0:T(8,128)S(1)}, f32[256,256]{1,0:T(8,128)S(1)}) custom-call(f32[2,256,256]{2,1,0:T(8,128)S(1)} %get-tuple-element.26.refs_0_, f32[192,256]{1,0:T(8,128)S(1)} %collective-permute-done.5.refs_6_.refs_3_.refs_1_, f32[256,128]{1,0:T(8,128)S(1)} %get-tuple-element.17.refs_4_.refs_2_.refs_0_, ...), custom_call_target="tpu_custom_call" | custom-call | tf_op jit(solution)/shard_map/pallas_call | solution.py:38
  26.4 0.0 collective-permute-done.12.refs_2_
  26.4 0.3 shard_map.43.refs_2_.refs_7_
  26.7 0.1 collective-permute-start.14
  26.8 3.6 %collective-permute-start.15 = (f32[256,128]{1,0:T(8,128)S(1)}, f32[256,128]{1,0:T(8,128)S(1)}, u32[]{:S(2)}, u32[]{:S(2)}) collective-permute-start(f32[256,128]{1,0:T(8,128)S(1)} %shard_map.43.refs_2_.refs_7_), channel_id=1, source_target_pairs={{0,1},{1,0},{2,3},{3,2},{4,5},{5,4},{6,7},{7,6},{8,16},{9,17},{10,... | collective-permute-start | bytes 393224 | tf_op jit(solution)/shard_map/ppermute | solution.py:70
  30.4 0.0 collective-permute-done.10.refs_0_
  30.4 1.2 %collective-permute-done.11.refs_1_ = f32[256,128]{1,0:T(8,128)S(1)} collective-permute-done((f32[256,128]{1,0:T(8,128)S(1)}, f32[256,128]{1,0:T(8,128)S(1)}, u32[]{:S(2)}, u32[]{:S(2)}) %collective-permute-start.11) | collective-permute-done | bytes 131104 | tf_op jit(solution)/shard_map/ppermute | solution.py:70
  31.6 0.2 collective-permute-start.13
  31.8 0.0 collective-permute-done.14.refs_0_
  31.8 5.3 %collective-permute-done.15.refs_1_ = f32[256,128]{1,0:T(8,128)S(1)} collective-permute-done((f32[256,128]{1,0:T(8,128)S(1)}, f32[256,128]{1,0:T(8,128)S(1)}, u32[]{:S(2)}, u32[]{:S(2)}) %collective-permute-start.15) | collective-permute-done | bytes 131104 | tf_op jit(solution)/shard_map/ppermute | solution.py:70
  37.1 0.3 collective-permute-start.16
  37.4 0.3 shard_map.45.refs_0_
  37.7 0.0 collective-permute-done.13.refs_5_
  37.7 0.3 shard_map.46.refs_0_
  38.0 0.3 shard_map.48.refs_0_
  38.4 4.0 %collective-permute-done.16.refs_5_ = f32[256,128]{1,0:T(8,128)S(1)} collective-permute-done((f32[256,128]{1,0:T(8,128)S(1)}, f32[256,128]{1,0:T(8,128)S(1)}, u32[]{:S(2)}, u32[]{:S(2)}) %collective-permute-start.16) | collective-permute-done | bytes 131104 | tf_op jit(solution)/shard_map/ppermute | solution.py:70
  42.3 1.0 %shard_map.49 = f32[256,128]{1,0:T(8,128)} custom-call(f32[256,128]{1,0:T(8,128)S(1)} %shard_map.48.refs_0_, f32[832,256]{1,0:T(8,128)S(1)} %shard_map.38.refs_0_.refs_3_.refs_1_, f32[832,256]{1,0:T(8,128)S(1)} %collective-permute-done.6.refs_1_.refs_4_.refs_2_, f32[128,256]{1,0:T(8,128)S(1)} %shard_map.41.refs_5_.refs_3_, ...), custom_call_target="tpu_custom_call" | custom-call | tf_op jit(solution)/shard_map/pallas_call | solution.py:38
  (4 shorter events, 0.1 us)
Async XLA Ops:
  1.1 11.4 %collective-permute-start.3 = (f32[256,256]{1,0:T(8,128)S(1)}, f32[256,256]{1,0:T(8,128)S(1)}, u32[]{:S(2)}, u32[]{:S(2)}) collective-permute-start(f32[256,256]{1,0:T(8,128)S(1)} %get-tuple-element.21.refs_3_), channel_id=1, source_target_pairs={{0,2},{1,3},{2,0},{3,1},{4,6},{5,7},{6,4},{7,5},{8,10},{9,11},{10,... | collective-permute-start | bytes 786440 | tf_op jit(solution)/shard_map/ppermute | solution.py:70
  2.7 9.8 %collective-permute-start.5 = (f32[192,256]{1,0:T(8,128)S(1)}, f32[192,256]{1,0:T(8,128)S(1)}, u32[]{:S(2)}, u32[]{:S(2)}) collective-permute-start(f32[192,256]{1,0:T(8,128)S(1)} %get-tuple-element.23), channel_id=1, source_target_pairs={{0,4},{1,5},{2,6},{3,7},{4,0},{5,1},{6,2},{7,3},{8,12},{9,13},{10,... | collective-permute-start | bytes 589832 | tf_op jit(solution)/shard_map/ppermute | solution.py:70
  2.7 4.9 %collective-permute-start = (f32[64,256]{1,0:T(8,128)S(1)}, f32[64,256]{1,0:T(8,128)S(1)}, u32[]{:S(2)}, u32[]{:S(2)}) collective-permute-start(f32[64,256]{1,0:T(8,128)S(1)} %get-tuple-element.18), channel_id=1, source_target_pairs={{0,8},{1,12},{2,10},{3,14},{4,9},{5,13},{6,11},{7,15},{8,0},{9,4},... | collective-permute-start | bytes 196616 | tf_op jit(solution)/shard_map/ppermute | solution.py:70
  4.4 8.1 %collective-permute-start.4 = (f32[128,256]{1,0:T(8,128)S(1)}, f32[128,256]{1,0:T(8,128)S(1)}, u32[]{:S(2)}, u32[]{:S(2)}) collective-permute-start(f32[128,256]{1,0:T(8,128)S(1)} %get-tuple-element.22), channel_id=1, source_target_pairs={{0,1},{1,0},{2,3},{3,2},{4,5},{5,4},{6,7},{7,6},{8,12},{9,13},{10,... | collective-permute-start | bytes 393224 | tf_op jit(solution)/shard_map/ppermute | solution.py:70
  4.5 5.9 %collective-permute-start.1 = (f32[64,256]{1,0:T(8,128)S(1)}, f32[64,256]{1,0:T(8,128)S(1)}, u32[]{:S(2)}, u32[]{:S(2)}) collective-permute-start(f32[64,256]{1,0:T(8,128)S(1)} %get-tuple-element.19), channel_id=1, source_target_pairs={{0,16},{1,20},{2,18},{3,22},{4,17},{5,21},{6,19},{7,23},{8,24},{9,... | collective-permute-start | bytes 196616 | tf_op jit(solution)/shard_map/ppermute | solution.py:70
  7.7 4.9 %collective-permute-start.2 = (f32[64,256]{1,0:T(8,128)S(1)}, f32[64,256]{1,0:T(8,128)S(1)}, u32[]{:S(2)}, u32[]{:S(2)}) collective-permute-start(f32[64,256]{1,0:T(8,128)S(1)} %get-tuple-element.20), channel_id=1, source_target_pairs={{0,24},{1,28},{2,26},{3,30},{4,25},{5,29},{6,27},{7,31},{8,16},{9,... | collective-permute-start | bytes 196616 | tf_op jit(solution)/shard_map/ppermute | solution.py:70
  12.6 2.4 %collective-permute-start.6 = (f32[832,256]{1,0:T(8,128)S(1)}, f32[832,256]{1,0:T(8,128)S(1)}, u32[]{:S(2)}, u32[]{:S(2)}) collective-permute-start(f32[832,256]{1,0:T(8,128)S(1)} %shard_map.38.refs_0_.refs_3_.refs_1_), channel_id=1, source_target_pairs={{0,1},{1,0},{2,3},{3,2},{4,5},{5,4},{6,7},{7,6},{8,9},{9,8},{10,11... | collective-permute-start | bytes 2555912 | tf_op jit(solution)/shard_map/ppermute | solution.py:70
  12.7 3.5 %collective-permute-start.7 = (f32[128,256]{1,0:T(8,128)S(1)}, f32[128,256]{1,0:T(8,128)S(1)}, u32[]{:S(2)}, u32[]{:S(2)}) collective-permute-start(f32[128,256]{1,0:T(8,128)S(1)} %shard_map.39), channel_id=1, source_target_pairs={{0,1},{1,0},{2,3},{3,2},{4,5},{5,4},{6,7},{7,6},{8,10},{9,11},{10,... | collective-permute-start | bytes 393224 | tf_op jit(solution)/shard_map/ppermute | solution.py:70
  15.9 1.4 %collective-permute-start.8 = (f32[256,128]{1,0:T(8,128)S(1)}, f32[256,128]{1,0:T(8,128)S(1)}, u32[]{:S(2)}, u32[]{:S(2)}) collective-permute-start(f32[256,128]{1,0:T(8,128)S(1)} %get-tuple-element.25.refs_6_), channel_id=1, source_target_pairs={{0,8},{1,9},{2,10},{3,11},{4,12},{5,13},{6,14},{7,15},{8,0},{9,1},... | collective-permute-start | bytes 393224 | tf_op jit(solution)/shard_map/ppermute | solution.py:70
  17.4 7.6 %collective-permute-start.9 = (f32[128,256]{1,0:T(8,128)S(1)}, f32[128,256]{1,0:T(8,128)S(1)}, u32[]{:S(2)}, u32[]{:S(2)}) collective-permute-start(f32[128,256]{1,0:T(8,128)S(1)} %shard_map.41.refs_5_.refs_3_), channel_id=1, source_target_pairs={{0,1},{1,0},{2,3},{3,2},{4,5},{5,4},{6,7},{7,6},{8,9},{9,8},{10,11... | collective-permute-start | bytes 393224 | tf_op jit(solution)/shard_map/ppermute | solution.py:70
  17.6 8.9 %collective-permute-start.12 = (f32[256,128]{1,0:T(8,128)S(1)}, f32[256,128]{1,0:T(8,128)S(1)}, u32[]{:S(2)}, u32[]{:S(2)}) collective-permute-start(f32[256,128]{1,0:T(8,128)S(1)} %collective-permute-done.8.refs_1_.refs_7_), channel_id=1, source_target_pairs={{0,1},{1,0},{2,3},{3,2},{4,5},{5,4},{6,7},{7,6},{8,12},{9,13},{10,... | collective-permute-start | bytes 393224 | tf_op jit(solution)/shard_map/ppermute | solution.py:70
  17.9 12.4 %collective-permute-start.10 = (f32[256,128]{1,0:T(8,128)S(1)}, f32[256,128]{1,0:T(8,128)S(1)}, u32[]{:S(2)}, u32[]{:S(2)}) collective-permute-start(f32[256,128]{1,0:T(8,128)S(1)} %get-tuple-element.25.refs_6_), channel_id=1, source_target_pairs={{0,24},{1,25},{2,26},{3,27},{4,28},{5,29},{6,30},{7,31},{8,9},{9,8... | collective-permute-start | bytes 393224 | tf_op jit(solution)/shard_map/ppermute | solution.py:70
  18.1 13.4 %collective-permute-start.11 = (f32[256,128]{1,0:T(8,128)S(1)}, f32[256,128]{1,0:T(8,128)S(1)}, u32[]{:S(2)}, u32[]{:S(2)}) collective-permute-start(f32[256,128]{1,0:T(8,128)S(1)} %get-tuple-element.25.refs_6_), channel_id=1, source_target_pairs={{0,16},{1,17},{2,18},{3,19},{4,20},{5,21},{6,22},{7,23},{8,9},{9,8... | collective-permute-start | bytes 393224 | tf_op jit(solution)/shard_map/ppermute | solution.py:70
  26.7 5.1 %collective-permute-start.14 = (f32[256,128]{1,0:T(8,128)S(1)}, f32[256,128]{1,0:T(8,128)S(1)}, u32[]{:S(2)}, u32[]{:S(2)}) collective-permute-start(f32[256,128]{1,0:T(8,128)S(1)} %shard_map.43.refs_2_.refs_7_), channel_id=1, source_target_pairs={{0,1},{1,0},{2,3},{3,2},{4,5},{5,4},{6,7},{7,6},{8,24},{9,25},{10,... | collective-permute-start | bytes 393224 | tf_op jit(solution)/shard_map/ppermute | solution.py:70
  26.8 10.3 %collective-permute-start.15 = (f32[256,128]{1,0:T(8,128)S(1)}, f32[256,128]{1,0:T(8,128)S(1)}, u32[]{:S(2)}, u32[]{:S(2)}) collective-permute-start(f32[256,128]{1,0:T(8,128)S(1)} %shard_map.43.refs_2_.refs_7_), channel_id=1, source_target_pairs={{0,1},{1,0},{2,3},{3,2},{4,5},{5,4},{6,7},{7,6},{8,16},{9,17},{10,... | collective-permute-start | bytes 393224 | tf_op jit(solution)/shard_map/ppermute | solution.py:70
  31.6 6.1 %collective-permute-start.13 = (f32[256,128]{1,0:T(8,128)S(1)}, f32[256,128]{1,0:T(8,128)S(1)}, u32[]{:S(2)}, u32[]{:S(2)}) collective-permute-start(f32[256,128]{1,0:T(8,128)S(1)} %shard_map.44.refs_5_), channel_id=1, source_target_pairs={{0,1},{1,0},{2,3},{3,2},{4,5},{5,4},{6,7},{7,6},{8,9},{9,8},{10,11... | collective-permute-start | bytes 393224 | tf_op jit(solution)/shard_map/ppermute | solution.py:70
  37.1 5.2 %collective-permute-start.16 = (f32[256,128]{1,0:T(8,128)S(1)}, f32[256,128]{1,0:T(8,128)S(1)}, u32[]{:S(2)}, u32[]{:S(2)}) collective-permute-start(f32[256,128]{1,0:T(8,128)S(1)} %shard_map.47.refs_5_), channel_id=1, source_target_pairs={{0,1},{1,0},{2,3},{3,2},{4,5},{5,4},{6,7},{7,6},{8,9},{9,8},{10,11... | collective-permute-start | bytes 393224 | tf_op jit(solution)/shard_map/ppermute | solution.py:70

commit v5 on v4

--- a/solution.py
+++ b/solution.py
@@ -121,7 +121,7 @@
 
         across = jnp.transpose(factor, (1, 2, 0)).reshape(-1, rows)
 
-        def prepare(rhs, across, inverses, packed, near, own, here, mine, *refs):
+        def prepare(rhs, across, inverses, packed, own, here, mine, *refs):
             sent, panels, sems = refs[:-2], refs[-2], refs[-1]
             q = place()[0]
             copies = [
@@ -141,20 +141,19 @@
             for s, ref in enumerate(sent, 1):
                 ref[...] = both(jnp.bitwise_xor(q, s))
             mine[...] = both(q)
-            packed[half:] = mine[...]
+            packed[half : half + pair] = mine[...]
             copies[2].wait()
-            near[...] = own[:units]
-
-        packed, near, own, rhs, mine, *sent = call(
+            packed[half + pair :] = own[:units]
+
+        packed, own, rhs, mine, *sent = call(
             prepare,
-            [(half + pair, wide), (units, rows), (whole, rows), (rows, width)] + [(pair, wide)] * n_pair,
+            [(half + pair + units, wide), (whole, rows), (rows, width)] + [(pair, wide)] * n_pair,
             [],
             first=[rhs, across, inverses],
             scratch=[pltpu.VMEM((n_pan, shard, wide), jnp.float32), pltpu.SemaphoreType.DMA((3,))],
         )
 
         beside = swap_rows(packed, lambda q: q < n_win)
-        near = swap_rows(near, lambda q: 0 < q < n_win)
         parts = [hop(sent[s - 1], lambda q, x, j, k, s=s: (q ^ s, k, j, x)) for s in range(1, n_pair)]
         own_along = along(own)
 
@@ -164,9 +163,16 @@
                 refs[-1][at : at + ref.shape[0]] = ref[...]
                 at += ref.shape[0]
 
-        soon = call(stack, [(at_beside + units, wide)], [*parts, own, *own_along, near], last=[beside])
+        def mix(beside, *refs):
+            stack(*refs)
+            refs[-1][at_beside:] = beside[half + pair :]
+
+        def cut(beside, near):
+            near[...] = beside[half + pair :]
+
+        soon = call(mix, [(at_beside + units, wide)], [beside, *parts, own, *own_along])
         soon = [soon, swap_cores(soon)]
-        near_along = along(call(stack, [(units, rows)], [near], last=parts), lambda q: 0 < q < n_win)
+        near_along = along(call(cut, [(units, rows)], [beside], last=parts), lambda q: 0 < q < n_win)
 
         def columns(blocks, panel, count, row=0):
             got = []
@@ -183,7 +189,7 @@
 
         def solve_first(soon, other, mine, beside, rhs, either, inverse, scratch):
             q, x, j, k = place()
-            theirs = beside[half:]
+            theirs = beside[half : half + pair]
             for m in range(2):
                 at = m * shard
                 got = [mine[at : at + shard], theirs[at : at + shard]]
@@ -259,7 +265,7 @@
             either = call(solve_next, [(rows, width)], [fixed, slope, there])
             results.append(either)
 
-        final = [climb(either, n_win - 1, t) for t in range(n_pair - 1, n_win - 1, -1)]
+        final = [climb(either, n_win - 1, t) for t in range(n_win, n_pair)][::-1]
         left = rhs
         for i, values in enumerate([*early, final]):
             value = call(arrive, [(rows, width)], values, last=[either] if i < len(early) else [])

time: 43.4 us -> 42.3 us (0.975)
  starting transfers between devices: 18.1 us -> 16 us
  waiting for transfers between devices: 19.2 us -> 20.2 us
    ppermute x17 -> x16, starting transfers between devices: 18.1 us -> 16 us  [hop(): return lax.ppermute(value, AXES, edges)]
    ppermute x17 -> x16, waiting for transfers between devices: 19.2 us -> 20.2 us  [hop(): return lax.ppermute(value, AXES, edges)]
  transfers between devices with their start and end apart: 17 -> 16, of which waited for: 8 -> 8; matrix products, arithmetic and copies ran while one was open for 0% -> 0% of each run, Pallas kernels for 8% -> 9%
where the time goes in v5:
time: 42.3 us; the launch traced here: 42.1 us
  waiting for transfers between devices  20.2 us (48%)
  starting transfers between devices  16 us (38%)
  Pallas kernels  5.82 us (14%)
    ppermute x16, waiting for transfers between devices, hop(): return lax.ppermute(value, AXES, edges)  20.2 us
    ppermute x16, starting transfers between devices, hop(): return lax.ppermute(value, AXES, edges)  16 us
    pallas_call x13, Pallas kernels, call(): pl.pallas_call(kernel, out_shape=out, in_specs=[ANY] * len(first) + [VMEM...  5.82 us
  transfers between devices with their start and end apart: 16, of which 8 were waited for; matrix products, arithmetic and copies ran while one was open for 0% of the time, Pallas kernels for 9%

profile of v5, /device:TPU:18, one launch (start us, length us, event | category | flops | bytes accessed | tf_op | source)
XLA Modules:
  0.0 42.1 jit_solution(2875546076487087385)
XLA Ops:
  0.0 1.1 %shard_map.37 = (f32[320,256]{1,0:T(8,128)S(1)}, f32[256,256]{1,0:T(8,128)S(1)}, f32[256,128]{1,0:T(8,128)S(1)}, f32[64,256]{1,0:T(8,128)S(1)}, f32[64,256]{1,0:...) custom-call(f32[256,128]{1,0:T(8,128)} %refs_0_.1, f32[256,256]{1,0:T(8,128)} %bitcast.3, f32[4,32,256]{2,1,0:T(8,128)} %refs_2_.1), custom_call_target="tpu_custom_call" | custom-call | tf_op jit(solution)/shard_map/pallas_call | solution.py:38
  1.1 0.1 collective-permute-start
  1.2 1.6 %collective-permute-start.4 = (f32[256,256]{1,0:T(8,128)S(1)}, f32[256,256]{1,0:T(8,128)S(1)}, u32[]{:S(2)}, u32[]{:S(2)}) collective-permute-start(f32[256,256]{1,0:T(8,128)S(1)} %get-tuple-element.21.refs_4_), channel_id=1, source_target_pairs={{0,2},{1,3},{2,0},{3,1},{4,6},{5,7},{6,4},{7,5},{8,10},{9,11},{10,... | collective-permute-start | bytes 786440 | tf_op jit(solution)/shard_map/ppermute | solution.py:70
  2.8 1.3 %collective-permute-start.1 = (f32[64,256]{1,0:T(8,128)S(1)}, f32[64,256]{1,0:T(8,128)S(1)}, u32[]{:S(2)}, u32[]{:S(2)}) collective-permute-start(f32[64,256]{1,0:T(8,128)S(1)} %get-tuple-element.18), channel_id=1, source_target_pairs={{0,8},{1,12},{2,10},{3,14},{4,9},{5,13},{6,11},{7,15},{8,0},{9,4},... | collective-permute-start | bytes 196616 | tf_op jit(solution)/shard_map/ppermute | solution.py:70
  4.1 1.7 %collective-permute-start.2 = (f32[64,256]{1,0:T(8,128)S(1)}, f32[64,256]{1,0:T(8,128)S(1)}, u32[]{:S(2)}, u32[]{:S(2)}) collective-permute-start(f32[64,256]{1,0:T(8,128)S(1)} %get-tuple-element.19), channel_id=1, source_target_pairs={{0,16},{1,20},{2,18},{3,22},{4,17},{5,21},{6,19},{7,23},{8,24},{9,... | collective-permute-start | bytes 196616 | tf_op jit(solution)/shard_map/ppermute | solution.py:70
  5.8 0.9 %collective-permute-start.3 = (f32[64,256]{1,0:T(8,128)S(1)}, f32[64,256]{1,0:T(8,128)S(1)}, u32[]{:S(2)}, u32[]{:S(2)}) collective-permute-start(f32[64,256]{1,0:T(8,128)S(1)} %get-tuple-element.20), channel_id=1, source_target_pairs={{0,24},{1,28},{2,26},{3,30},{4,25},{5,29},{6,27},{7,31},{8,16},{9,... | collective-permute-start | bytes 196616 | tf_op jit(solution)/shard_map/ppermute | solution.py:70
  6.6 1.1 %collective-permute-done.1.refs_1_ = f32[64,256]{1,0:T(8,128)S(1)} collective-permute-done((f32[64,256]{1,0:T(8,128)S(1)}, f32[64,256]{1,0:T(8,128)S(1)}, u32[]{:S(2)}, u32[]{:S(2)}) %collective-permute-start.1) | collective-permute-done | bytes 65568 | tf_op jit(solution)/shard_map/ppermute | solution.py:70
  7.7 2.6 %collective-permute-done.2.refs_2_ = f32[64,256]{1,0:T(8,128)S(1)} collective-permute-done((f32[64,256]{1,0:T(8,128)S(1)}, f32[64,256]{1,0:T(8,128)S(1)}, u32[]{:S(2)}, u32[]{:S(2)}) %collective-permute-start.2) | collective-permute-done | bytes 65568 | tf_op jit(solution)/shard_map/ppermute | solution.py:70
  10.3 3.1 %collective-permute-done.3.refs_3_ = f32[64,256]{1,0:T(8,128)S(1)} collective-permute-done((f32[64,256]{1,0:T(8,128)S(1)}, f32[64,256]{1,0:T(8,128)S(1)}, u32[]{:S(2)}, u32[]{:S(2)}) %collective-permute-start.3) | collective-permute-done | bytes 65568 | tf_op jit(solution)/shard_map/ppermute | solution.py:70
  13.4 0.0 collective-permute-done.4.refs_5_
  13.4 0.0 collective-permute-done.refs_0_.refs_3_.refs_1_
  13.4 0.1 shard_map.38.refs_0_.refs_3_.refs_1_
  13.5 0.1 collective-permute-start.5
  13.6 0.6 %collective-permute-start.6 = (f32[128,256]{1,0:T(8,128)S(1)}, f32[128,256]{1,0:T(8,128)S(1)}, u32[]{:S(2)}, u32[]{:S(2)}) collective-permute-start(f32[128,256]{1,0:T(8,128)S(1)} %shard_map.39), channel_id=1, source_target_pairs={{0,1},{1,0},{2,3},{3,2},{4,5},{5,4},{6,7},{7,6},{8,10},{9,11},{10,... | collective-permute-start | bytes 393224 | tf_op jit(solution)/shard_map/ppermute | solution.py:70
  14.1 1.8 %collective-permute-done.5.refs_1_.refs_4_.refs_2_ = f32[832,256]{1,0:T(8,128)S(1)} collective-permute-done((f32[832,256]{1,0:T(8,128)S(1)}, f32[832,256]{1,0:T(8,128)S(1)}, u32[]{:S(2)}, u32[]{:S(2)}) %collective-permute-start.5) | collective-permute-done | bytes 852000 | tf_op jit(solution)/shard_map/ppermute | solution.py:70
  15.9 0.9 %shard_map.40 = (f32[256,128]{1,0:T(8,128)S(1)}, f32[2,256,256]{2,1,0:T(8,128)S(1)}) custom-call(f32[832,256]{1,0:T(8,128)S(1)} %shard_map.38.refs_0_.refs_3_.refs_1_, f32[832,256]{1,0:T(8,128)S(1)} %collective-permute-done.5.refs_1_.refs_4_.refs_2_, f32[64,256]{1,0:T(8,128)S(1)} %get-tuple-element.22.refs_2_, ...), custom_call_target="tpu_custom_call" | custom-call | tf_op jit(solution)/shard_map/pallas_call | solution.py:38
  16.8 0.2 collective-permute-start.7
  17.0 0.0 collective-permute-done.6.refs_0_
  17.0 1.2 %collective-permute-done.7.refs_1_.refs_7_ = f32[256,128]{1,0:T(8,128)S(1)} collective-permute-done((f32[256,128]{1,0:T(8,128)S(1)}, f32[256,128]{1,0:T(8,128)S(1)}, u32[]{:S(2)}, u32[]{:S(2)}) %collective-permute-start.7) | collective-permute-done | bytes 131104 | tf_op jit(solution)/shard_map/ppermute | solution.py:70
  18.2 0.2 collective-permute-start.8
  18.5 0.4 collective-permute-start.11
  18.8 5.1 %collective-permute-start.10 = (f32[256,128]{1,0:T(8,128)S(1)}, f32[256,128]{1,0:T(8,128)S(1)}, u32[]{:S(2)}, u32[]{:S(2)}) collective-permute-start(f32[256,128]{1,0:T(8,128)S(1)} %get-tuple-element.23.refs_6_), channel_id=1, source_target_pairs={{0,16},{1,17},{2,18},{3,19},{4,20},{5,21},{6,22},{7,23},{8,9},{9,8... | collective-permute-start | bytes 393224 | tf_op jit(solution)/shard_map/ppermute | solution.py:70
  23.9 0.0 collective-permute-start.9
  23.9 0.0 collective-permute-done.8.refs_6_.refs_4_
  23.9 1.5 %shard_map.42 = (f32[256,128]{1,0:T(8,128)S(1)}, f32[256,256]{1,0:T(8,128)S(1)}) custom-call(f32[2,256,256]{2,1,0:T(8,128)S(1)} %get-tuple-element.24.refs_0_, f32[320,256]{1,0:T(8,128)S(1)} %collective-permute-done.refs_0_.refs_3_.refs_1_, f32[256,128]{1,0:T(8,128)S(1)} %get-tuple-element.16.refs_4_.refs_2_.refs_0_, ...), custom_call_target="tpu_custom_call" | custom-call | tf_op jit(solution)/shard_map/pallas_call | solution.py:38
  25.4 0.0 collective-permute-done.11.refs_2_
  25.4 0.3 shard_map.43.refs_2_.refs_7_
  25.7 0.6 %collective-permute-start.13 = (f32[256,128]{1,0:T(8,128)S(1)}, f32[256,128]{1,0:T(8,128)S(1)}, u32[]{:S(2)}, u32[]{:S(2)}) collective-permute-start(f32[256,128]{1,0:T(8,128)S(1)} %shard_map.43.refs_2_.refs_7_), channel_id=1, source_target_pairs={{0,1},{1,0},{2,3},{3,2},{4,5},{5,4},{6,7},{7,6},{8,24},{9,25},{10,... | collective-permute-start | bytes 393224 | tf_op jit(solution)/shard_map/ppermute | solution.py:70
  26.3 3.2 %collective-permute-start.14 = (f32[256,128]{1,0:T(8,128)S(1)}, f32[256,128]{1,0:T(8,128)S(1)}, u32[]{:S(2)}, u32[]{:S(2)}) collective-permute-start(f32[256,128]{1,0:T(8,128)S(1)} %shard_map.43.refs_2_.refs_7_), channel_id=1, source_target_pairs={{0,1},{1,0},{2,3},{3,2},{4,5},{5,4},{6,7},{7,6},{8,16},{9,17},{10,... | collective-permute-start | bytes 393224 | tf_op jit(solution)/shard_map/ppermute | solution.py:70
  29.5 0.6 %collective-permute-done.10.refs_1_ = f32[256,128]{1,0:T(8,128)S(1)} collective-permute-done((f32[256,128]{1,0:T(8,128)S(1)}, f32[256,128]{1,0:T(8,128)S(1)}, u32[]{:S(2)}, u32[]{:S(2)}) %collective-permute-start.10) | collective-permute-done | bytes 131104 | tf_op jit(solution)/shard_map/ppermute | solution.py:70
  30.1 0.0 collective-permute-done.9.refs_0_
  30.1 0.1 collective-permute-start.12
  30.2 0.0 collective-permute-done.13.refs_0_
  30.2 5.9 %collective-permute-done.14.refs_1_ = f32[256,128]{1,0:T(8,128)S(1)} collective-permute-done((f32[256,128]{1,0:T(8,128)S(1)}, f32[256,128]{1,0:T(8,128)S(1)}, u32[]{:S(2)}, u32[]{:S(2)}) %collective-permute-start.14) | collective-permute-done | bytes 131104 | tf_op jit(solution)/shard_map/ppermute | solution.py:70
  36.1 0.1 collective-permute-start.15
  36.2 0.3 shard_map.45.refs_0_
  36.6 0.0 collective-permute-done.12.refs_5_
  36.6 0.3 shard_map.46.refs_0_
  36.9 0.3 shard_map.48.refs_0_
  37.2 3.9 %collective-permute-done.15.refs_5_ = f32[256,128]{1,0:T(8,128)S(1)} collective-permute-done((f32[256,128]{1,0:T(8,128)S(1)}, f32[256,128]{1,0:T(8,128)S(1)}, u32[]{:S(2)}, u32[]{:S(2)}) %collective-permute-start.15) | collective-permute-done | bytes 131104 | tf_op jit(solution)/shard_map/ppermute | solution.py:70
  41.2 1.0 %shard_map.49 = f32[256,128]{1,0:T(8,128)} custom-call(f32[256,128]{1,0:T(8,128)S(1)} %shard_map.48.refs_0_, f32[832,256]{1,0:T(8,128)S(1)} %shard_map.38.refs_0_.refs_3_.refs_1_, f32[832,256]{1,0:T(8,128)S(1)} %collective-permute-done.5.refs_1_.refs_4_.refs_2_, f32[128,256]{1,0:T(8,128)S(1)} %shard_map.41.refs_5_.refs_3_, ...), custom_call_target="tpu_custom_call" | custom-call | tf_op jit(solution)/shard_map/pallas_call | solution.py:38
  (4 shorter events, 0.1 us)
Async XLA Ops:
  1.1 12.3 %collective-permute-start = (f32[320,256]{1,0:T(8,128)S(1)}, f32[320,256]{1,0:T(8,128)S(1)}, u32[]{:S(2)}, u32[]{:S(2)}) collective-permute-start(f32[320,256]{1,0:T(8,128)S(1)} %get-tuple-element.17), channel_id=1, source_target_pairs={{0,4},{1,5},{2,6},{3,7},{4,0},{5,1},{6,2},{7,3},{8,12},{9,13},{10,... | collective-permute-start | bytes 983048 | tf_op jit(solution)/shard_map/ppermute | solution.py:70
  1.2 12.2 %collective-permute-start.4 = (f32[256,256]{1,0:T(8,128)S(1)}, f32[256,256]{1,0:T(8,128)S(1)}, u32[]{:S(2)}, u32[]{:S(2)}) collective-permute-start(f32[256,256]{1,0:T(8,128)S(1)} %get-tuple-element.21.refs_4_), channel_id=1, source_target_pairs={{0,2},{1,3},{2,0},{3,1},{4,6},{5,7},{6,4},{7,5},{8,10},{9,11},{10,... | collective-permute-start | bytes 786440 | tf_op jit(solution)/shard_map/ppermute | solution.py:70
  2.8 4.9 %collective-permute-start.1 = (f32[64,256]{1,0:T(8,128)S(1)}, f32[64,256]{1,0:T(8,128)S(1)}, u32[]{:S(2)}, u32[]{:S(2)}) collective-permute-start(f32[64,256]{1,0:T(8,128)S(1)} %get-tuple-element.18), channel_id=1, source_target_pairs={{0,8},{1,12},{2,10},{3,14},{4,9},{5,13},{6,11},{7,15},{8,0},{9,4},... | collective-permute-start | bytes 196616 | tf_op jit(solution)/shard_map/ppermute | solution.py:70
  4.1 6.2 %collective-permute-start.2 = (f32[64,256]{1,0:T(8,128)S(1)}, f32[64,256]{1,0:T(8,128)S(1)}, u32[]{:S(2)}, u32[]{:S(2)}) collective-permute-start(f32[64,256]{1,0:T(8,128)S(1)} %get-tuple-element.19), channel_id=1, source_target_pairs={{0,16},{1,20},{2,18},{3,22},{4,17},{5,21},{6,19},{7,23},{8,24},{9,... | collective-permute-start | bytes 196616 | tf_op jit(solution)/shard_map/ppermute | solution.py:70
  5.8 7.6 %collective-permute-start.3 = (f32[64,256]{1,0:T(8,128)S(1)}, f32[64,256]{1,0:T(8,128)S(1)}, u32[]{:S(2)}, u32[]{:S(2)}) collective-permute-start(f32[64,256]{1,0:T(8,128)S(1)} %get-tuple-element.20), channel_id=1, source_target_pairs={{0,24},{1,28},{2,26},{3,30},{4,25},{5,29},{6,27},{7,31},{8,16},{9,... | collective-permute-start | bytes 196616 | tf_op jit(solution)/shard_map/ppermute | solution.py:70
  13.5 2.4 %collective-permute-start.5 = (f32[832,256]{1,0:T(8,128)S(1)}, f32[832,256]{1,0:T(8,128)S(1)}, u32[]{:S(2)}, u32[]{:S(2)}) collective-permute-start(f32[832,256]{1,0:T(8,128)S(1)} %shard_map.38.refs_0_.refs_3_.refs_1_), channel_id=1, source_target_pairs={{0,1},{1,0},{2,3},{3,2},{4,5},{5,4},{6,7},{7,6},{8,9},{9,8},{10,11... | collective-permute-start | bytes 2555912 | tf_op jit(solution)/shard_map/ppermute | solution.py:70
  13.6 3.5 %collective-permute-start.6 = (f32[128,256]{1,0:T(8,128)S(1)}, f32[128,256]{1,0:T(8,128)S(1)}, u32[]{:S(2)}, u32[]{:S(2)}) collective-permute-start(f32[128,256]{1,0:T(8,128)S(1)} %shard_map.39), channel_id=1, source_target_pairs={{0,1},{1,0},{2,3},{3,2},{4,5},{5,4},{6,7},{7,6},{8,10},{9,11},{10,... | collective-permute-start | bytes 393224 | tf_op jit(solution)/shard_map/ppermute | solution.py:70
  16.8 1.4 %collective-permute-start.7 = (f32[256,128]{1,0:T(8,128)S(1)}, f32[256,128]{1,0:T(8,128)S(1)}, u32[]{:S(2)}, u32[]{:S(2)}) collective-permute-start(f32[256,128]{1,0:T(8,128)S(1)} %get-tuple-element.23.refs_6_), channel_id=1, source_target_pairs={{0,8},{1,9},{2,10},{3,11},{4,12},{5,13},{6,14},{7,15},{8,0},{9,1},... | collective-permute-start | bytes 393224 | tf_op jit(solution)/shard_map/ppermute | solution.py:70
  18.2 5.7 %collective-permute-start.8 = (f32[128,256]{1,0:T(8,128)S(1)}, f32[128,256]{1,0:T(8,128)S(1)}, u32[]{:S(2)}, u32[]{:S(2)}) collective-permute-start(f32[128,256]{1,0:T(8,128)S(1)} %shard_map.41.refs_5_.refs_3_), channel_id=1, source_target_pairs={{0,1},{1,0},{2,3},{3,2},{4,5},{5,4},{6,7},{7,6},{8,9},{9,8},{10,11... | collective-permute-start | bytes 393224 | tf_op jit(solution)/shard_map/ppermute | solution.py:70
  18.5 7.0 %collective-permute-start.11 = (f32[256,128]{1,0:T(8,128)S(1)}, f32[256,128]{1,0:T(8,128)S(1)}, u32[]{:S(2)}, u32[]{:S(2)}) collective-permute-start(f32[256,128]{1,0:T(8,128)S(1)} %collective-permute-done.7.refs_1_.refs_7_), channel_id=1, source_target_pairs={{0,1},{1,0},{2,3},{3,2},{4,5},{5,4},{6,7},{7,6},{8,12},{9,13},{10,... | collective-permute-start | bytes 393224 | tf_op jit(solution)/shard_map/ppermute | solution.py:70
  18.8 11.3 %collective-permute-start.10 = (f32[256,128]{1,0:T(8,128)S(1)}, f32[256,128]{1,0:T(8,128)S(1)}, u32[]{:S(2)}, u32[]{:S(2)}) collective-permute-start(f32[256,128]{1,0:T(8,128)S(1)} %get-tuple-element.23.refs_6_), channel_id=1, source_target_pairs={{0,16},{1,17},{2,18},{3,19},{4,20},{5,21},{6,22},{7,23},{8,9},{9,8... | collective-permute-start | bytes 393224 | tf_op jit(solution)/shard_map/ppermute | solution.py:70
  23.9 6.2 %collective-permute-start.9 = (f32[256,128]{1,0:T(8,128)S(1)}, f32[256,128]{1,0:T(8,128)S(1)}, u32[]{:S(2)}, u32[]{:S(2)}) collective-permute-start(f32[256,128]{1,0:T(8,128)S(1)} %get-tuple-element.23.refs_6_), channel_id=1, source_target_pairs={{0,24},{1,25},{2,26},{3,27},{4,28},{5,29},{6,30},{7,31},{8,9},{9,8... | collective-permute-start | bytes 393224 | tf_op jit(solution)/shard_map/ppermute | solution.py:70
  25.7 4.5 %collective-permute-start.13 = (f32[256,128]{1,0:T(8,128)S(1)}, f32[256,128]{1,0:T(8,128)S(1)}, u32[]{:S(2)}, u32[]{:S(2)}) collective-permute-start(f32[256,128]{1,0:T(8,128)S(1)} %shard_map.43.refs_2_.refs_7_), channel_id=1, source_target_pairs={{0,1},{1,0},{2,3},{3,2},{4,5},{5,4},{6,7},{7,6},{8,24},{9,25},{10,... | collective-permute-start | bytes 393224 | tf_op jit(solution)/shard_map/ppermute | solution.py:70
  26.3 9.8 %collective-permute-start.14 = (f32[256,128]{1,0:T(8,128)S(1)}, f32[256,128]{1,0:T(8,128)S(1)}, u32[]{:S(2)}, u32[]{:S(2)}) collective-permute-start(f32[256,128]{1,0:T(8,128)S(1)} %shard_map.43.refs_2_.refs_7_), channel_id=1, source_target_pairs={{0,1},{1,0},{2,3},{3,2},{4,5},{5,4},{6,7},{7,6},{8,16},{9,17},{10,... | collective-permute-start | bytes 393224 | tf_op jit(solution)/shard_map/ppermute | solution.py:70
  30.1 6.4 %collective-permute-start.12 = (f32[256,128]{1,0:T(8,128)S(1)}, f32[256,128]{1,0:T(8,128)S(1)}, u32[]{:S(2)}, u32[]{:S(2)}) collective-permute-start(f32[256,128]{1,0:T(8,128)S(1)} %shard_map.44.refs_5_), channel_id=1, source_target_pairs={{0,1},{1,0},{2,3},{3,2},{4,5},{5,4},{6,7},{7,6},{8,9},{9,8},{10,11... | collective-permute-start | bytes 393224 | tf_op jit(solution)/shard_map/ppermute | solution.py:70
  36.1 5.1 %collective-permute-start.15 = (f32[256,128]{1,0:T(8,128)S(1)}, f32[256,128]{1,0:T(8,128)S(1)}, u32[]{:S(2)}, u32[]{:S(2)}) collective-permute-start(f32[256,128]{1,0:T(8,128)S(1)} %shard_map.47.refs_5_), channel_id=1, source_target_pairs={{0,1},{1,0},{2,3},{3,2},{4,5},{5,4},{6,7},{7,6},{8,9},{9,8},{10,11... | collective-permute-start | bytes 393224 | tf_op jit(solution)/shard_map/ppermute | solution.py:70

commit v6 on v5

--- a/solution.py
+++ b/solution.py
@@ -95,7 +95,7 @@
         half, pair, whole = rows // 2, 2 * shard, n_pan * part
         units = (n_pan - 2) * part
         at_own = (n_pair - 1) * pair
-        at_beside = at_own + n_half * whole
+        far = whole - part
 
         def unfold(ref):
             return jnp.concatenate([ref[:half, :width], ref[:half, width:]])
@@ -157,37 +157,44 @@
         parts = [hop(sent[s - 1], lambda q, x, j, k, s=s: (q ^ s, k, j, x)) for s in range(1, n_pair)]
         own_along = along(own)
 
-        def stack(*refs):
-            at = 0
-            for ref in refs[:-1]:
-                refs[-1][at : at + ref.shape[0]] = ref[...]
-                at += ref.shape[0]
-
-        def mix(beside, *refs):
-            stack(*refs)
-            refs[-1][at_beside:] = beside[half + pair :]
+        def mix(*refs):
+            parts, own, packed = refs[: n_pair - 1], refs[n_pair - 1 : -1], refs[-1]
+            for s, ref in enumerate(parts):
+                packed[s * pair : (s + 1) * pair] = ref[...]
+            for s, ref in enumerate(own):
+                packed[at_own + s * part : at_own + (s + 1) * part] = ref[:part]
+
+        soon = call(mix, [(at_own + n_half * part, wide)], [*parts, own, *own_along], last=[beside])
+        soon = [soon, swap_cores(soon)]
 
         def cut(beside, near):
             near[...] = beside[half + pair :]
 
-        soon = call(mix, [(at_beside + units, wide)], [beside, *parts, own, *own_along])
-        soon = [soon, swap_cores(soon)]
-        near_along = along(call(cut, [(units, rows)], [beside], last=parts), lambda q: 0 < q < n_win)
+        near = call(cut, [(units, rows)], [beside], last=parts)
+        near = [near, *along(near, lambda q: 0 < q < n_win)]
+
+        def rest(*refs):
+            own, near, packed = refs[:n_half], refs[n_half:-1], refs[-1]
+            for s, ref in enumerate(own):
+                packed[s * far : (s + 1) * far] = ref[part:]
+            for s, ref in enumerate(near):
+                packed[n_half * far + s * units : n_half * far + (s + 1) * units] = ref[...]
 
         def columns(blocks, panel, count, row=0):
             got = []
             for p in range(panel, panel + count):
                 for core in range(2):
                     for s in range(n_half):
-                        ref, at = blocks[core], at_own + s * whole
                         if row:
-                            at = at_beside
-                            if s:
-                                ref, at = blocks[2 + core], (s - 1) * units
-                        got.append(ref[at + p * part : at + (p + 1) * part])
+                            ref, at = blocks[2 + core], n_half * far + s * units + p * part
+                        elif p:
+                            ref, at = blocks[2 + core], s * far + (p - 1) * part
+                        else:
+                            ref, at = blocks[core], at_own + s * part
+                        got.append(ref[at : at + part])
             return jnp.concatenate(got)
 
-        def solve_first(soon, other, mine, beside, rhs, either, inverse, scratch):
+        def assemble(soon, other, mine, beside, inverse):
             q, x, j, k = place()
             theirs = beside[half : half + pair]
             for m in range(2):
@@ -198,38 +205,45 @@
                     a, b = (ref[s * pair + at : s * pair + at + shard] for ref in (soon, other))
                     got += [jnp.where(k == 0, a, b), jnp.where(k == 0, b, a)]
                 inverse[m] = jnp.concatenate(got)
-            first = turn(dot(inverse[0], jnp.where(x == 0, rhs[...], unfold(beside))))
-            scratch[...] = first
-            either[...] = first
-
-            @pl.when(x == 1)
+
+        def solve_first(soon, other, mine, beside, rhs, either, inverse, scratch):
+            x = place()[1]
+
+            @pl.when(place()[0] == 0)
             def _():
-                left = rhs[...] - dot(columns([soon, other], 0, 1), ordered(scratch), (0, 0))
-                either[...] = turn(dot(inverse[1], left))
+                assemble(soon, other, mine, beside, inverse)
+                first = turn(dot(inverse[0], jnp.where(x == 0, rhs[...], unfold(beside))))
+                scratch[...] = first
+                either[...] = first
+
+                @pl.when(x == 1)
+                def _():
+                    left = rhs[...] - dot(columns([soon, other], 0, 1), ordered(scratch), (0, 0))
+                    either[...] = turn(dot(inverse[1], left))
 
         panel = pltpu.VMEM((rows, width), jnp.float32)
-        either, inverse = call(
-            solve_first, [(rows, width), (2, wide, wide)], [*soon, mine, beside, rhs], scratch=[panel]
-        )
+        inverse = pltpu.VMEM((2, wide, wide), jnp.float32)
+        either = call(solve_first, [(rows, width)], [*soon, mine, beside, rhs], scratch=[inverse, panel])
         results = [either]
 
-        def arrive(*refs):
+        def arrive(*refs, pairs):
             got = refs[0][...]
-            for i, ref in enumerate(refs[1:-1], 1):
-                got = jnp.where(place()[0] == n_pair - 1 - i, ref[...], got)
+            for t, ref in zip(pairs[1:], refs[1:-1], strict=True):
+                got = jnp.where(place()[0] == t, ref[...], got)
             refs[-1][...] = got
 
         early, blocks = [], None
         for w in range(n_win - 1):
             here = climb(either, w, w + 1)
             there = swap_rows(here, lambda q, w=w: q == w + 1)
-            early.append([climb(either, w, t) for t in range(n_pair - 1, w + 1, -1)])
-            late = call(stack, [((n_half - 1) * units, rows)], near_along, last=[here])
+            early.append([climb(here, w + 1, t) for t in range(n_pair - 1, w + 1, -1)])
+            late = call(rest, [(n_half * (far + units), rows)], [own, *own_along, *near], last=[here])
             blocks = [*soon, late, swap_cores(late)]
 
-            def lean(inverse, beside, rhs, *refs):
-                blocks, here, (fixed, slope, kept) = refs[:4], refs[4], refs[5:]
+            def lean(mine, beside, rhs, *refs):
+                blocks, here, (fixed, slope, kept, inverse) = refs[:4], refs[4], refs[5:]
                 x = place()[1]
+                assemble(*blocks[:2], mine, beside, inverse)
 
                 def solve(m, start, block, other):
                     fixed[...] = turn(dot(inverse[m], start))
@@ -259,16 +273,18 @@
             fixed, slope = call(
                 lean,
                 [(rows, width), (rows, wide)],
-                [inverse, beside, rhs, *blocks, here],
-                scratch=[pltpu.VMEM((rows, wide), jnp.float32)],
+                [mine, beside, rhs, *blocks, here],
+                scratch=[pltpu.VMEM((rows, wide), jnp.float32), inverse],
             )
             either = call(solve_next, [(rows, width)], [fixed, slope, there])
             results.append(either)
 
-        final = [climb(either, n_win - 1, t) for t in range(n_win, n_pair)][::-1]
+        final = [climb(either, n_win - 1, t) for t in range(n_win, n_pair)]
         left = rhs
         for i, values in enumerate([*early, final]):
-            value = call(arrive, [(rows, width)], values, last=[either] if i < len(early) else [])
+            pairs = range(n_win, n_pair) if i == len(early) else range(n_pair - 1, i + 1, -1)
+            which = functools.partial(arrive, pairs=pairs)
+            value = call(which, [(rows, width)], values, last=[either] if i < len(early) else [])
             traded = swap_rows(value, lambda q: q >= n_win)
 
             def update(start, *refs, other, at=2 * i):

time: 42.3 us -> 41.4 us (0.979); the launches traced: 42.1 us -> 40.7 us
  waiting for transfers between devices: 20.2 us -> 17.7 us
  starting transfers between devices: 16 us -> 17.9 us
  Pallas kernels: 5.82 us -> 4.98 us
    ppermute x16, waiting for transfers between devices: 20.2 us -> 17.7 us  [hop(): return lax.ppermute(value, AXES, edges)]
    ppermute x16, starting transfers between devices: 16 us -> 17.9 us  [hop(): return lax.ppermute(value, AXES, edges)]
    pallas_call x13, Pallas kernels: 5.82 us -> 4.98 us  [call(): pl.pallas_call(kernel, out_shape=out, in_specs=[ANY] * len(first) + [VMEM...]
  transfers between devices with their start and end apart: 16 -> 16, of which waited for: 8 -> 9; matrix products, arithmetic and copies ran while one was open for 0% -> 0% of each run, Pallas kernels for 9% -> 7%
where the time goes in v6:
time: 41.4 us; the launch traced here: 40.7 us
  starting transfers between devices  17.9 us (43%)
  waiting for transfers between devices  17.7 us (43%)
  Pallas kernels  4.98 us (12%)
    ppermute x16, starting transfers between devices, hop(): return lax.ppermute(value, AXES, edges)  17.9 us
    ppermute x16, waiting for transfers between devices, hop(): return lax.ppermute(value, AXES, edges)  17.7 us
    pallas_call x13, Pallas kernels, call(): pl.pallas_call(kernel, out_shape=out, in_specs=[ANY] * len(first) + [VMEM...  4.98 us
  transfers between devices with their start and end apart: 16, of which 9 were waited for; matrix products, arithmetic and copies ran while one was open for 0% of the time, Pallas kernels for 7%

profile of v6, /device:TPU:18, one launch (start us, length us, event | category | flops | bytes accessed | tf_op | source)
XLA Modules:
  0.0 40.7 jit_solution(4031932505633724173)
XLA Ops:
  0.0 1.1 %shard_map.37 = (f32[320,256]{1,0:T(8,128)S(1)}, f32[256,256]{1,0:T(8,128)S(1)}, f32[256,128]{1,0:T(8,128)S(1)}, f32[64,256]{1,0:T(8,128)S(1)}, f32[64,256]{1,0:...) custom-call(f32[256,128]{1,0:T(8,128)} %refs_0_.1, f32[256,256]{1,0:T(8,128)} %bitcast.3, f32[4,32,256]{2,1,0:T(8,128)} %refs_2_.1), custom_call_target="tpu_custom_call" | custom-call | tf_op jit(solution)/shard_map/pallas_call | solution.py:38
  1.1 0.1 collective-permute-start.4
  1.2 1.6 %collective-permute-start.3 = (f32[256,256]{1,0:T(8,128)S(1)}, f32[256,256]{1,0:T(8,128)S(1)}, u32[]{:S(2)}, u32[]{:S(2)}) collective-permute-start(f32[256,256]{1,0:T(8,128)S(1)} %get-tuple-element.18.refs_3_.refs_0_), channel_id=1, source_target_pairs={{0,2},{1,3},{2,0},{3,1},{4,6},{5,7},{6,4},{7,5},{8,10},{9,11},{10,... | collective-permute-start | bytes 786440 | tf_op jit(solution)/shard_map/ppermute | solution.py:70
  2.8 1.3 %collective-permute-start = (f32[64,256]{1,0:T(8,128)S(1)}, f32[64,256]{1,0:T(8,128)S(1)}, u32[]{:S(2)}, u32[]{:S(2)}) collective-permute-start(f32[64,256]{1,0:T(8,128)S(1)} %get-tuple-element.15), channel_id=1, source_target_pairs={{0,8},{1,12},{2,10},{3,14},{4,9},{5,13},{6,11},{7,15},{8,0},{9,4},... | collective-permute-start | bytes 196616 | tf_op jit(solution)/shard_map/ppermute | solution.py:70
  4.1 1.7 %collective-permute-start.1 = (f32[64,256]{1,0:T(8,128)S(1)}, f32[64,256]{1,0:T(8,128)S(1)}, u32[]{:S(2)}, u32[]{:S(2)}) collective-permute-start(f32[64,256]{1,0:T(8,128)S(1)} %get-tuple-element.16), channel_id=1, source_target_pairs={{0,16},{1,20},{2,18},{3,22},{4,17},{5,21},{6,19},{7,23},{8,24},{9,... | collective-permute-start | bytes 196616 | tf_op jit(solution)/shard_map/ppermute | solution.py:70
  5.8 0.9 %collective-permute-start.2 = (f32[64,256]{1,0:T(8,128)S(1)}, f32[64,256]{1,0:T(8,128)S(1)}, u32[]{:S(2)}, u32[]{:S(2)}) collective-permute-start(f32[64,256]{1,0:T(8,128)S(1)} %get-tuple-element.17), channel_id=1, source_target_pairs={{0,24},{1,28},{2,26},{3,30},{4,25},{5,29},{6,27},{7,31},{8,16},{9,... | collective-permute-start | bytes 196616 | tf_op jit(solution)/shard_map/ppermute | solution.py:70
  6.6 1.1 %collective-permute-done.refs_0_.refs_1_ = f32[64,256]{1,0:T(8,128)S(1)} collective-permute-done((f32[64,256]{1,0:T(8,128)S(1)}, f32[64,256]{1,0:T(8,128)S(1)}, u32[]{:S(2)}, u32[]{:S(2)}) %collective-permute-start) | collective-permute-done | bytes 65568 | tf_op jit(solution)/shard_map/ppermute | solution.py:70
  7.7 2.6 %collective-permute-done.1.refs_1_.refs_2_ = f32[64,256]{1,0:T(8,128)S(1)} collective-permute-done((f32[64,256]{1,0:T(8,128)S(1)}, f32[64,256]{1,0:T(8,128)S(1)}, u32[]{:S(2)}, u32[]{:S(2)}) %collective-permute-start.1) | collective-permute-done | bytes 65568 | tf_op jit(solution)/shard_map/ppermute | solution.py:70
  10.3 3.1 %collective-permute-done.2.refs_2_.refs_3_ = f32[64,256]{1,0:T(8,128)S(1)} collective-permute-done((f32[64,256]{1,0:T(8,128)S(1)}, f32[64,256]{1,0:T(8,128)S(1)}, u32[]{:S(2)}, u32[]{:S(2)}) %collective-permute-start.2) | collective-permute-done | bytes 65568 | tf_op jit(solution)/shard_map/ppermute | solution.py:70
  13.4 0.0 collective-permute-done.3.refs_4_.refs_1_
  13.4 0.0 collective-permute-done.4.refs_5_.refs_0_.refs_3_.refs_1_
  13.4 0.1 collective-permute-start.5
  13.5 0.6 %collective-permute-start.6 = (f32[128,256]{1,0:T(8,128)S(1)}, f32[128,256]{1,0:T(8,128)S(1)}, u32[]{:S(2)}, u32[]{:S(2)}) collective-permute-start(f32[128,256]{1,0:T(8,128)S(1)} %shard_map.39.refs_2_), channel_id=1, source_target_pairs={{0,1},{1,0},{2,3},{3,2},{4,5},{5,4},{6,7},{7,6},{8,10},{9,11},{10,... | collective-permute-start | bytes 393224 | tf_op jit(solution)/shard_map/ppermute | solution.py:70
  14.1 1.0 %collective-permute-done.5.refs_1_.refs_4_.refs_2_ = f32[320,256]{1,0:T(8,128)S(1)} collective-permute-done((f32[320,256]{1,0:T(8,128)S(1)}, f32[320,256]{1,0:T(8,128)S(1)}, u32[]{:S(2)}, u32[]{:S(2)}) %collective-permute-start.5) | collective-permute-done | bytes 327712 | tf_op jit(solution)/shard_map/ppermute | solution.py:70
  15.1 0.1 collective-permute-start.7
  15.3 0.0 collective-permute-done.6.refs_3_
  15.3 1.2 %collective-permute-done.7.refs_4_.refs_7_ = f32[256,128]{1,0:T(8,128)S(1)} collective-permute-done((f32[256,128]{1,0:T(8,128)S(1)}, f32[256,128]{1,0:T(8,128)S(1)}, u32[]{:S(2)}, u32[]{:S(2)}) %collective-permute-start.7) | collective-permute-done | bytes 131104 | tf_op jit(solution)/shard_map/ppermute | solution.py:70
  16.5 0.2 collective-permute-start.8
  16.7 0.4 collective-permute-start.11
  17.1 5.4 %collective-permute-start.10 = (f32[256,128]{1,0:T(8,128)S(1)}, f32[256,128]{1,0:T(8,128)S(1)}, u32[]{:S(2)}, u32[]{:S(2)}) collective-permute-start(f32[256,128]{1,0:T(8,128)S(1)} %collective-permute-done.7.refs_4_.refs_7_), channel_id=1, source_target_pairs={{0,1},{1,0},{2,3},{3,2},{4,5},{5,4},{6,7},{7,6},{8,16},{9,17},{10,... | collective-permute-start | bytes 393224 | tf_op jit(solution)/shard_map/ppermute | solution.py:70
  22.5 0.0 collective-permute-start.9
  22.5 0.0 collective-permute-done.8.refs_6_.refs_4_
  22.5 1.5 %shard_map.42 = (f32[256,128]{1,0:T(8,128)S(1)}, f32[256,256]{1,0:T(8,128)S(1)}) custom-call(f32[64,256]{1,0:T(8,128)S(1)} %get-tuple-element.20.refs_2_.refs_0_, f32[320,256]{1,0:T(8,128)S(1)} %collective-permute-done.4.refs_5_.refs_0_.refs_3_.refs_1_, f32[256,128]{1,0:T(8,128)S(1)} %get-tuple-element.14.refs_4_.refs_2_.refs_0_, ...), custom_call_target="tpu_custom_call" | custom-call | tf_op jit(solution)/shard_map/pallas_call | solution.py:38
  24.1 0.0 collective-permute-done.11.refs_2_
  24.1 0.3 shard_map.43.refs_2_.refs_7_
  24.3 3.4 %collective-permute-start.13 = (f32[256,128]{1,0:T(8,128)S(1)}, f32[256,128]{1,0:T(8,128)S(1)}, u32[]{:S(2)}, u32[]{:S(2)}) collective-permute-start(f32[256,128]{1,0:T(8,128)S(1)} %shard_map.43.refs_2_.refs_7_), channel_id=1, source_target_pairs={{0,1},{1,0},{2,3},{3,2},{4,5},{5,4},{6,7},{7,6},{8,16},{9,17},{10,... | collective-permute-start | bytes 393224 | tf_op jit(solution)/shard_map/ppermute | solution.py:70
  27.7 0.0 collective-permute-start.14
  27.7 4.1 %collective-permute-done.10.refs_1_ = f32[256,128]{1,0:T(8,128)S(1)} collective-permute-done((f32[256,128]{1,0:T(8,128)S(1)}, f32[256,128]{1,0:T(8,128)S(1)}, u32[]{:S(2)}, u32[]{:S(2)}) %collective-permute-start.10) | collective-permute-done | bytes 131104 | tf_op jit(solution)/shard_map/ppermute | solution.py:70
  31.8 0.0 collective-permute-done.9.refs_0_
  31.9 1.1 %collective-permute-start.12 = (f32[256,128]{1,0:T(8,128)S(1)}, f32[256,128]{1,0:T(8,128)S(1)}, u32[]{:S(2)}, u32[]{:S(2)}) collective-permute-start(f32[256,128]{1,0:T(8,128)S(1)} %shard_map.44.refs_5_), channel_id=1, source_target_pairs={{0,1},{1,0},{2,3},{3,2},{4,5},{5,4},{6,7},{7,6},{8,9},{9,8},{10,11... | collective-permute-start | bytes 393224 | tf_op jit(solution)/shard_map/ppermute | solution.py:70
  33.0 1.0 %collective-permute-done.13.refs_0_ = f32[256,128]{1,0:T(8,128)S(1)} collective-permute-done((f32[256,128]{1,0:T(8,128)S(1)}, f32[256,128]{1,0:T(8,128)S(1)}, u32[]{:S(2)}, u32[]{:S(2)}) %collective-permute-start.13) | collective-permute-done | bytes 131104 | tf_op jit(solution)/shard_map/ppermute | solution.py:70
  34.0 0.0 collective-permute-done.14.refs_1_
  34.0 1.1 %collective-permute-start.15 = (f32[256,128]{1,0:T(8,128)S(1)}, f32[256,128]{1,0:T(8,128)S(1)}, u32[]{:S(2)}, u32[]{:S(2)}) collective-permute-start(f32[256,128]{1,0:T(8,128)S(1)} %shard_map.47.refs_5_), channel_id=1, source_target_pairs={{0,1},{1,0},{2,3},{3,2},{4,5},{5,4},{6,7},{7,6},{8,9},{9,8},{10,11... | collective-permute-start | bytes 393224 | tf_op jit(solution)/shard_map/ppermute | solution.py:70
  35.2 0.3 shard_map.45.refs_0_
  35.5 2.3 %collective-permute-done.12.refs_5_ = f32[256,128]{1,0:T(8,128)S(1)} collective-permute-done((f32[256,128]{1,0:T(8,128)S(1)}, f32[256,128]{1,0:T(8,128)S(1)}, u32[]{:S(2)}, u32[]{:S(2)}) %collective-permute-start.12) | collective-permute-done | bytes 131104 | tf_op jit(solution)/shard_map/ppermute | solution.py:70
  37.8 0.3 shard_map.46.refs_0_
  38.1 0.3 shard_map.48.refs_0_
  38.5 1.2 %collective-permute-done.15.refs_5_ = f32[256,128]{1,0:T(8,128)S(1)} collective-permute-done((f32[256,128]{1,0:T(8,128)S(1)}, f32[256,128]{1,0:T(8,128)S(1)}, u32[]{:S(2)}, u32[]{:S(2)}) %collective-permute-start.15) | collective-permute-done | bytes 131104 | tf_op jit(solution)/shard_map/ppermute | solution.py:70
  39.7 1.0 %shard_map.49 = f32[256,128]{1,0:T(8,128)} custom-call(f32[256,128]{1,0:T(8,128)S(1)} %shard_map.48.refs_0_, f32[320,256]{1,0:T(8,128)S(1)} %shard_map.38.refs_0_.refs_3_.refs_1_, f32[320,256]{1,0:T(8,128)S(1)} %collective-permute-done.5.refs_1_.refs_4_.refs_2_, f32[640,256]{1,0:T(8,128)S(1)} %shard_map.41.refs_5_.refs_3_, ...), custom_call_target="tpu_custom_call" | custom-call | tf_op jit(solution)/shard_map/pallas_call | solution.py:38
  (6 shorter events, 0.1 us)
Async XLA Ops:
  1.1 12.3 %collective-permute-start.4 = (f32[320,256]{1,0:T(8,128)S(1)}, f32[320,256]{1,0:T(8,128)S(1)}, u32[]{:S(2)}, u32[]{:S(2)}) collective-permute-start(f32[320,256]{1,0:T(8,128)S(1)} %get-tuple-element.19), channel_id=1, source_target_pairs={{0,4},{1,5},{2,6},{3,7},{4,0},{5,1},{6,2},{7,3},{8,12},{9,13},{10,... | collective-permute-start | bytes 983048 | tf_op jit(solution)/shard_map/ppermute | solution.py:70
  1.2 12.2 %collective-permute-start.3 = (f32[256,256]{1,0:T(8,128)S(1)}, f32[256,256]{1,0:T(8,128)S(1)}, u32[]{:S(2)}, u32[]{:S(2)}) collective-permute-start(f32[256,256]{1,0:T(8,128)S(1)} %get-tuple-element.18.refs_3_.refs_0_), channel_id=1, source_target_pairs={{0,2},{1,3},{2,0},{3,1},{4,6},{5,7},{6,4},{7,5},{8,10},{9,11},{10,... | collective-permute-start | bytes 786440 | tf_op jit(solution)/shard_map/ppermute | solution.py:70
  2.8 4.9 %collective-permute-start = (f32[64,256]{1,0:T(8,128)S(1)}, f32[64,256]{1,0:T(8,128)S(1)}, u32[]{:S(2)}, u32[]{:S(2)}) collective-permute-start(f32[64,256]{1,0:T(8,128)S(1)} %get-tuple-element.15), channel_id=1, source_target_pairs={{0,8},{1,12},{2,10},{3,14},{4,9},{5,13},{6,11},{7,15},{8,0},{9,4},... | collective-permute-start | bytes 196616 | tf_op jit(solution)/shard_map/ppermute | solution.py:70
  4.1 6.2 %collective-permute-start.1 = (f32[64,256]{1,0:T(8,128)S(1)}, f32[64,256]{1,0:T(8,128)S(1)}, u32[]{:S(2)}, u32[]{:S(2)}) collective-permute-start(f32[64,256]{1,0:T(8,128)S(1)} %get-tuple-element.16), channel_id=1, source_target_pairs={{0,16},{1,20},{2,18},{3,22},{4,17},{5,21},{6,19},{7,23},{8,24},{9,... | collective-permute-start | bytes 196616 | tf_op jit(solution)/shard_map/ppermute | solution.py:70
  5.8 7.6 %collective-permute-start.2 = (f32[64,256]{1,0:T(8,128)S(1)}, f32[64,256]{1,0:T(8,128)S(1)}, u32[]{:S(2)}, u32[]{:S(2)}) collective-permute-start(f32[64,256]{1,0:T(8,128)S(1)} %get-tuple-element.17), channel_id=1, source_target_pairs={{0,24},{1,28},{2,26},{3,30},{4,25},{5,29},{6,27},{7,31},{8,16},{9,... | collective-permute-start | bytes 196616 | tf_op jit(solution)/shard_map/ppermute | solution.py:70
  13.4 1.7 %collective-permute-start.5 = (f32[320,256]{1,0:T(8,128)S(1)}, f32[320,256]{1,0:T(8,128)S(1)}, u32[]{:S(2)}, u32[]{:S(2)}) collective-permute-start(f32[320,256]{1,0:T(8,128)S(1)} %shard_map.38.refs_0_.refs_3_.refs_1_), channel_id=1, source_target_pairs={{0,1},{1,0},{2,3},{3,2},{4,5},{5,4},{6,7},{7,6},{8,9},{9,8},{10,11... | collective-permute-start | bytes 983048 | tf_op jit(solution)/shard_map/ppermute | solution.py:70
  13.5 1.8 %collective-permute-start.6 = (f32[128,256]{1,0:T(8,128)S(1)}, f32[128,256]{1,0:T(8,128)S(1)}, u32[]{:S(2)}, u32[]{:S(2)}) collective-permute-start(f32[128,256]{1,0:T(8,128)S(1)} %shard_map.39.refs_2_), channel_id=1, source_target_pairs={{0,1},{1,0},{2,3},{3,2},{4,5},{5,4},{6,7},{7,6},{8,10},{9,11},{10,... | collective-permute-start | bytes 393224 | tf_op jit(solution)/shard_map/ppermute | solution.py:70
  15.1 1.3 %collective-permute-start.7 = (f32[256,128]{1,0:T(8,128)S(1)}, f32[256,128]{1,0:T(8,128)S(1)}, u32[]{:S(2)}, u32[]{:S(2)}) collective-permute-start(f32[256,128]{1,0:T(8,128)S(1)} %shard_map.40.refs_6_), channel_id=1, source_target_pairs={{0,8},{1,9},{2,10},{3,11},{4,12},{5,13},{6,14},{7,15},{8,0},{9,1},... | collective-permute-start | bytes 393224 | tf_op jit(solution)/shard_map/ppermute | solution.py:70
  16.5 6.0 %collective-permute-start.8 = (f32[640,256]{1,0:T(8,128)S(1)}, f32[640,256]{1,0:T(8,128)S(1)}, u32[]{:S(2)}, u32[]{:S(2)}) collective-permute-start(f32[640,256]{1,0:T(8,128)S(1)} %shard_map.41.refs_5_.refs_3_), channel_id=1, source_target_pairs={{0,1},{1,0},{2,3},{3,2},{4,5},{5,4},{6,7},{7,6},{8,9},{9,8},{10,11... | collective-permute-start | bytes 1966088 | tf_op jit(solution)/shard_map/ppermute | solution.py:70
  16.7 7.3 %collective-permute-start.11 = (f32[256,128]{1,0:T(8,128)S(1)}, f32[256,128]{1,0:T(8,128)S(1)}, u32[]{:S(2)}, u32[]{:S(2)}) collective-permute-start(f32[256,128]{1,0:T(8,128)S(1)} %collective-permute-done.7.refs_4_.refs_7_), channel_id=1, source_target_pairs={{0,1},{1,0},{2,3},{3,2},{4,5},{5,4},{6,7},{7,6},{8,12},{9,13},{10,... | collective-permute-start | bytes 393224 | tf_op jit(solution)/shard_map/ppermute | solution.py:70
  17.1 14.7 %collective-permute-start.10 = (f32[256,128]{1,0:T(8,128)S(1)}, f32[256,128]{1,0:T(8,128)S(1)}, u32[]{:S(2)}, u32[]{:S(2)}) collective-permute-start(f32[256,128]{1,0:T(8,128)S(1)} %collective-permute-done.7.refs_4_.refs_7_), channel_id=1, source_target_pairs={{0,1},{1,0},{2,3},{3,2},{4,5},{5,4},{6,7},{7,6},{8,16},{9,17},{10,... | collective-permute-start | bytes 393224 | tf_op jit(solution)/shard_map/ppermute | solution.py:70
  22.5 9.3 %collective-permute-start.9 = (f32[256,128]{1,0:T(8,128)S(1)}, f32[256,128]{1,0:T(8,128)S(1)}, u32[]{:S(2)}, u32[]{:S(2)}) collective-permute-start(f32[256,128]{1,0:T(8,128)S(1)} %collective-permute-done.7.refs_4_.refs_7_), channel_id=1, source_target_pairs={{0,1},{1,0},{2,3},{3,2},{4,5},{5,4},{6,7},{7,6},{8,24},{9,25},{10,... | collective-permute-start | bytes 393224 | tf_op jit(solution)/shard_map/ppermute | solution.py:70
  24.3 9.7 %collective-permute-start.13 = (f32[256,128]{1,0:T(8,128)S(1)}, f32[256,128]{1,0:T(8,128)S(1)}, u32[]{:S(2)}, u32[]{:S(2)}) collective-permute-start(f32[256,128]{1,0:T(8,128)S(1)} %shard_map.43.refs_2_.refs_7_), channel_id=1, source_target_pairs={{0,1},{1,0},{2,3},{3,2},{4,5},{5,4},{6,7},{7,6},{8,16},{9,17},{10,... | collective-permute-start | bytes 393224 | tf_op jit(solution)/shard_map/ppermute | solution.py:70
  27.7 6.3 %collective-permute-start.14 = (f32[256,128]{1,0:T(8,128)S(1)}, f32[256,128]{1,0:T(8,128)S(1)}, u32[]{:S(2)}, u32[]{:S(2)}) collective-permute-start(f32[256,128]{1,0:T(8,128)S(1)} %shard_map.43.refs_2_.refs_7_), channel_id=1, source_target_pairs={{0,1},{1,0},{2,3},{3,2},{4,5},{5,4},{6,7},{7,6},{8,24},{9,25},{10,... | collective-permute-start | bytes 393224 | tf_op jit(solution)/shard_map/ppermute | solution.py:70
  31.9 6.0 %collective-permute-start.12 = (f32[256,128]{1,0:T(8,128)S(1)}, f32[256,128]{1,0:T(8,128)S(1)}, u32[]{:S(2)}, u32[]{:S(2)}) collective-permute-start(f32[256,128]{1,0:T(8,128)S(1)} %shard_map.44.refs_5_), channel_id=1, source_target_pairs={{0,1},{1,0},{2,3},{3,2},{4,5},{5,4},{6,7},{7,6},{8,9},{9,8},{10,11... | collective-permute-start | bytes 393224 | tf_op jit(solution)/shard_map/ppermute | solution.py:70
  34.0 5.7 %collective-permute-start.15 = (f32[256,128]{1,0:T(8,128)S(1)}, f32[256,128]{1,0:T(8,128)S(1)}, u32[]{:S(2)}, u32[]{:S(2)}) collective-permute-start(f32[256,128]{1,0:T(8,128)S(1)} %shard_map.47.refs_5_), channel_id=1, source_target_pairs={{0,1},{1,0},{2,3},{3,2},{4,5},{5,4},{6,7},{7,6},{8,9},{9,8},{10,11... | collective-permute-start | bytes 393224 | tf_op jit(solution)/shard_map/ppermute | solution.py:70

commit v7 on v6

--- a/solution.py
+++ b/solution.py
@@ -174,11 +174,17 @@
         near = [near, *along(near, lambda q: 0 < q < n_win)]
 
         def rest(*refs):
-            own, near, packed = refs[:n_half], refs[n_half:-1], refs[-1]
+            own, near, packed = refs[:n_half], refs[n_half], refs[-1]
             for s, ref in enumerate(own):
                 packed[s * far : (s + 1) * far] = ref[part:]
-            for s, ref in enumerate(near):
-                packed[n_half * far + s * units : n_half * far + (s + 1) * units] = ref[...]
+            packed[n_half * far :] = near[...]
+
+        more = call(rest, [(n_half * far + units, rows)], [own, *own_along, near[0]])
+        more = [more, swap_cores(more)]
+
+        def stack(*refs):
+            for s, ref in enumerate(refs[:-1]):
+                refs[-1][s * units : (s + 1) * units] = ref[...]
 
         def columns(blocks, panel, count, row=0):
             got = []
@@ -186,7 +192,9 @@
                 for core in range(2):
                     for s in range(n_half):
                         if row:
-                            ref, at = blocks[2 + core], n_half * far + s * units + p * part
+                            ref, at = blocks[2 + core], n_half * far + p * part
+                            if s:
+                                ref, at = blocks[4 + core], (s - 1) * units + p * part
                         elif p:
                             ref, at = blocks[2 + core], s * far + (p - 1) * part
                         else:
@@ -227,9 +235,9 @@
         results = [either]
 
         def arrive(*refs, pairs):
-            got = refs[0][...]
+            got = refs[0][:rows]
             for t, ref in zip(pairs[1:], refs[1:-1], strict=True):
-                got = jnp.where(place()[0] == t, ref[...], got)
+                got = jnp.where(place()[0] == t, ref[:rows], got)
             refs[-1][...] = got
 
         early, blocks = [], None
@@ -237,11 +245,11 @@
             here = climb(either, w, w + 1)
             there = swap_rows(here, lambda q, w=w: q == w + 1)
             early.append([climb(here, w + 1, t) for t in range(n_pair - 1, w + 1, -1)])
-            late = call(rest, [(n_half * (far + units), rows)], [own, *own_along, *near], last=[here])
-            blocks = [*soon, late, swap_cores(late)]
+            late = call(stack, [((n_half - 1) * units, rows)], near[1:], last=[either])
+            blocks = [*soon, *more, late, swap_cores(late)]
 
             def lean(mine, beside, rhs, *refs):
-                blocks, here, (fixed, slope, kept, inverse) = refs[:4], refs[4], refs[5:]
+                blocks, here, (fixed, slope, kept, inverse) = refs[:6], refs[6], refs[7:]
                 x = place()[1]
                 assemble(*blocks[:2], mine, beside, inverse)
 
@@ -288,7 +296,7 @@
             traded = swap_rows(value, lambda q: q >= n_win)
 
             def update(start, *refs, other, at=2 * i):
-                blocks, value, out = refs[:4], refs[4], refs[5]
+                blocks, value, out = refs[:6], refs[6], refs[7]
                 a, b = columns(blocks, at, 1), columns(blocks, at + 1, 1)
                 block = jnp.where((place()[1] == 0) == other, b, a)
                 out[...] = start[...] - dot(block, ordered(value), (0, 0))
@@ -299,12 +307,12 @@
                 left = call(functools.partial(update, other=True), [(rows, width)], [left, *blocks, traded])
 
         def finish(*refs):
-            update(*refs[:6], refs[-1], other=True)
+            update(*refs[:8], refs[-1], other=True)
             for w in range(n_win):
 
                 @pl.when(place()[0] == w)
                 def _(w=w):
-                    refs[-1][...] = refs[6 + w][...]
+                    refs[-1][...] = refs[8 + w][...]
 
         return call(finish, [(rows, width)], [left, *blocks, traded, *results], home=True)
 

time: 41.4 us -> 40.5 us (0.978)
  starting transfers between devices: 17.9 us -> 17.2 us
    ppermute x16 -> x17, starting transfers between devices: 17.9 us -> 17.2 us  [hop(): return lax.ppermute(value, AXES, edges)]
    ppermute x16 -> x17, waiting for transfers between devices: 17.7 us -> 17.6 us  [hop(): return lax.ppermute(value, AXES, edges)]
    pallas_call x13 -> x14, Pallas kernels: 4.98 us -> 4.97 us  [call(): pl.pallas_call(kernel, out_shape=out, in_specs=[ANY] * len(first) + [VMEM...]
  transfers between devices with their start and end apart: 16 -> 17, of which waited for: 9 -> 10; matrix products, arithmetic and copies ran while one was open for 0% -> 0% of each run, Pallas kernels for 7% -> 7%
where the time goes in v7:
time: 40.5 us; the launch traced here: 39.8 us
  waiting for transfers between devices  17.6 us (43%)
  starting transfers between devices  17.2 us (42%)
  Pallas kernels  4.97 us (12%)
    ppermute x17, waiting for transfers between devices, hop(): return lax.ppermute(value, AXES, edges)  17.6 us
    ppermute x17, starting transfers between devices, hop(): return lax.ppermute(value, AXES, edges)  17.2 us
    pallas_call x14, Pallas kernels, call(): pl.pallas_call(kernel, out_shape=out, in_specs=[ANY] * len(first) + [VMEM...  4.97 us
  transfers between devices with their start and end apart: 17, of which 10 were waited for; matrix products, arithmetic and copies ran while one was open for 0% of the time, Pallas kernels for 7%

profile of v7, /device:TPU:18, one launch (start us, length us, event | category | flops | bytes accessed | tf_op | source)
XLA Modules:
  0.0 39.8 jit_solution(8916885411395471537)
XLA Ops:
  0.0 1.1 %shard_map.37 = (f32[320,256]{1,0:T(8,128)S(1)}, f32[256,256]{1,0:T(8,128)S(1)}, f32[256,128]{1,0:T(8,128)S(1)}, f32[64,256]{1,0:T(8,128)S(1)}, f32[64,256]{1,0:...) custom-call(f32[256,128]{1,0:T(8,128)} %refs_0_.1, f32[256,256]{1,0:T(8,128)} %bitcast.3, f32[4,32,256]{2,1,0:T(8,128)} %refs_2_.1), custom_call_target="tpu_custom_call" | custom-call | tf_op jit(solution)/shard_map/pallas_call | solution.py:38
  1.1 0.1 collective-permute-start.4
  1.2 1.6 %collective-permute-start.3 = (f32[256,256]{1,0:T(8,128)S(1)}, f32[256,256]{1,0:T(8,128)S(1)}, u32[]{:S(2)}, u32[]{:S(2)}) collective-permute-start(f32[256,256]{1,0:T(8,128)S(1)} %get-tuple-element.18.refs_3_.refs_0_), channel_id=1, source_target_pairs={{0,2},{1,3},{2,0},{3,1},{4,6},{5,7},{6,4},{7,5},{8,10},{9,11},{10,... | collective-permute-start | bytes 786440 | tf_op jit(solution)/shard_map/ppermute | solution.py:70
  2.8 1.3 %collective-permute-start = (f32[64,256]{1,0:T(8,128)S(1)}, f32[64,256]{1,0:T(8,128)S(1)}, u32[]{:S(2)}, u32[]{:S(2)}) collective-permute-start(f32[64,256]{1,0:T(8,128)S(1)} %get-tuple-element.15), channel_id=1, source_target_pairs={{0,8},{1,12},{2,10},{3,14},{4,9},{5,13},{6,11},{7,15},{8,0},{9,4},... | collective-permute-start | bytes 196616 | tf_op jit(solution)/shard_map/ppermute | solution.py:70
  4.1 1.7 %collective-permute-start.1 = (f32[64,256]{1,0:T(8,128)S(1)}, f32[64,256]{1,0:T(8,128)S(1)}, u32[]{:S(2)}, u32[]{:S(2)}) collective-permute-start(f32[64,256]{1,0:T(8,128)S(1)} %get-tuple-element.16), channel_id=1, source_target_pairs={{0,16},{1,20},{2,18},{3,22},{4,17},{5,21},{6,19},{7,23},{8,24},{9,... | collective-permute-start | bytes 196616 | tf_op jit(solution)/shard_map/ppermute | solution.py:70
  5.8 0.9 %collective-permute-start.2 = (f32[64,256]{1,0:T(8,128)S(1)}, f32[64,256]{1,0:T(8,128)S(1)}, u32[]{:S(2)}, u32[]{:S(2)}) collective-permute-start(f32[64,256]{1,0:T(8,128)S(1)} %get-tuple-element.17), channel_id=1, source_target_pairs={{0,24},{1,28},{2,26},{3,30},{4,25},{5,29},{6,27},{7,31},{8,16},{9,... | collective-permute-start | bytes 196616 | tf_op jit(solution)/shard_map/ppermute | solution.py:70
  6.6 1.1 %collective-permute-done.refs_0_.refs_1_ = f32[64,256]{1,0:T(8,128)S(1)} collective-permute-done((f32[64,256]{1,0:T(8,128)S(1)}, f32[64,256]{1,0:T(8,128)S(1)}, u32[]{:S(2)}, u32[]{:S(2)}) %collective-permute-start) | collective-permute-done | bytes 65568 | tf_op jit(solution)/shard_map/ppermute | solution.py:70
  7.7 2.6 %collective-permute-done.1.refs_1_.refs_2_ = f32[64,256]{1,0:T(8,128)S(1)} collective-permute-done((f32[64,256]{1,0:T(8,128)S(1)}, f32[64,256]{1,0:T(8,128)S(1)}, u32[]{:S(2)}, u32[]{:S(2)}) %collective-permute-start.1) | collective-permute-done | bytes 65568 | tf_op jit(solution)/shard_map/ppermute | solution.py:70
  10.3 3.1 %collective-permute-done.2.refs_2_.refs_3_ = f32[64,256]{1,0:T(8,128)S(1)} collective-permute-done((f32[64,256]{1,0:T(8,128)S(1)}, f32[64,256]{1,0:T(8,128)S(1)}, u32[]{:S(2)}, u32[]{:S(2)}) %collective-permute-start.2) | collective-permute-done | bytes 65568 | tf_op jit(solution)/shard_map/ppermute | solution.py:70
  13.4 0.0 collective-permute-done.3.refs_4_.refs_1_
  13.4 0.0 collective-permute-done.4.refs_5_.refs_0_.refs_3_.refs_1_
  13.4 0.1 collective-permute-start.5
  13.6 0.6 %collective-permute-start.6 = (f32[512,256]{1,0:T(8,128)S(1)}, f32[512,256]{1,0:T(8,128)S(1)}, u32[]{:S(2)}, u32[]{:S(2)}) collective-permute-start(f32[512,256]{1,0:T(8,128)S(1)} %shard_map.40.refs_5_.refs_3_), channel_id=1, source_target_pairs={{0,1},{1,0},{2,3},{3,2},{4,5},{5,4},{6,7},{7,6},{8,9},{9,8},{10,11... | collective-permute-start | bytes 1572872 | tf_op jit(solution)/shard_map/ppermute | solution.py:70
  14.1 0.1 collective-permute-start.7
  14.2 0.9 %collective-permute-done.5.refs_1_.refs_4_.refs_2_ = f32[320,256]{1,0:T(8,128)S(1)} collective-permute-done((f32[320,256]{1,0:T(8,128)S(1)}, f32[320,256]{1,0:T(8,128)S(1)}, u32[]{:S(2)}, u32[]{:S(2)}) %collective-permute-start.5) | collective-permute-done | bytes 327712 | tf_op jit(solution)/shard_map/ppermute | solution.py:70
  15.1 0.1 collective-permute-start.9
  15.3 0.8 %collective-permute-done.7.refs_0_ = f32[128,256]{1,0:T(8,128)S(1)} collective-permute-done((f32[128,256]{1,0:T(8,128)S(1)}, f32[128,256]{1,0:T(8,128)S(1)}, u32[]{:S(2)}, u32[]{:S(2)}) %collective-permute-start.7) | collective-permute-done | bytes 131104 | tf_op jit(solution)/shard_map/ppermute | solution.py:70
  16.1 0.2 collective-permute-start.8
  16.3 0.2 collective-permute-done.9.refs_9_
  16.5 0.2 collective-permute-start.12
  16.7 0.3 collective-permute-start.10
  17.0 5.3 %collective-permute-start.11 = (f32[256,128]{1,0:T(8,128)S(1)}, f32[256,128]{1,0:T(8,128)S(1)}, u32[]{:S(2)}, u32[]{:S(2)}) collective-permute-start(f32[256,128]{1,0:T(8,128)S(1)} %collective-permute-done.9.refs_9_), channel_id=1, source_target_pairs={{0,1},{1,0},{2,3},{3,2},{4,5},{5,4},{6,7},{7,6},{8,16},{9,17},{10,... | collective-permute-start | bytes 393224 | tf_op jit(solution)/shard_map/ppermute | solution.py:70
  22.3 0.0 collective-permute-done.8.refs_8_.refs_6_
  22.3 0.0 collective-permute-done.6.refs_6_.refs_4_
  22.3 1.5 %shard_map.43 = (f32[256,128]{1,0:T(8,128)S(1)}, f32[256,256]{1,0:T(8,128)S(1)}) custom-call(f32[64,256]{1,0:T(8,128)S(1)} %get-tuple-element.20.refs_2_.refs_0_, f32[320,256]{1,0:T(8,128)S(1)} %collective-permute-done.4.refs_5_.refs_0_.refs_3_.refs_1_, f32[256,128]{1,0:T(8,128)S(1)} %get-tuple-element.14.refs_4_.refs_2_.refs_0_, ...), custom_call_target="tpu_custom_call" | custom-call | tf_op jit(solution)/shard_map/pallas_call | solution.py:38
  23.9 0.0 collective-permute-done.12.refs_2_
  23.9 0.3 shard_map.44.refs_2_.refs_9_
  24.1 2.5 %collective-permute-start.14 = (f32[256,128]{1,0:T(8,128)S(1)}, f32[256,128]{1,0:T(8,128)S(1)}, u32[]{:S(2)}, u32[]{:S(2)}) collective-permute-start(f32[256,128]{1,0:T(8,128)S(1)} %shard_map.44.refs_2_.refs_9_), channel_id=1, source_target_pairs={{0,1},{1,0},{2,3},{3,2},{4,5},{5,4},{6,7},{7,6},{8,16},{9,17},{10,... | collective-permute-start | bytes 393224 | tf_op jit(solution)/shard_map/ppermute | solution.py:70
  26.7 0.0 collective-permute-start.15
  26.7 0.0 collective-permute-done.10.refs_0_
  26.7 4.5 %collective-permute-done.11.refs_1_ = f32[256,128]{1,0:T(8,128)S(1)} collective-permute-done((f32[256,128]{1,0:T(8,128)S(1)}, f32[256,128]{1,0:T(8,128)S(1)}, u32[]{:S(2)}, u32[]{:S(2)}) %collective-permute-start.11) | collective-permute-done | bytes 131104 | tf_op jit(solution)/shard_map/ppermute | solution.py:70
  31.2 1.1 %collective-permute-start.13 = (f32[256,128]{1,0:T(8,128)S(1)}, f32[256,128]{1,0:T(8,128)S(1)}, u32[]{:S(2)}, u32[]{:S(2)}) collective-permute-start(f32[256,128]{1,0:T(8,128)S(1)} %shard_map.45.refs_7_), channel_id=1, source_target_pairs={{0,1},{1,0},{2,3},{3,2},{4,5},{5,4},{6,7},{7,6},{8,9},{9,8},{10,11... | collective-permute-start | bytes 393224 | tf_op jit(solution)/shard_map/ppermute | solution.py:70
  32.3 0.6 %collective-permute-done.14.refs_0_ = f32[256,128]{1,0:T(8,128)S(1)} collective-permute-done((f32[256,128]{1,0:T(8,128)S(1)}, f32[256,128]{1,0:T(8,128)S(1)}, u32[]{:S(2)}, u32[]{:S(2)}) %collective-permute-start.14) | collective-permute-done | bytes 131104 | tf_op jit(solution)/shard_map/ppermute | solution.py:70
  32.9 0.0 collective-permute-done.15.refs_1_
  32.9 1.1 %collective-permute-start.16 = (f32[256,128]{1,0:T(8,128)S(1)}, f32[256,128]{1,0:T(8,128)S(1)}, u32[]{:S(2)}, u32[]{:S(2)}) collective-permute-start(f32[256,128]{1,0:T(8,128)S(1)} %shard_map.48.refs_7_), channel_id=1, source_target_pairs={{0,1},{1,0},{2,3},{3,2},{4,5},{5,4},{6,7},{7,6},{8,9},{9,8},{10,11... | collective-permute-start | bytes 393224 | tf_op jit(solution)/shard_map/ppermute | solution.py:70
  34.1 0.3 shard_map.46.refs_0_
  34.4 3.1 %collective-permute-done.13.refs_7_ = f32[256,128]{1,0:T(8,128)S(1)} collective-permute-done((f32[256,128]{1,0:T(8,128)S(1)}, f32[256,128]{1,0:T(8,128)S(1)}, u32[]{:S(2)}, u32[]{:S(2)}) %collective-permute-start.13) | collective-permute-done | bytes 131104 | tf_op jit(solution)/shard_map/ppermute | solution.py:70
  37.5 0.3 shard_map.47.refs_0_
  37.8 0.3 shard_map.49.refs_0_
  38.1 0.8 %collective-permute-done.16.refs_7_ = f32[256,128]{1,0:T(8,128)S(1)} collective-permute-done((f32[256,128]{1,0:T(8,128)S(1)}, f32[256,128]{1,0:T(8,128)S(1)}, u32[]{:S(2)}, u32[]{:S(2)}) %collective-permute-start.16) | collective-permute-done | bytes 131104 | tf_op jit(solution)/shard_map/ppermute | solution.py:70
  38.9 1.0 %shard_map.50 = f32[256,128]{1,0:T(8,128)} custom-call(f32[256,128]{1,0:T(8,128)S(1)} %shard_map.49.refs_0_, f32[320,256]{1,0:T(8,128)S(1)} %shard_map.38.refs_0_.refs_3_.refs_1_, f32[320,256]{1,0:T(8,128)S(1)} %collective-permute-done.5.refs_1_.refs_4_.refs_2_, f32[512,256]{1,0:T(8,128)S(1)} %shard_map.40.refs_5_.refs_3_, ...), custom_call_target="tpu_custom_call" | custom-call | tf_op jit(solution)/shard_map/pallas_call | solution.py:38
  (7 shorter events, 0.1 us)
Async XLA Ops:
  1.1 12.3 %collective-permute-start.4 = (f32[320,256]{1,0:T(8,128)S(1)}, f32[320,256]{1,0:T(8,128)S(1)}, u32[]{:S(2)}, u32[]{:S(2)}) collective-permute-start(f32[320,256]{1,0:T(8,128)S(1)} %get-tuple-element.19), channel_id=1, source_target_pairs={{0,4},{1,5},{2,6},{3,7},{4,0},{5,1},{6,2},{7,3},{8,12},{9,13},{10,... | collective-permute-start | bytes 983048 | tf_op jit(solution)/shard_map/ppermute | solution.py:70
  1.2 12.2 %collective-permute-start.3 = (f32[256,256]{1,0:T(8,128)S(1)}, f32[256,256]{1,0:T(8,128)S(1)}, u32[]{:S(2)}, u32[]{:S(2)}) collective-permute-start(f32[256,256]{1,0:T(8,128)S(1)} %get-tuple-element.18.refs_3_.refs_0_), channel_id=1, source_target_pairs={{0,2},{1,3},{2,0},{3,1},{4,6},{5,7},{6,4},{7,5},{8,10},{9,11},{10,... | collective-permute-start | bytes 786440 | tf_op jit(solution)/shard_map/ppermute | solution.py:70
  2.8 4.9 %collective-permute-start = (f32[64,256]{1,0:T(8,128)S(1)}, f32[64,256]{1,0:T(8,128)S(1)}, u32[]{:S(2)}, u32[]{:S(2)}) collective-permute-start(f32[64,256]{1,0:T(8,128)S(1)} %get-tuple-element.15), channel_id=1, source_target_pairs={{0,8},{1,12},{2,10},{3,14},{4,9},{5,13},{6,11},{7,15},{8,0},{9,4},... | collective-permute-start | bytes 196616 | tf_op jit(solution)/shard_map/ppermute | solution.py:70
  4.1 6.2 %collective-permute-start.1 = (f32[64,256]{1,0:T(8,128)S(1)}, f32[64,256]{1,0:T(8,128)S(1)}, u32[]{:S(2)}, u32[]{:S(2)}) collective-permute-start(f32[64,256]{1,0:T(8,128)S(1)} %get-tuple-element.16), channel_id=1, source_target_pairs={{0,16},{1,20},{2,18},{3,22},{4,17},{5,21},{6,19},{7,23},{8,24},{9,... | collective-permute-start | bytes 196616 | tf_op jit(solution)/shard_map/ppermute | solution.py:70
  5.8 7.6 %collective-permute-start.2 = (f32[64,256]{1,0:T(8,128)S(1)}, f32[64,256]{1,0:T(8,128)S(1)}, u32[]{:S(2)}, u32[]{:S(2)}) collective-permute-start(f32[64,256]{1,0:T(8,128)S(1)} %get-tuple-element.17), channel_id=1, source_target_pairs={{0,24},{1,28},{2,26},{3,30},{4,25},{5,29},{6,27},{7,31},{8,16},{9,... | collective-permute-start | bytes 196616 | tf_op jit(solution)/shard_map/ppermute | solution.py:70
  13.4 1.7 %collective-permute-start.5 = (f32[320,256]{1,0:T(8,128)S(1)}, f32[320,256]{1,0:T(8,128)S(1)}, u32[]{:S(2)}, u32[]{:S(2)}) collective-permute-start(f32[320,256]{1,0:T(8,128)S(1)} %shard_map.38.refs_0_.refs_3_.refs_1_), channel_id=1, source_target_pairs={{0,1},{1,0},{2,3},{3,2},{4,5},{5,4},{6,7},{7,6},{8,9},{9,8},{10,11... | collective-permute-start | bytes 983048 | tf_op jit(solution)/shard_map/ppermute | solution.py:70
  13.6 8.7 %collective-permute-start.6 = (f32[512,256]{1,0:T(8,128)S(1)}, f32[512,256]{1,0:T(8,128)S(1)}, u32[]{:S(2)}, u32[]{:S(2)}) collective-permute-start(f32[512,256]{1,0:T(8,128)S(1)} %shard_map.40.refs_5_.refs_3_), channel_id=1, source_target_pairs={{0,1},{1,0},{2,3},{3,2},{4,5},{5,4},{6,7},{7,6},{8,9},{9,8},{10,11... | collective-permute-start | bytes 1572872 | tf_op jit(solution)/shard_map/ppermute | solution.py:70
  14.1 1.9 %collective-permute-start.7 = (f32[128,256]{1,0:T(8,128)S(1)}, f32[128,256]{1,0:T(8,128)S(1)}, u32[]{:S(2)}, u32[]{:S(2)}) collective-permute-start(f32[128,256]{1,0:T(8,128)S(1)} %shard_map.39.refs_2_), channel_id=1, source_target_pairs={{0,1},{1,0},{2,3},{3,2},{4,5},{5,4},{6,7},{7,6},{8,10},{9,11},{10,... | collective-permute-start | bytes 393224 | tf_op jit(solution)/shard_map/ppermute | solution.py:70
  15.1 1.3 %collective-permute-start.9 = (f32[256,128]{1,0:T(8,128)S(1)}, f32[256,128]{1,0:T(8,128)S(1)}, u32[]{:S(2)}, u32[]{:S(2)}) collective-permute-start(f32[256,128]{1,0:T(8,128)S(1)} %shard_map.41.refs_1_.refs_8_), channel_id=1, source_target_pairs={{0,8},{1,9},{2,10},{3,11},{4,12},{5,13},{6,14},{7,15},{8,0},{9,1},... | collective-permute-start | bytes 393224 | tf_op jit(solution)/shard_map/ppermute | solution.py:70
  16.1 6.2 %collective-permute-start.8 = (f32[128,256]{1,0:T(8,128)S(1)}, f32[128,256]{1,0:T(8,128)S(1)}, u32[]{:S(2)}, u32[]{:S(2)}) collective-permute-start(f32[128,256]{1,0:T(8,128)S(1)} %shard_map.42.refs_7_.refs_5_), channel_id=1, source_target_pairs={{0,1},{1,0},{2,3},{3,2},{4,5},{5,4},{6,7},{7,6},{8,9},{9,8},{10,11... | collective-permute-start | bytes 393224 | tf_op jit(solution)/shard_map/ppermute | solution.py:70
  16.5 7.4 %collective-permute-start.12 = (f32[256,128]{1,0:T(8,128)S(1)}, f32[256,128]{1,0:T(8,128)S(1)}, u32[]{:S(2)}, u32[]{:S(2)}) collective-permute-start(f32[256,128]{1,0:T(8,128)S(1)} %collective-permute-done.9.refs_9_), channel_id=1, source_target_pairs={{0,1},{1,0},{2,3},{3,2},{4,5},{5,4},{6,7},{7,6},{8,12},{9,13},{10,... | collective-permute-start | bytes 393224 | tf_op jit(solution)/shard_map/ppermute | solution.py:70
  16.7 10.0 %collective-permute-start.10 = (f32[256,128]{1,0:T(8,128)S(1)}, f32[256,128]{1,0:T(8,128)S(1)}, u32[]{:S(2)}, u32[]{:S(2)}) collective-permute-start(f32[256,128]{1,0:T(8,128)S(1)} %collective-permute-done.9.refs_9_), channel_id=1, source_target_pairs={{0,1},{1,0},{2,3},{3,2},{4,5},{5,4},{6,7},{7,6},{8,24},{9,25},{10,... | collective-permute-start | bytes 393224 | tf_op jit(solution)/shard_map/ppermute | solution.py:70
  17.0 14.2 %collective-permute-start.11 = (f32[256,128]{1,0:T(8,128)S(1)}, f32[256,128]{1,0:T(8,128)S(1)}, u32[]{:S(2)}, u32[]{:S(2)}) collective-permute-start(f32[256,128]{1,0:T(8,128)S(1)} %collective-permute-done.9.refs_9_), channel_id=1, source_target_pairs={{0,1},{1,0},{2,3},{3,2},{4,5},{5,4},{6,7},{7,6},{8,16},{9,17},{10,... | collective-permute-start | bytes 393224 | tf_op jit(solution)/shard_map/ppermute | solution.py:70
  24.1 8.8 %collective-permute-start.14 = (f32[256,128]{1,0:T(8,128)S(1)}, f32[256,128]{1,0:T(8,128)S(1)}, u32[]{:S(2)}, u32[]{:S(2)}) collective-permute-start(f32[256,128]{1,0:T(8,128)S(1)} %shard_map.44.refs_2_.refs_9_), channel_id=1, source_target_pairs={{0,1},{1,0},{2,3},{3,2},{4,5},{5,4},{6,7},{7,6},{8,16},{9,17},{10,... | collective-permute-start | bytes 393224 | tf_op jit(solution)/shard_map/ppermute | solution.py:70
  26.7 6.3 %collective-permute-start.15 = (f32[256,128]{1,0:T(8,128)S(1)}, f32[256,128]{1,0:T(8,128)S(1)}, u32[]{:S(2)}, u32[]{:S(2)}) collective-permute-start(f32[256,128]{1,0:T(8,128)S(1)} %shard_map.44.refs_2_.refs_9_), channel_id=1, source_target_pairs={{0,1},{1,0},{2,3},{3,2},{4,5},{5,4},{6,7},{7,6},{8,24},{9,25},{10,... | collective-permute-start | bytes 393224 | tf_op jit(solution)/shard_map/ppermute | solution.py:70
  31.2 6.3 %collective-permute-start.13 = (f32[256,128]{1,0:T(8,128)S(1)}, f32[256,128]{1,0:T(8,128)S(1)}, u32[]{:S(2)}, u32[]{:S(2)}) collective-permute-start(f32[256,128]{1,0:T(8,128)S(1)} %shard_map.45.refs_7_), channel_id=1, source_target_pairs={{0,1},{1,0},{2,3},{3,2},{4,5},{5,4},{6,7},{7,6},{8,9},{9,8},{10,11... | collective-permute-start | bytes 393224 | tf_op jit(solution)/shard_map/ppermute | solution.py:70
  32.9 5.9 %collective-permute-start.16 = (f32[256,128]{1,0:T(8,128)S(1)}, f32[256,128]{1,0:T(8,128)S(1)}, u32[]{:S(2)}, u32[]{:S(2)}) collective-permute-start(f32[256,128]{1,0:T(8,128)S(1)} %shard_map.48.refs_7_), channel_id=1, source_target_pairs={{0,1},{1,0},{2,3},{3,2},{4,5},{5,4},{6,7},{7,6},{8,9},{9,8},{10,11... | collective-permute-start | bytes 393224 | tf_op jit(solution)/shard_map/ppermute | solution.py:70

commit v8 on v7

--- a/solution.py
+++ b/solution.py
@@ -248,10 +248,14 @@
             late = call(stack, [((n_half - 1) * units, rows)], near[1:], last=[either])
             blocks = [*soon, *more, late, swap_cores(late)]
 
-            def lean(mine, beside, rhs, *refs):
+            def lean(mine, beside, rhs, *refs, w=w):
                 blocks, here, (fixed, slope, kept, inverse) = refs[:6], refs[6], refs[7:]
                 x = place()[1]
-                assemble(*blocks[:2], mine, beside, inverse)
+                here_too = place()[0] == w + 1
+
+                @pl.when(here_too)
+                def _():
+                    assemble(*blocks[:2], mine, beside, inverse)
 
                 def solve(m, start, block, other):
                     fixed[...] = turn(dot(inverse[m], start))
@@ -259,12 +263,12 @@
 
                 mine = ordered(here)
 
-                @pl.when(x == 0)
+                @pl.when(jnp.logical_and(here_too, x == 0))
                 def _():
                     start = rhs[...] - dot(columns(blocks, 0, 1), mine, (0, 0))
                     solve(0, start, columns(blocks, 1, 1), True)
 
-                @pl.when(x == 1)
+                @pl.when(jnp.logical_and(here_too, x == 1))
                 def _():
                     start = unfold(beside) - dot(columns(blocks, 1, 1, 1), mine, (0, 0))
                     solve(0, start, columns(blocks, 0, 1, 1), True)

time: 40.5 us -> 40.5 us (level)
  Pallas kernels: 4.97 us -> 3.45 us
  starting transfers between devices: 17.2 us -> 18.7 us
    pallas_call x14, Pallas kernels: 4.97 us -> 3.45 us  [call(): pl.pallas_call(kernel, out_shape=out, in_specs=[ANY] * len(first) + [VMEM...]
    ppermute x17, starting transfers between devices: 17.2 us -> 18.7 us  [hop(): return lax.ppermute(value, AXES, edges)]
  transfers between devices with their start and end apart: 17 -> 17, of which waited for: 10 -> 10; matrix products, arithmetic and copies ran while one was open for 0% -> 0% of each run, Pallas kernels for 7% -> 3%
where the time goes in v8:
time: 40.5 us; the launch traced here: 39.8 us
  starting transfers between devices  18.7 us (46%)
  waiting for transfers between devices  17.6 us (43%)
  Pallas kernels  3.45 us (9%)
    ppermute x17, starting transfers between devices, hop(): return lax.ppermute(value, AXES, edges)  18.7 us
    ppermute x17, waiting for transfers between devices, hop(): return lax.ppermute(value, AXES, edges)  17.6 us
    pallas_call x14, Pallas kernels, call(): pl.pallas_call(kernel, out_shape=out, in_specs=[ANY] * len(first) + [VMEM...  3.45 us
  transfers between devices with their start and end apart: 17, of which 10 were waited for; matrix products, arithmetic and copies ran while one was open for 0% of the time, Pallas kernels for 3%

profile of v8, /device:TPU:18, one launch (start us, length us, event | category | flops | bytes accessed | tf_op | source)
XLA Modules:
  0.0 39.8 jit_solution(510928600264920068)
XLA Ops:
  0.0 1.1 %shard_map.37 = (f32[320,256]{1,0:T(8,128)S(1)}, f32[256,256]{1,0:T(8,128)S(1)}, f32[256,128]{1,0:T(8,128)S(1)}, f32[64,256]{1,0:T(8,128)S(1)}, f32[64,256]{1,0:...) custom-call(f32[256,128]{1,0:T(8,128)} %refs_0_.1, f32[256,256]{1,0:T(8,128)} %bitcast.3, f32[4,32,256]{2,1,0:T(8,128)} %refs_2_.1), custom_call_target="tpu_custom_call" | custom-call | tf_op jit(solution)/shard_map/pallas_call | solution.py:38
  1.1 0.1 collective-permute-start.4
  1.2 1.6 %collective-permute-start.3 = (f32[256,256]{1,0:T(8,128)S(1)}, f32[256,256]{1,0:T(8,128)S(1)}, u32[]{:S(2)}, u32[]{:S(2)}) collective-permute-start(f32[256,256]{1,0:T(8,128)S(1)} %get-tuple-element.18.refs_3_.refs_0_), channel_id=1, source_target_pairs={{0,2},{1,3},{2,0},{3,1},{4,6},{5,7},{6,4},{7,5},{8,10},{9,11},{10,... | collective-permute-start | bytes 786440 | tf_op jit(solution)/shard_map/ppermute | solution.py:70
  2.8 1.3 %collective-permute-start = (f32[64,256]{1,0:T(8,128)S(1)}, f32[64,256]{1,0:T(8,128)S(1)}, u32[]{:S(2)}, u32[]{:S(2)}) collective-permute-start(f32[64,256]{1,0:T(8,128)S(1)} %get-tuple-element.15), channel_id=1, source_target_pairs={{0,8},{1,12},{2,10},{3,14},{4,9},{5,13},{6,11},{7,15},{8,0},{9,4},... | collective-permute-start | bytes 196616 | tf_op jit(solution)/shard_map/ppermute | solution.py:70
  4.1 1.7 %collective-permute-start.1 = (f32[64,256]{1,0:T(8,128)S(1)}, f32[64,256]{1,0:T(8,128)S(1)}, u32[]{:S(2)}, u32[]{:S(2)}) collective-permute-start(f32[64,256]{1,0:T(8,128)S(1)} %get-tuple-element.16), channel_id=1, source_target_pairs={{0,16},{1,20},{2,18},{3,22},{4,17},{5,21},{6,19},{7,23},{8,24},{9,... | collective-permute-start | bytes 196616 | tf_op jit(solution)/shard_map/ppermute | solution.py:70
  5.8 0.9 %collective-permute-start.2 = (f32[64,256]{1,0:T(8,128)S(1)}, f32[64,256]{1,0:T(8,128)S(1)}, u32[]{:S(2)}, u32[]{:S(2)}) collective-permute-start(f32[64,256]{1,0:T(8,128)S(1)} %get-tuple-element.17), channel_id=1, source_target_pairs={{0,24},{1,28},{2,26},{3,30},{4,25},{5,29},{6,27},{7,31},{8,16},{9,... | collective-permute-start | bytes 196616 | tf_op jit(solution)/shard_map/ppermute | solution.py:70
  6.6 1.1 %collective-permute-done.refs_0_.refs_1_ = f32[64,256]{1,0:T(8,128)S(1)} collective-permute-done((f32[64,256]{1,0:T(8,128)S(1)}, f32[64,256]{1,0:T(8,128)S(1)}, u32[]{:S(2)}, u32[]{:S(2)}) %collective-permute-start) | collective-permute-done | bytes 65568 | tf_op jit(solution)/shard_map/ppermute | solution.py:70
  7.7 2.6 %collective-permute-done.1.refs_1_.refs_2_ = f32[64,256]{1,0:T(8,128)S(1)} collective-permute-done((f32[64,256]{1,0:T(8,128)S(1)}, f32[64,256]{1,0:T(8,128)S(1)}, u32[]{:S(2)}, u32[]{:S(2)}) %collective-permute-start.1) | collective-permute-done | bytes 65568 | tf_op jit(solution)/shard_map/ppermute | solution.py:70
  10.3 3.1 %collective-permute-done.2.refs_2_.refs_3_ = f32[64,256]{1,0:T(8,128)S(1)} collective-permute-done((f32[64,256]{1,0:T(8,128)S(1)}, f32[64,256]{1,0:T(8,128)S(1)}, u32[]{:S(2)}, u32[]{:S(2)}) %collective-permute-start.2) | collective-permute-done | bytes 65568 | tf_op jit(solution)/shard_map/ppermute | solution.py:70
  13.4 0.0 collective-permute-done.3.refs_4_.refs_1_
  13.4 0.0 collective-permute-done.4.refs_5_.refs_0_.refs_3_.refs_1_
  13.4 0.1 collective-permute-start.5
  13.6 0.6 %collective-permute-start.6 = (f32[512,256]{1,0:T(8,128)S(1)}, f32[512,256]{1,0:T(8,128)S(1)}, u32[]{:S(2)}, u32[]{:S(2)}) collective-permute-start(f32[512,256]{1,0:T(8,128)S(1)} %shard_map.40.refs_5_.refs_3_), channel_id=1, source_target_pairs={{0,1},{1,0},{2,3},{3,2},{4,5},{5,4},{6,7},{7,6},{8,9},{9,8},{10,11... | collective-permute-start | bytes 1572872 | tf_op jit(solution)/shard_map/ppermute | solution.py:70
  14.1 0.1 collective-permute-start.7
  14.2 0.9 %collective-permute-done.5.refs_1_.refs_4_.refs_2_ = f32[320,256]{1,0:T(8,128)S(1)} collective-permute-done((f32[320,256]{1,0:T(8,128)S(1)}, f32[320,256]{1,0:T(8,128)S(1)}, u32[]{:S(2)}, u32[]{:S(2)}) %collective-permute-start.5) | collective-permute-done | bytes 327712 | tf_op jit(solution)/shard_map/ppermute | solution.py:70
  15.1 0.1 collective-permute-start.9
  15.3 0.8 %collective-permute-done.7.refs_0_ = f32[128,256]{1,0:T(8,128)S(1)} collective-permute-done((f32[128,256]{1,0:T(8,128)S(1)}, f32[128,256]{1,0:T(8,128)S(1)}, u32[]{:S(2)}, u32[]{:S(2)}) %collective-permute-start.7) | collective-permute-done | bytes 131104 | tf_op jit(solution)/shard_map/ppermute | solution.py:70
  16.1 0.2 collective-permute-start.8
  16.3 0.2 collective-permute-done.9.refs_9_
  16.5 0.2 collective-permute-start.12
  16.7 0.3 collective-permute-start.10
  17.0 5.3 %collective-permute-start.11 = (f32[256,128]{1,0:T(8,128)S(1)}, f32[256,128]{1,0:T(8,128)S(1)}, u32[]{:S(2)}, u32[]{:S(2)}) collective-permute-start(f32[256,128]{1,0:T(8,128)S(1)} %collective-permute-done.9.refs_9_), channel_id=1, source_target_pairs={{0,1},{1,0},{2,3},{3,2},{4,5},{5,4},{6,7},{7,6},{8,16},{9,17},{10,... | collective-permute-start | bytes 393224 | tf_op jit(solution)/shard_map/ppermute | solution.py:70
  22.3 0.0 collective-permute-done.8.refs_8_.refs_6_
  22.3 0.0 collective-permute-done.6.refs_6_.refs_4_
  22.3 0.0 collective-permute-done.12.refs_2_
  22.3 0.3 shard_map.44.refs_2_.refs_9_
  22.6 4.0 %collective-permute-start.14 = (f32[256,128]{1,0:T(8,128)S(1)}, f32[256,128]{1,0:T(8,128)S(1)}, u32[]{:S(2)}, u32[]{:S(2)}) collective-permute-start(f32[256,128]{1,0:T(8,128)S(1)} %shard_map.44.refs_2_.refs_9_), channel_id=1, source_target_pairs={{0,1},{1,0},{2,3},{3,2},{4,5},{5,4},{6,7},{7,6},{8,16},{9,17},{10,... | collective-permute-start | bytes 393224 | tf_op jit(solution)/shard_map/ppermute | solution.py:70
  26.7 0.0 collective-permute-start.15
  26.7 0.0 collective-permute-done.10.refs_0_
  26.7 4.5 %collective-permute-done.11.refs_1_ = f32[256,128]{1,0:T(8,128)S(1)} collective-permute-done((f32[256,128]{1,0:T(8,128)S(1)}, f32[256,128]{1,0:T(8,128)S(1)}, u32[]{:S(2)}, u32[]{:S(2)}) %collective-permute-start.11) | collective-permute-done | bytes 131104 | tf_op jit(solution)/shard_map/ppermute | solution.py:70
  31.2 1.1 %collective-permute-start.13 = (f32[256,128]{1,0:T(8,128)S(1)}, f32[256,128]{1,0:T(8,128)S(1)}, u32[]{:S(2)}, u32[]{:S(2)}) collective-permute-start(f32[256,128]{1,0:T(8,128)S(1)} %shard_map.45.refs_7_), channel_id=1, source_target_pairs={{0,1},{1,0},{2,3},{3,2},{4,5},{5,4},{6,7},{7,6},{8,9},{9,8},{10,11... | collective-permute-start | bytes 393224 | tf_op jit(solution)/shard_map/ppermute | solution.py:70
  32.3 0.6 %collective-permute-done.14.refs_0_ = f32[256,128]{1,0:T(8,128)S(1)} collective-permute-done((f32[256,128]{1,0:T(8,128)S(1)}, f32[256,128]{1,0:T(8,128)S(1)}, u32[]{:S(2)}, u32[]{:S(2)}) %collective-permute-start.14) | collective-permute-done | bytes 131104 | tf_op jit(solution)/shard_map/ppermute | solution.py:70
  32.9 0.0 collective-permute-done.15.refs_1_
  32.9 1.1 %collective-permute-start.16 = (f32[256,128]{1,0:T(8,128)S(1)}, f32[256,128]{1,0:T(8,128)S(1)}, u32[]{:S(2)}, u32[]{:S(2)}) collective-permute-start(f32[256,128]{1,0:T(8,128)S(1)} %shard_map.48.refs_7_), channel_id=1, source_target_pairs={{0,1},{1,0},{2,3},{3,2},{4,5},{5,4},{6,7},{7,6},{8,9},{9,8},{10,11... | collective-permute-start | bytes 393224 | tf_op jit(solution)/shard_map/ppermute | solution.py:70
  34.1 0.3 shard_map.46.refs_0_
  34.4 3.1 %collective-permute-done.13.refs_7_ = f32[256,128]{1,0:T(8,128)S(1)} collective-permute-done((f32[256,128]{1,0:T(8,128)S(1)}, f32[256,128]{1,0:T(8,128)S(1)}, u32[]{:S(2)}, u32[]{:S(2)}) %collective-permute-start.13) | collective-permute-done | bytes 131104 | tf_op jit(solution)/shard_map/ppermute | solution.py:70
  37.5 0.3 shard_map.47.refs_0_
  37.8 0.3 shard_map.49.refs_0_
  38.1 0.8 %collective-permute-done.16.refs_7_ = f32[256,128]{1,0:T(8,128)S(1)} collective-permute-done((f32[256,128]{1,0:T(8,128)S(1)}, f32[256,128]{1,0:T(8,128)S(1)}, u32[]{:S(2)}, u32[]{:S(2)}) %collective-permute-start.16) | collective-permute-done | bytes 131104 | tf_op jit(solution)/shard_map/ppermute | solution.py:70
  38.9 1.0 %shard_map.50 = f32[256,128]{1,0:T(8,128)} custom-call(f32[256,128]{1,0:T(8,128)S(1)} %shard_map.49.refs_0_, f32[320,256]{1,0:T(8,128)S(1)} %shard_map.38.refs_0_.refs_3_.refs_1_, f32[320,256]{1,0:T(8,128)S(1)} %collective-permute-done.5.refs_1_.refs_4_.refs_2_, f32[512,256]{1,0:T(8,128)S(1)} %shard_map.40.refs_5_.refs_3_, ...), custom_call_target="tpu_custom_call" | custom-call | tf_op jit(solution)/shard_map/pallas_call | solution.py:38
  (8 shorter events, 0.1 us)
Async XLA Ops:
  1.1 12.3 %collective-permute-start.4 = (f32[320,256]{1,0:T(8,128)S(1)}, f32[320,256]{1,0:T(8,128)S(1)}, u32[]{:S(2)}, u32[]{:S(2)}) collective-permute-start(f32[320,256]{1,0:T(8,128)S(1)} %get-tuple-element.19), channel_id=1, source_target_pairs={{0,4},{1,5},{2,6},{3,7},{4,0},{5,1},{6,2},{7,3},{8,12},{9,13},{10,... | collective-permute-start | bytes 983048 | tf_op jit(solution)/shard_map/ppermute | solution.py:70
  1.2 12.2 %collective-permute-start.3 = (f32[256,256]{1,0:T(8,128)S(1)}, f32[256,256]{1,0:T(8,128)S(1)}, u32[]{:S(2)}, u32[]{:S(2)}) collective-permute-start(f32[256,256]{1,0:T(8,128)S(1)} %get-tuple-element.18.refs_3_.refs_0_), channel_id=1, source_target_pairs={{0,2},{1,3},{2,0},{3,1},{4,6},{5,7},{6,4},{7,5},{8,10},{9,11},{10,... | collective-permute-start | bytes 786440 | tf_op jit(solution)/shard_map/ppermute | solution.py:70
  2.8 4.9 %collective-permute-start = (f32[64,256]{1,0:T(8,128)S(1)}, f32[64,256]{1,0:T(8,128)S(1)}, u32[]{:S(2)}, u32[]{:S(2)}) collective-permute-start(f32[64,256]{1,0:T(8,128)S(1)} %get-tuple-element.15), channel_id=1, source_target_pairs={{0,8},{1,12},{2,10},{3,14},{4,9},{5,13},{6,11},{7,15},{8,0},{9,4},... | collective-permute-start | bytes 196616 | tf_op jit(solution)/shard_map/ppermute | solution.py:70
  4.1 6.2 %collective-permute-start.1 = (f32[64,256]{1,0:T(8,128)S(1)}, f32[64,256]{1,0:T(8,128)S(1)}, u32[]{:S(2)}, u32[]{:S(2)}) collective-permute-start(f32[64,256]{1,0:T(8,128)S(1)} %get-tuple-element.16), channel_id=1, source_target_pairs={{0,16},{1,20},{2,18},{3,22},{4,17},{5,21},{6,19},{7,23},{8,24},{9,... | collective-permute-start | bytes 196616 | tf_op jit(solution)/shard_map/ppermute | solution.py:70
  5.8 7.6 %collective-permute-start.2 = (f32[64,256]{1,0:T(8,128)S(1)}, f32[64,256]{1,0:T(8,128)S(1)}, u32[]{:S(2)}, u32[]{:S(2)}) collective-permute-start(f32[64,256]{1,0:T(8,128)S(1)} %get-tuple-element.17), channel_id=1, source_target_pairs={{0,24},{1,28},{2,26},{3,30},{4,25},{5,29},{6,27},{7,31},{8,16},{9,... | collective-permute-start | bytes 196616 | tf_op jit(solution)/shard_map/ppermute | solution.py:70
  13.4 1.7 %collective-permute-start.5 = (f32[320,256]{1,0:T(8,128)S(1)}, f32[320,256]{1,0:T(8,128)S(1)}, u32[]{:S(2)}, u32[]{:S(2)}) collective-permute-start(f32[320,256]{1,0:T(8,128)S(1)} %shard_map.38.refs_0_.refs_3_.refs_1_), channel_id=1, source_target_pairs={{0,1},{1,0},{2,3},{3,2},{4,5},{5,4},{6,7},{7,6},{8,9},{9,8},{10,11... | collective-permute-start | bytes 983048 | tf_op jit(solution)/shard_map/ppermute | solution.py:70
  13.6 8.7 %collective-permute-start.6 = (f32[512,256]{1,0:T(8,128)S(1)}, f32[512,256]{1,0:T(8,128)S(1)}, u32[]{:S(2)}, u32[]{:S(2)}) collective-permute-start(f32[512,256]{1,0:T(8,128)S(1)} %shard_map.40.refs_5_.refs_3_), channel_id=1, source_target_pairs={{0,1},{1,0},{2,3},{3,2},{4,5},{5,4},{6,7},{7,6},{8,9},{9,8},{10,11... | collective-permute-start | bytes 1572872 | tf_op jit(solution)/shard_map/ppermute | solution.py:70
  14.1 1.9 %collective-permute-start.7 = (f32[128,256]{1,0:T(8,128)S(1)}, f32[128,256]{1,0:T(8,128)S(1)}, u32[]{:S(2)}, u32[]{:S(2)}) collective-permute-start(f32[128,256]{1,0:T(8,128)S(1)} %shard_map.39.refs_2_), channel_id=1, source_target_pairs={{0,1},{1,0},{2,3},{3,2},{4,5},{5,4},{6,7},{7,6},{8,10},{9,11},{10,... | collective-permute-start | bytes 393224 | tf_op jit(solution)/shard_map/ppermute | solution.py:70
  15.1 1.3 %collective-permute-start.9 = (f32[256,128]{1,0:T(8,128)S(1)}, f32[256,128]{1,0:T(8,128)S(1)}, u32[]{:S(2)}, u32[]{:S(2)}) collective-permute-start(f32[256,128]{1,0:T(8,128)S(1)} %shard_map.41.refs_1_.refs_8_), channel_id=1, source_target_pairs={{0,8},{1,9},{2,10},{3,11},{4,12},{5,13},{6,14},{7,15},{8,0},{9,1},... | collective-permute-start | bytes 393224 | tf_op jit(solution)/shard_map/ppermute | solution.py:70
  16.1 6.2 %collective-permute-start.8 = (f32[128,256]{1,0:T(8,128)S(1)}, f32[128,256]{1,0:T(8,128)S(1)}, u32[]{:S(2)}, u32[]{:S(2)}) collective-permute-start(f32[128,256]{1,0:T(8,128)S(1)} %shard_map.42.refs_7_.refs_5_), channel_id=1, source_target_pairs={{0,1},{1,0},{2,3},{3,2},{4,5},{5,4},{6,7},{7,6},{8,9},{9,8},{10,11... | collective-permute-start | bytes 393224 | tf_op jit(solution)/shard_map/ppermute | solution.py:70
  16.5 5.9 %collective-permute-start.12 = (f32[256,128]{1,0:T(8,128)S(1)}, f32[256,128]{1,0:T(8,128)S(1)}, u32[]{:S(2)}, u32[]{:S(2)}) collective-permute-start(f32[256,128]{1,0:T(8,128)S(1)} %collective-permute-done.9.refs_9_), channel_id=1, source_target_pairs={{0,1},{1,0},{2,3},{3,2},{4,5},{5,4},{6,7},{7,6},{8,12},{9,13},{10,... | collective-permute-start | bytes 393224 | tf_op jit(solution)/shard_map/ppermute | solution.py:70
  16.7 10.0 %collective-permute-start.10 = (f32[256,128]{1,0:T(8,128)S(1)}, f32[256,128]{1,0:T(8,128)S(1)}, u32[]{:S(2)}, u32[]{:S(2)}) collective-permute-start(f32[256,128]{1,0:T(8,128)S(1)} %collective-permute-done.9.refs_9_), channel_id=1, source_target_pairs={{0,1},{1,0},{2,3},{3,2},{4,5},{5,4},{6,7},{7,6},{8,24},{9,25},{10,... | collective-permute-start | bytes 393224 | tf_op jit(solution)/shard_map/ppermute | solution.py:70
  17.0 14.2 %collective-permute-start.11 = (f32[256,128]{1,0:T(8,128)S(1)}, f32[256,128]{1,0:T(8,128)S(1)}, u32[]{:S(2)}, u32[]{:S(2)}) collective-permute-start(f32[256,128]{1,0:T(8,128)S(1)} %collective-permute-done.9.refs_9_), channel_id=1, source_target_pairs={{0,1},{1,0},{2,3},{3,2},{4,5},{5,4},{6,7},{7,6},{8,16},{9,17},{10,... | collective-permute-start | bytes 393224 | tf_op jit(solution)/shard_map/ppermute | solution.py:70
  22.6 10.3 %collective-permute-start.14 = (f32[256,128]{1,0:T(8,128)S(1)}, f32[256,128]{1,0:T(8,128)S(1)}, u32[]{:S(2)}, u32[]{:S(2)}) collective-permute-start(f32[256,128]{1,0:T(8,128)S(1)} %shard_map.44.refs_2_.refs_9_), channel_id=1, source_target_pairs={{0,1},{1,0},{2,3},{3,2},{4,5},{5,4},{6,7},{7,6},{8,16},{9,17},{10,... | collective-permute-start | bytes 393224 | tf_op jit(solution)/shard_map/ppermute | solution.py:70
  26.7 6.3 %collective-permute-start.15 = (f32[256,128]{1,0:T(8,128)S(1)}, f32[256,128]{1,0:T(8,128)S(1)}, u32[]{:S(2)}, u32[]{:S(2)}) collective-permute-start(f32[256,128]{1,0:T(8,128)S(1)} %shard_map.44.refs_2_.refs_9_), channel_id=1, source_target_pairs={{0,1},{1,0},{2,3},{3,2},{4,5},{5,4},{6,7},{7,6},{8,24},{9,25},{10,... | collective-permute-start | bytes 393224 | tf_op jit(solution)/shard_map/ppermute | solution.py:70
  31.2 6.3 %collective-permute-start.13 = (f32[256,128]{1,0:T(8,128)S(1)}, f32[256,128]{1,0:T(8,128)S(1)}, u32[]{:S(2)}, u32[]{:S(2)}) collective-permute-start(f32[256,128]{1,0:T(8,128)S(1)} %shard_map.45.refs_7_), channel_id=1, source_target_pairs={{0,1},{1,0},{2,3},{3,2},{4,5},{5,4},{6,7},{7,6},{8,9},{9,8},{10,11... | collective-permute-start | bytes 393224 | tf_op jit(solution)/shard_map/ppermute | solution.py:70
  32.9 5.9 %collective-permute-start.16 = (f32[256,128]{1,0:T(8,128)S(1)}, f32[256,128]{1,0:T(8,128)S(1)}, u32[]{:S(2)}, u32[]{:S(2)}) collective-permute-start(f32[256,128]{1,0:T(8,128)S(1)} %shard_map.48.refs_7_), channel_id=1, source_target_pairs={{0,1},{1,0},{2,3},{3,2},{4,5},{5,4},{6,7},{7,6},{8,9},{9,8},{10,11... | collective-permute-start | bytes 393224 | tf_op jit(solution)/shard_map/ppermute | solution.py:70

commit v9 on v8

--- a/solution.py
+++ b/solution.py
@@ -244,7 +244,7 @@
         for w in range(n_win - 1):
             here = climb(either, w, w + 1)
             there = swap_rows(here, lambda q, w=w: q == w + 1)
-            early.append([climb(here, w + 1, t) for t in range(n_pair - 1, w + 1, -1)])
+            early.append([climb(here, w + 1, t) for t in range(w + 2, n_pair)])
             late = call(stack, [((n_half - 1) * units, rows)], near[1:], last=[either])
             blocks = [*soon, *more, late, swap_cores(late)]
 
@@ -294,7 +294,7 @@
         final = [climb(either, n_win - 1, t) for t in range(n_win, n_pair)]
         left = rhs
         for i, values in enumerate([*early, final]):
-            pairs = range(n_win, n_pair) if i == len(early) else range(n_pair - 1, i + 1, -1)
+            pairs = range(n_win, n_pair) if i == len(early) else range(i + 2, n_pair)
             which = functools.partial(arrive, pairs=pairs)
             value = call(which, [(rows, width)], values, last=[either] if i < len(early) else [])
             traded = swap_rows(value, lambda q: q >= n_win)

time: 40.5 us -> 40.5 us (level)
  no operation moved by 1% of the time
where the time goes in v9:
time: 40.5 us; the launch traced here: 39.8 us
  starting transfers between devices  18.6 us (46%)
  waiting for transfers between devices  17.6 us (43%)
  Pallas kernels  3.49 us (9%)
    ppermute x17, starting transfers between devices, hop(): return lax.ppermute(value, AXES, edges)  18.6 us
    ppermute x17, waiting for transfers between devices, hop(): return lax.ppermute(value, AXES, edges)  17.6 us
    pallas_call x14, Pallas kernels, call(): pl.pallas_call(kernel, out_shape=out, in_specs=[ANY] * len(first) + [VMEM...  3.49 us
  transfers between devices with their start and end apart: 17, of which 10 were waited for; matrix products, arithmetic and copies ran while one was open for 0% of the time, Pallas kernels for 3%

profile of v9, /device:TPU:18, one launch (start us, length us, event | category | flops | bytes accessed | tf_op | source)
XLA Modules:
  0.0 39.8 jit_solution(1076478663255380149)
XLA Ops:
  0.0 1.1 %shard_map.37 = (f32[320,256]{1,0:T(8,128)S(1)}, f32[256,256]{1,0:T(8,128)S(1)}, f32[256,128]{1,0:T(8,128)S(1)}, f32[64,256]{1,0:T(8,128)S(1)}, f32[64,256]{1,0:...) custom-call(f32[256,128]{1,0:T(8,128)} %refs_0_.1, f32[256,256]{1,0:T(8,128)} %bitcast.3, f32[4,32,256]{2,1,0:T(8,128)} %refs_2_.1), custom_call_target="tpu_custom_call" | custom-call | tf_op jit(solution)/shard_map/pallas_call | solution.py:38
  1.1 0.1 collective-permute-start.4
  1.2 1.6 %collective-permute-start.3 = (f32[256,256]{1,0:T(8,128)S(1)}, f32[256,256]{1,0:T(8,128)S(1)}, u32[]{:S(2)}, u32[]{:S(2)}) collective-permute-start(f32[256,256]{1,0:T(8,128)S(1)} %get-tuple-element.18.refs_3_.refs_0_), channel_id=1, source_target_pairs={{0,2},{1,3},{2,0},{3,1},{4,6},{5,7},{6,4},{7,5},{8,10},{9,11},{10,... | collective-permute-start | bytes 786440 | tf_op jit(solution)/shard_map/ppermute | solution.py:70
  2.8 1.3 %collective-permute-start = (f32[64,256]{1,0:T(8,128)S(1)}, f32[64,256]{1,0:T(8,128)S(1)}, u32[]{:S(2)}, u32[]{:S(2)}) collective-permute-start(f32[64,256]{1,0:T(8,128)S(1)} %get-tuple-element.15), channel_id=1, source_target_pairs={{0,8},{1,12},{2,10},{3,14},{4,9},{5,13},{6,11},{7,15},{8,0},{9,4},... | collective-permute-start | bytes 196616 | tf_op jit(solution)/shard_map/ppermute | solution.py:70
  4.1 1.7 %collective-permute-start.1 = (f32[64,256]{1,0:T(8,128)S(1)}, f32[64,256]{1,0:T(8,128)S(1)}, u32[]{:S(2)}, u32[]{:S(2)}) collective-permute-start(f32[64,256]{1,0:T(8,128)S(1)} %get-tuple-element.16), channel_id=1, source_target_pairs={{0,16},{1,20},{2,18},{3,22},{4,17},{5,21},{6,19},{7,23},{8,24},{9,... | collective-permute-start | bytes 196616 | tf_op jit(solution)/shard_map/ppermute | solution.py:70
  5.8 0.9 %collective-permute-start.2 = (f32[64,256]{1,0:T(8,128)S(1)}, f32[64,256]{1,0:T(8,128)S(1)}, u32[]{:S(2)}, u32[]{:S(2)}) collective-permute-start(f32[64,256]{1,0:T(8,128)S(1)} %get-tuple-element.17), channel_id=1, source_target_pairs={{0,24},{1,28},{2,26},{3,30},{4,25},{5,29},{6,27},{7,31},{8,16},{9,... | collective-permute-start | bytes 196616 | tf_op jit(solution)/shard_map/ppermute | solution.py:70
  6.6 1.1 %collective-permute-done.refs_0_.refs_1_ = f32[64,256]{1,0:T(8,128)S(1)} collective-permute-done((f32[64,256]{1,0:T(8,128)S(1)}, f32[64,256]{1,0:T(8,128)S(1)}, u32[]{:S(2)}, u32[]{:S(2)}) %collective-permute-start) | collective-permute-done | bytes 65568 | tf_op jit(solution)/shard_map/ppermute | solution.py:70
  7.7 2.6 %collective-permute-done.1.refs_1_.refs_2_ = f32[64,256]{1,0:T(8,128)S(1)} collective-permute-done((f32[64,256]{1,0:T(8,128)S(1)}, f32[64,256]{1,0:T(8,128)S(1)}, u32[]{:S(2)}, u32[]{:S(2)}) %collective-permute-start.1) | collective-permute-done | bytes 65568 | tf_op jit(solution)/shard_map/ppermute | solution.py:70
  10.3 3.1 %collective-permute-done.2.refs_2_.refs_3_ = f32[64,256]{1,0:T(8,128)S(1)} collective-permute-done((f32[64,256]{1,0:T(8,128)S(1)}, f32[64,256]{1,0:T(8,128)S(1)}, u32[]{:S(2)}, u32[]{:S(2)}) %collective-permute-start.2) | collective-permute-done | bytes 65568 | tf_op jit(solution)/shard_map/ppermute | solution.py:70
  13.4 0.0 collective-permute-done.3.refs_4_.refs_1_
  13.4 0.0 collective-permute-done.4.refs_5_.refs_0_.refs_3_.refs_1_
  13.4 0.1 collective-permute-start.5
  13.6 0.6 %collective-permute-start.6 = (f32[512,256]{1,0:T(8,128)S(1)}, f32[512,256]{1,0:T(8,128)S(1)}, u32[]{:S(2)}, u32[]{:S(2)}) collective-permute-start(f32[512,256]{1,0:T(8,128)S(1)} %shard_map.40.refs_5_.refs_3_), channel_id=1, source_target_pairs={{0,1},{1,0},{2,3},{3,2},{4,5},{5,4},{6,7},{7,6},{8,9},{9,8},{10,11... | collective-permute-start | bytes 1572872 | tf_op jit(solution)/shard_map/ppermute | solution.py:70
  14.1 0.1 collective-permute-start.7
  14.2 0.9 %collective-permute-done.5.refs_1_.refs_4_.refs_2_ = f32[320,256]{1,0:T(8,128)S(1)} collective-permute-done((f32[320,256]{1,0:T(8,128)S(1)}, f32[320,256]{1,0:T(8,128)S(1)}, u32[]{:S(2)}, u32[]{:S(2)}) %collective-permute-start.5) | collective-permute-done | bytes 327712 | tf_op jit(solution)/shard_map/ppermute | solution.py:70
  15.1 0.1 collective-permute-start.9
  15.3 0.8 %collective-permute-done.7.refs_0_ = f32[128,256]{1,0:T(8,128)S(1)} collective-permute-done((f32[128,256]{1,0:T(8,128)S(1)}, f32[128,256]{1,0:T(8,128)S(1)}, u32[]{:S(2)}, u32[]{:S(2)}) %collective-permute-start.7) | collective-permute-done | bytes 131104 | tf_op jit(solution)/shard_map/ppermute | solution.py:70
  16.1 0.2 collective-permute-start.8
  16.3 0.2 collective-permute-done.9.refs_9_
  16.5 0.2 collective-permute-start.12
  16.7 5.6 %collective-permute-start.10 = (f32[256,128]{1,0:T(8,128)S(1)}, f32[256,128]{1,0:T(8,128)S(1)}, u32[]{:S(2)}, u32[]{:S(2)}) collective-permute-start(f32[256,128]{1,0:T(8,128)S(1)} %collective-permute-done.9.refs_9_), channel_id=1, source_target_pairs={{0,1},{1,0},{2,3},{3,2},{4,5},{5,4},{6,7},{7,6},{8,16},{9,17},{10,... | collective-permute-start | bytes 393224 | tf_op jit(solution)/shard_map/ppermute | solution.py:70
  22.3 0.0 collective-permute-start.11
  22.3 0.0 collective-permute-done.8.refs_8_.refs_6_
  22.3 0.0 collective-permute-done.6.refs_6_.refs_4_
  22.3 0.1 shard_map.43
  22.4 0.0 collective-permute-done.12.refs_2_
  22.4 0.3 shard_map.44.refs_2_.refs_9_
  22.7 4.0 %collective-permute-start.14 = (f32[256,128]{1,0:T(8,128)S(1)}, f32[256,128]{1,0:T(8,128)S(1)}, u32[]{:S(2)}, u32[]{:S(2)}) collective-permute-start(f32[256,128]{1,0:T(8,128)S(1)} %shard_map.44.refs_2_.refs_9_), channel_id=1, source_target_pairs={{0,1},{1,0},{2,3},{3,2},{4,5},{5,4},{6,7},{7,6},{8,16},{9,17},{10,... | collective-permute-start | bytes 393224 | tf_op jit(solution)/shard_map/ppermute | solution.py:70
  26.7 0.0 collective-permute-start.15
  26.7 4.5 %collective-permute-done.10.refs_0_ = f32[256,128]{1,0:T(8,128)S(1)} collective-permute-done((f32[256,128]{1,0:T(8,128)S(1)}, f32[256,128]{1,0:T(8,128)S(1)}, u32[]{:S(2)}, u32[]{:S(2)}) %collective-permute-start.10) | collective-permute-done | bytes 131104 | tf_op jit(solution)/shard_map/ppermute | solution.py:70
  31.2 0.0 collective-permute-done.11.refs_1_
  31.2 1.1 %collective-permute-start.13 = (f32[256,128]{1,0:T(8,128)S(1)}, f32[256,128]{1,0:T(8,128)S(1)}, u32[]{:S(2)}, u32[]{:S(2)}) collective-permute-start(f32[256,128]{1,0:T(8,128)S(1)} %shard_map.45.refs_7_), channel_id=1, source_target_pairs={{0,1},{1,0},{2,3},{3,2},{4,5},{5,4},{6,7},{7,6},{8,9},{9,8},{10,11... | collective-permute-start | bytes 393224 | tf_op jit(solution)/shard_map/ppermute | solution.py:70
  32.3 0.6 %collective-permute-done.14.refs_0_ = f32[256,128]{1,0:T(8,128)S(1)} collective-permute-done((f32[256,128]{1,0:T(8,128)S(1)}, f32[256,128]{1,0:T(8,128)S(1)}, u32[]{:S(2)}, u32[]{:S(2)}) %collective-permute-start.14) | collective-permute-done | bytes 131104 | tf_op jit(solution)/shard_map/ppermute | solution.py:70
  32.9 0.0 collective-permute-done.15.refs_1_
  32.9 1.1 %collective-permute-start.16 = (f32[256,128]{1,0:T(8,128)S(1)}, f32[256,128]{1,0:T(8,128)S(1)}, u32[]{:S(2)}, u32[]{:S(2)}) collective-permute-start(f32[256,128]{1,0:T(8,128)S(1)} %shard_map.48.refs_7_), channel_id=1, source_target_pairs={{0,1},{1,0},{2,3},{3,2},{4,5},{5,4},{6,7},{7,6},{8,9},{9,8},{10,11... | collective-permute-start | bytes 393224 | tf_op jit(solution)/shard_map/ppermute | solution.py:70
  34.1 0.3 shard_map.46.refs_0_
  34.4 3.1 %collective-permute-done.13.refs_7_ = f32[256,128]{1,0:T(8,128)S(1)} collective-permute-done((f32[256,128]{1,0:T(8,128)S(1)}, f32[256,128]{1,0:T(8,128)S(1)}, u32[]{:S(2)}, u32[]{:S(2)}) %collective-permute-start.13) | collective-permute-done | bytes 131104 | tf_op jit(solution)/shard_map/ppermute | solution.py:70
  37.5 0.3 shard_map.47.refs_0_
  37.8 0.3 shard_map.49.refs_0_
  38.1 0.8 %collective-permute-done.16.refs_7_ = f32[256,128]{1,0:T(8,128)S(1)} collective-permute-done((f32[256,128]{1,0:T(8,128)S(1)}, f32[256,128]{1,0:T(8,128)S(1)}, u32[]{:S(2)}, u32[]{:S(2)}) %collective-permute-start.16) | collective-permute-done | bytes 131104 | tf_op jit(solution)/shard_map/ppermute | solution.py:70
  38.9 1.0 %shard_map.50 = f32[256,128]{1,0:T(8,128)} custom-call(f32[256,128]{1,0:T(8,128)S(1)} %shard_map.49.refs_0_, f32[320,256]{1,0:T(8,128)S(1)} %shard_map.38.refs_0_.refs_3_.refs_1_, f32[320,256]{1,0:T(8,128)S(1)} %collective-permute-done.5.refs_1_.refs_4_.refs_2_, f32[512,256]{1,0:T(8,128)S(1)} %shard_map.40.refs_5_.refs_3_, ...), custom_call_target="tpu_custom_call" | custom-call | tf_op jit(solution)/shard_map/pallas_call | solution.py:38
  (7 shorter events, 0.1 us)
Async XLA Ops:
  1.1 12.3 %collective-permute-start.4 = (f32[320,256]{1,0:T(8,128)S(1)}, f32[320,256]{1,0:T(8,128)S(1)}, u32[]{:S(2)}, u32[]{:S(2)}) collective-permute-start(f32[320,256]{1,0:T(8,128)S(1)} %get-tuple-element.19), channel_id=1, source_target_pairs={{0,4},{1,5},{2,6},{3,7},{4,0},{5,1},{6,2},{7,3},{8,12},{9,13},{10,... | collective-permute-start | bytes 983048 | tf_op jit(solution)/shard_map/ppermute | solution.py:70
  1.2 12.2 %collective-permute-start.3 = (f32[256,256]{1,0:T(8,128)S(1)}, f32[256,256]{1,0:T(8,128)S(1)}, u32[]{:S(2)}, u32[]{:S(2)}) collective-permute-start(f32[256,256]{1,0:T(8,128)S(1)} %get-tuple-element.18.refs_3_.refs_0_), channel_id=1, source_target_pairs={{0,2},{1,3},{2,0},{3,1},{4,6},{5,7},{6,4},{7,5},{8,10},{9,11},{10,... | collective-permute-start | bytes 786440 | tf_op jit(solution)/shard_map/ppermute | solution.py:70
  2.8 4.9 %collective-permute-start = (f32[64,256]{1,0:T(8,128)S(1)}, f32[64,256]{1,0:T(8,128)S(1)}, u32[]{:S(2)}, u32[]{:S(2)}) collective-permute-start(f32[64,256]{1,0:T(8,128)S(1)} %get-tuple-element.15), channel_id=1, source_target_pairs={{0,8},{1,12},{2,10},{3,14},{4,9},{5,13},{6,11},{7,15},{8,0},{9,4},... | collective-permute-start | bytes 196616 | tf_op jit(solution)/shard_map/ppermute | solution.py:70
  4.1 6.2 %collective-permute-start.1 = (f32[64,256]{1,0:T(8,128)S(1)}, f32[64,256]{1,0:T(8,128)S(1)}, u32[]{:S(2)}, u32[]{:S(2)}) collective-permute-start(f32[64,256]{1,0:T(8,128)S(1)} %get-tuple-element.16), channel_id=1, source_target_pairs={{0,16},{1,20},{2,18},{3,22},{4,17},{5,21},{6,19},{7,23},{8,24},{9,... | collective-permute-start | bytes 196616 | tf_op jit(solution)/shard_map/ppermute | solution.py:70
  5.8 7.6 %collective-permute-start.2 = (f32[64,256]{1,0:T(8,128)S(1)}, f32[64,256]{1,0:T(8,128)S(1)}, u32[]{:S(2)}, u32[]{:S(2)}) collective-permute-start(f32[64,256]{1,0:T(8,128)S(1)} %get-tuple-element.17), channel_id=1, source_target_pairs={{0,24},{1,28},{2,26},{3,30},{4,25},{5,29},{6,27},{7,31},{8,16},{9,... | collective-permute-start | bytes 196616 | tf_op jit(solution)/shard_map/ppermute | solution.py:70
  13.4 1.7 %collective-permute-start.5 = (f32[320,256]{1,0:T(8,128)S(1)}, f32[320,256]{1,0:T(8,128)S(1)}, u32[]{:S(2)}, u32[]{:S(2)}) collective-permute-start(f32[320,256]{1,0:T(8,128)S(1)} %shard_map.38.refs_0_.refs_3_.refs_1_), channel_id=1, source_target_pairs={{0,1},{1,0},{2,3},{3,2},{4,5},{5,4},{6,7},{7,6},{8,9},{9,8},{10,11... | collective-permute-start | bytes 983048 | tf_op jit(solution)/shard_map/ppermute | solution.py:70
  13.6 8.7 %collective-permute-start.6 = (f32[512,256]{1,0:T(8,128)S(1)}, f32[512,256]{1,0:T(8,128)S(1)}, u32[]{:S(2)}, u32[]{:S(2)}) collective-permute-start(f32[512,256]{1,0:T(8,128)S(1)} %shard_map.40.refs_5_.refs_3_), channel_id=1, source_target_pairs={{0,1},{1,0},{2,3},{3,2},{4,5},{5,4},{6,7},{7,6},{8,9},{9,8},{10,11... | collective-permute-start | bytes 1572872 | tf_op jit(solution)/shard_map/ppermute | solution.py:70
  14.1 1.9 %collective-permute-start.7 = (f32[128,256]{1,0:T(8,128)S(1)}, f32[128,256]{1,0:T(8,128)S(1)}, u32[]{:S(2)}, u32[]{:S(2)}) collective-permute-start(f32[128,256]{1,0:T(8,128)S(1)} %shard_map.39.refs_2_), channel_id=1, source_target_pairs={{0,1},{1,0},{2,3},{3,2},{4,5},{5,4},{6,7},{7,6},{8,10},{9,11},{10,... | collective-permute-start | bytes 393224 | tf_op jit(solution)/shard_map/ppermute | solution.py:70
  15.1 1.3 %collective-permute-start.9 = (f32[256,128]{1,0:T(8,128)S(1)}, f32[256,128]{1,0:T(8,128)S(1)}, u32[]{:S(2)}, u32[]{:S(2)}) collective-permute-start(f32[256,128]{1,0:T(8,128)S(1)} %shard_map.41.refs_1_.refs_8_), channel_id=1, source_target_pairs={{0,8},{1,9},{2,10},{3,11},{4,12},{5,13},{6,14},{7,15},{8,0},{9,1},... | collective-permute-start | bytes 393224 | tf_op jit(solution)/shard_map/ppermute | solution.py:70
  16.1 6.2 %collective-permute-start.8 = (f32[128,256]{1,0:T(8,128)S(1)}, f32[128,256]{1,0:T(8,128)S(1)}, u32[]{:S(2)}, u32[]{:S(2)}) collective-permute-start(f32[128,256]{1,0:T(8,128)S(1)} %shard_map.42.refs_7_.refs_5_), channel_id=1, source_target_pairs={{0,1},{1,0},{2,3},{3,2},{4,5},{5,4},{6,7},{7,6},{8,9},{9,8},{10,11... | collective-permute-start | bytes 393224 | tf_op jit(solution)/shard_map/ppermute | solution.py:70
  16.5 5.9 %collective-permute-start.12 = (f32[256,128]{1,0:T(8,128)S(1)}, f32[256,128]{1,0:T(8,128)S(1)}, u32[]{:S(2)}, u32[]{:S(2)}) collective-permute-start(f32[256,128]{1,0:T(8,128)S(1)} %collective-permute-done.9.refs_9_), channel_id=1, source_target_pairs={{0,1},{1,0},{2,3},{3,2},{4,5},{5,4},{6,7},{7,6},{8,12},{9,13},{10,... | collective-permute-start | bytes 393224 | tf_op jit(solution)/shard_map/ppermute | solution.py:70
  16.7 14.5 %collective-permute-start.10 = (f32[256,128]{1,0:T(8,128)S(1)}, f32[256,128]{1,0:T(8,128)S(1)}, u32[]{:S(2)}, u32[]{:S(2)}) collective-permute-start(f32[256,128]{1,0:T(8,128)S(1)} %collective-permute-done.9.refs_9_), channel_id=1, source_target_pairs={{0,1},{1,0},{2,3},{3,2},{4,5},{5,4},{6,7},{7,6},{8,16},{9,17},{10,... | collective-permute-start | bytes 393224 | tf_op jit(solution)/shard_map/ppermute | solution.py:70
  22.3 8.9 %collective-permute-start.11 = (f32[256,128]{1,0:T(8,128)S(1)}, f32[256,128]{1,0:T(8,128)S(1)}, u32[]{:S(2)}, u32[]{:S(2)}) collective-permute-start(f32[256,128]{1,0:T(8,128)S(1)} %collective-permute-done.9.refs_9_), channel_id=1, source_target_pairs={{0,1},{1,0},{2,3},{3,2},{4,5},{5,4},{6,7},{7,6},{8,24},{9,25},{10,... | collective-permute-start | bytes 393224 | tf_op jit(solution)/shard_map/ppermute | solution.py:70
  22.7 10.2 %collective-permute-start.14 = (f32[256,128]{1,0:T(8,128)S(1)}, f32[256,128]{1,0:T(8,128)S(1)}, u32[]{:S(2)}, u32[]{:S(2)}) collective-permute-start(f32[256,128]{1,0:T(8,128)S(1)} %shard_map.44.refs_2_.refs_9_), channel_id=1, source_target_pairs={{0,1},{1,0},{2,3},{3,2},{4,5},{5,4},{6,7},{7,6},{8,16},{9,17},{10,... | collective-permute-start | bytes 393224 | tf_op jit(solution)/shard_map/ppermute | solution.py:70
  26.7 6.3 %collective-permute-start.15 = (f32[256,128]{1,0:T(8,128)S(1)}, f32[256,128]{1,0:T(8,128)S(1)}, u32[]{:S(2)}, u32[]{:S(2)}) collective-permute-start(f32[256,128]{1,0:T(8,128)S(1)} %shard_map.44.refs_2_.refs_9_), channel_id=1, source_target_pairs={{0,1},{1,0},{2,3},{3,2},{4,5},{5,4},{6,7},{7,6},{8,24},{9,25},{10,... | collective-permute-start | bytes 393224 | tf_op jit(solution)/shard_map/ppermute | solution.py:70
  31.2 6.3 %collective-permute-start.13 = (f32[256,128]{1,0:T(8,128)S(1)}, f32[256,128]{1,0:T(8,128)S(1)}, u32[]{:S(2)}, u32[]{:S(2)}) collective-permute-start(f32[256,128]{1,0:T(8,128)S(1)} %shard_map.45.refs_7_), channel_id=1, source_target_pairs={{0,1},{1,0},{2,3},{3,2},{4,5},{5,4},{6,7},{7,6},{8,9},{9,8},{10,11... | collective-permute-start | bytes 393224 | tf_op jit(solution)/shard_map/ppermute | solution.py:70
  32.9 5.9 %collective-permute-start.16 = (f32[256,128]{1,0:T(8,128)S(1)}, f32[256,128]{1,0:T(8,128)S(1)}, u32[]{:S(2)}, u32[]{:S(2)}) collective-permute-start(f32[256,128]{1,0:T(8,128)S(1)} %shard_map.48.refs_7_), channel_id=1, source_target_pairs={{0,1},{1,0},{2,3},{3,2},{4,5},{5,4},{6,7},{7,6},{8,9},{9,8},{10,11... | collective-permute-start | bytes 393224 | tf_op jit(solution)/shard_map/ppermute | solution.py:70
